TPU v7x, 32 devices: a whole 2x2x4 slice. The times are simulated.
32 devices in a mesh: strip: 8 (over z, x), chan: 4 (over y, core).
Axes of the slice: x: 2, y: 2, z: 4, core: 2. Of those that a mesh axis runs over, the one named last changes fastest.
Arguments:
- cam_feats: bfloat16 [80, 131072], P('chan', 'strip'), may hold values from -3 to 3
- cell_index: int32 [131072], P('strip'), may hold values from 0 to 4096
- lidar_bev: bfloat16 [16, 256, 16, 128], P(None, 'chan', 'strip'), may hold values from -12 to 12
- w_cam: float32 [3, 3, 80, 256], P(None, None, None, 'chan'), may hold values from -0.109375 to 0.109375
- w_lidar: float32 [3, 3, 256, 256], P(None, None, None, 'chan'), may hold values from -0.109375 to 0.109375
- w_mid: float32 [3, 3, 256, 256], P(None, None, 'chan'), may hold values from -0.125 to 0.125
- bn_params: float32 [4, 256], P(None, 'chan'), may hold values from -1.5 to 6.5
- cotangent: bfloat16 [16, 256, 16, 128], P(None, 'chan', 'strip'), may hold values from -12 to 12
- m_cam: float32 [3, 3, 80, 256], P(None, None, None, 'chan'), may hold values from -0.0014648438 to 0.0014648438
- v_cam: float32 [3, 3, 80, 256], P(None, None, None, 'chan'), may hold values from 7.3260503e-10 to 2.9304201e-09
- m_lidar: float32 [3, 3, 256, 256], P(None, None, None, 'chan'), may hold values from -0.0014648438 to 0.0014648438
- v_lidar: float32 [3, 3, 256, 256], P(None, None, None, 'chan'), may hold values from 7.3260503e-10 to 2.9304201e-09
- m_mid: float32 [3, 3, 256, 256], P(None, None, 'chan'), may hold values from -0.0014648438 to 0.0014648438
- v_mid: float32 [3, 3, 256, 256], P(None, None, 'chan'), may hold values from 7.3260503e-10 to 2.9304201e-09
- m_bn: float32 [4, 256], P(None, 'chan'), may hold values from -0.0014648438 to 0.0014648438
- v_bn: float32 [4, 256], P(None, 'chan'), may hold values from 7.3260503e-10 to 2.9304201e-09
Outputs:
- mixed: float32 [16, 256, 16, 128], P(None, 'chan', 'strip')
- grad_cam: float32 [80, 131072], P('chan', 'strip')
- grad_lidar: float32 [16, 256, 16, 128], P(None, 'chan', 'strip')
- grad_norm: float32 [], replicated
- new_w_cam: float32 [3, 3, 80, 256], P(None, None, None, 'chan')
- new_m_cam: float32 [3, 3, 80, 256], P(None, None, None, 'chan')
- new_v_cam: float32 [3, 3, 80, 256], P(None, None, None, 'chan')
- new_w_lidar: float32 [3, 3, 256, 256], P(None, None, None, 'chan')
- new_m_lidar: float32 [3, 3, 256, 256], P(None, None, None, 'chan')
- new_v_lidar: float32 [3, 3, 256, 256], P(None, None, None, 'chan')
- new_w_mid: float32 [3, 3, 256, 256], P(None, None, 'chan')
- new_m_mid: float32 [3, 3, 256, 256], P(None, None, 'chan')
- new_v_mid: float32 [3, 3, 256, 256], P(None, None, 'chan')
- new_bn: float32 [4, 256], P(None, 'chan')
- new_m_bn: float32 [4, 256], P(None, 'chan')
- new_v_bn: float32 [4, 256], P(None, 'chan')
Inputs may be any that keep to these rules, and one draw needn't show every extreme that they name: `cell_index`: the cell of a point counts within the rows of the strip that holds the point, as (grid * 2 + row) * 128 + column; 4096 marks a point outside every grid.
All inputs are finite; a program needn't handle non-finite values.
Results may differ from a plain program's by a relative error of at most 0.0087.
Values may be sent and summed in bfloat16 or wider, within the bound.
No kernel may reach another device: no remote copies, remote signals or barrier semaphores. Data moves between devices by JAX's collectives and lax.ppermute only.
A program may use at most 128 MiB of HBM per device.

v0:
```python
import math

import jax
import jax.numpy as jnp
from jax import lax
from jax.sharding import PartitionSpec as P

STEP = 10


beta_one = 0.9
beta_two = 0.999
adam_eps = 1e-08
learn_rate = 0.02
norm_rate = 1.5
weight_decay = 0.01
norm_eps = 1e-05
clip_norm = 1.0


def with_halo(cells, sides, width):
    for axis, dim in sides:
        count = lax.axis_size(axis)
        ends = count - 1
        head = lax.slice_in_dim(cells, 0, width, axis=dim)
        tail = lax.slice_in_dim(cells, cells.shape[dim] - width, cells.shape[dim], axis=dim)
        cells = jnp.concatenate(
            [
                lax.ppermute(tail, axis, [(i, (i + 1) % count) for i in range(ends)]),
                cells,
                lax.ppermute(head, axis, [((i + 1) % count, i) for i in range(ends)]),
            ],
            axis=dim,
        )
    return cells


def pad_columns(values):
    return jnp.pad(values, ((0, 0), (0, 0), (0, 0), (1, 1)))


def chan_view(vector):
    return vector[None, :, None, None]


def silu_slope(values):
    sigmoid_value = jax.nn.sigmoid(values)
    return sigmoid_value * (1.0 + values * (1.0 - sigmoid_value))


def conv_taps(padded, kernel, row_count, col_count):
    result = None
    for row_tap in range(3):
        for col_tap in range(3):
            window = padded[:, :, row_tap : row_tap + row_count, col_tap : col_tap + col_count]
            partial_term = jnp.einsum(
                "gihw,io->gohw",
                window,
                kernel[row_tap, col_tap],
                preferred_element_type=jnp.float32,
            )
            result = partial_term if result is None else result + partial_term
    return result


def conv_back_input(padded_grad, kernel, row_count, col_count):
    result = None
    for row_tap in range(3):
        for col_tap in range(3):
            window = padded_grad[
                :, :, 2 - row_tap : 2 - row_tap + row_count, 2 - col_tap : 2 - col_tap + col_count
            ]
            partial_term = jnp.einsum(
                "gohw,io->gihw",
                window,
                kernel[row_tap, col_tap],
                preferred_element_type=jnp.float32,
            )
            result = partial_term if result is None else result + partial_term
    return result


def conv_back_weight(padded, grad_out, row_count, col_count):
    tap_rows = []
    for row_tap in range(3):
        tap_list = []
        for col_tap in range(3):
            window = padded[:, :, row_tap : row_tap + row_count, col_tap : col_tap + col_count]
            tap_list.append(
                jnp.einsum("gihw,gohw->io", window, grad_out, preferred_element_type=jnp.float32)
            )
        tap_rows.append(jnp.stack(tap_list))
    return jnp.stack(tap_rows)


def normalize(raw, sums, squares, gain, shift, pixel_count):
    mean_value = sums / pixel_count
    variance = squares / pixel_count - mean_value * mean_value
    inv_std = lax.rsqrt(variance + norm_eps)
    centred = (raw - chan_view(mean_value)) * chan_view(inv_std)
    return (centred, inv_std, chan_view(gain) * centred + chan_view(shift))


def norm_back(slope, centred, inv_std, gain, shift_grad, gain_grad, pixel_count):
    inner = (
        slope - chan_view(shift_grad / pixel_count) - centred * chan_view(gain_grad / pixel_count)
    )
    return chan_view(gain * inv_std) * inner


def adam_update(weight, gradient, first, second, rate):
    first = beta_one * first + (1.0 - beta_one) * gradient
    second = beta_two * second + (1.0 - beta_two) * gradient * gradient
    fix_one = 1.0 - beta_one**STEP
    fix_two = 1.0 - beta_two**STEP
    stepped = first / fix_one / (jnp.sqrt(second / fix_two) + adam_eps)
    return (weight - rate * (stepped + weight_decay * weight), first, second)


def shards(
    cam_feats,
    cell_index,
    lidar_bev,
    w_cam,
    w_lidar,
    w_mid,
    bn_params,
    cotangent,
    m_cam,
    v_cam,
    m_lidar,
    v_lidar,
    m_mid,
    v_mid,
    m_bn,
    v_bn,
):
    grid_count, lidar_own, row_count, col_count = lidar_bev.shape
    cam_own, point_count = cam_feats.shape
    chan_count = lax.axis_size("chan")
    strip_count = lax.axis_size("strip")
    cell_total = grid_count * row_count * col_count
    pixel_count = float(cell_total * strip_count)
    block_size = math.gcd(point_count, 1024)
    block_count = point_count // block_size
    feat_blocks = cam_feats.reshape(cam_own, block_count, block_size).transpose(1, 0, 2)
    cell_blocks = cell_index.reshape(block_count, block_size)
    slot_ids = lax.iota(jnp.int32, cell_total)

    def pool_step(totals, paired):
        feature, groups = paired
        table = (groups[None, :] == slot_ids[:, None]).astype(jnp.bfloat16)
        added = lax.dot_general(
            feature, table, (((1,), (1,)), ((), ())), preferred_element_type=jnp.float32
        )
        return (totals + added, None)

    pooled, unused = lax.scan(
        pool_step, jnp.zeros((cam_own, cell_total), jnp.float32), (feat_blocks, cell_blocks)
    )
    pooled_low = (
        pooled.reshape(cam_own, grid_count, row_count, col_count)
        .transpose(1, 0, 2, 3)
        .astype(jnp.bfloat16)
    )
    joined = jnp.concatenate([pooled_low, lidar_bev], axis=1)

    def gather_inputs():
        rimmed = with_halo(joined, (("strip", 2),), 1)
        gathered = lax.all_gather(rimmed, "chan", axis=1, tiled=True)
        gathered = gathered.reshape(
            grid_count, chan_count, cam_own + lidar_own, row_count + 2, col_count
        )
        cam_all = gathered[:, :, :cam_own].reshape(
            grid_count, chan_count * cam_own, row_count + 2, col_count
        )
        lidar_all = gathered[:, :, cam_own:].reshape(
            grid_count, chan_count * lidar_own, row_count + 2, col_count
        )
        return (pad_columns(cam_all), pad_columns(lidar_all))

    kernel_cam = w_cam.astype(jnp.bfloat16)
    kernel_lidar = w_lidar.astype(jnp.bfloat16)
    kernel_mid = w_mid.astype(jnp.bfloat16)
    cam_pad, lidar_pad = gather_inputs()
    first_conv = conv_taps(cam_pad, kernel_cam, row_count, col_count) + conv_taps(
        lidar_pad, kernel_lidar, row_count, col_count
    )
    sums_one, squares_one = lax.psum(
        (jnp.sum(first_conv, axis=(0, 2, 3)), jnp.sum(first_conv * first_conv, axis=(0, 2, 3))),
        "strip",
    )
    centred_one, inv_one, act_one = normalize(
        first_conv, sums_one, squares_one, bn_params[0], bn_params[1], pixel_count
    )
    hidden = jax.nn.silu(act_one)
    hidden_low = hidden.astype(jnp.bfloat16)
    hidden_rim = with_halo(hidden_low, (("strip", 2),), 1)
    hidden_pad = pad_columns(hidden_rim)
    partial_mid = conv_taps(hidden_pad, kernel_mid, row_count, col_count)
    encoded = lax.psum_scatter(partial_mid, "chan", scatter_dimension=1, tiled=True)
    sums_two, squares_two = lax.psum(
        (jnp.sum(encoded, axis=(0, 2, 3)), jnp.sum(encoded * encoded, axis=(0, 2, 3))), "strip"
    )
    centred_two, inv_two, act_two = normalize(
        encoded, sums_two, squares_two, bn_params[2], bn_params[3], pixel_count
    )
    mixed = hidden + jax.nn.silu(act_two)
    upstream = cotangent.astype(jnp.float32)
    slope_two = upstream * silu_slope(act_two)
    shift_grad2, gain_grad2 = lax.psum(
        (jnp.sum(slope_two, axis=(0, 2, 3)), jnp.sum(slope_two * centred_two, axis=(0, 2, 3))),
        "strip",
    )
    grad_enc = norm_back(
        slope_two, centred_two, inv_two, bn_params[2], shift_grad2, gain_grad2, pixel_count
    ).astype(jnp.bfloat16)
    grad_enc_rim = with_halo(grad_enc, (("strip", 2),), 1)
    grad_enc_all = lax.all_gather(grad_enc_rim, "chan", axis=1, tiled=True)
    grad_mid_local = conv_back_weight(
        hidden_pad, grad_enc_all[:, :, 1 : row_count + 1], row_count, col_count
    )
    grad_hidden = upstream + conv_back_input(
        pad_columns(grad_enc_all), kernel_mid, row_count, col_count
    )
    slope_one = grad_hidden * silu_slope(act_one)
    shift_grad1, gain_grad1 = lax.psum(
        (jnp.sum(slope_one, axis=(0, 2, 3)), jnp.sum(slope_one * centred_one, axis=(0, 2, 3))),
        "strip",
    )
    grad_first = norm_back(
        slope_one, centred_one, inv_one, bn_params[0], shift_grad1, gain_grad1, pixel_count
    ).astype(jnp.bfloat16)
    grad_first_rim = with_halo(grad_first, (("strip", 2),), 1)
    cam_again, lidar_again = gather_inputs()
    grad_wc_local = conv_back_weight(cam_again, grad_first, row_count, col_count)
    grad_wl_local = conv_back_weight(lidar_again, grad_first, row_count, col_count)
    grad_first_pad = pad_columns(grad_first_rim)
    back_cam = conv_back_input(grad_first_pad, kernel_cam, row_count, col_count)
    back_lidar = conv_back_input(grad_first_pad, kernel_lidar, row_count, col_count)
    combined = jnp.concatenate(
        [
            back_cam.reshape(grid_count, chan_count, cam_own, row_count, col_count),
            back_lidar.reshape(grid_count, chan_count, lidar_own, row_count, col_count),
        ],
        axis=2,
    )
    combined = combined.reshape(
        grid_count, chan_count * (cam_own + lidar_own), row_count, col_count
    )
    own_grads = lax.psum_scatter(combined, "chan", scatter_dimension=1, tiled=True)
    grad_lidar = own_grads[:, cam_own:]
    back_pool = own_grads[:, :cam_own]
    grad_pool = back_pool.astype(jnp.bfloat16).transpose(1, 0, 2, 3).reshape(cam_own, cell_total)

    def spread_block(groups):
        table = (groups[None, :] == slot_ids[:, None]).astype(jnp.bfloat16)
        return jnp.dot(grad_pool, table, preferred_element_type=jnp.float32)

    grad_cam = lax.map(spread_block, cell_blocks).transpose(1, 0, 2).reshape(cam_own, point_count)
    grad_wc, grad_wl, grad_mid = lax.psum((grad_wc_local, grad_wl_local, grad_mid_local), "strip")
    grad_bn = jnp.stack([gain_grad1, shift_grad1, gain_grad2, shift_grad2])
    local_squares = (
        jnp.sum(grad_wc * grad_wc)
        + jnp.sum(grad_wl * grad_wl)
        + jnp.sum(grad_mid * grad_mid)
        + jnp.sum(grad_bn * grad_bn)
    )
    grad_norm = jnp.sqrt(lax.psum(local_squares, "chan"))
    factor = jnp.minimum(1.0, clip_norm / (grad_norm + 1e-06))
    new_w_cam, new_m_cam, new_v_cam = adam_update(w_cam, factor * grad_wc, m_cam, v_cam, learn_rate)
    new_w_lidar, new_m_lidar, new_v_lidar = adam_update(
        w_lidar, factor * grad_wl, m_lidar, v_lidar, learn_rate
    )
    new_w_mid, new_m_mid, new_v_mid = adam_update(
        w_mid, factor * grad_mid, m_mid, v_mid, learn_rate
    )
    new_bn, new_m_bn, new_v_bn = adam_update(bn_params, factor * grad_bn, m_bn, v_bn, norm_rate)
    return (
        mixed,
        grad_cam,
        grad_lidar,
        grad_norm,
        new_w_cam,
        new_m_cam,
        new_v_cam,
        new_w_lidar,
        new_m_lidar,
        new_v_lidar,
        new_w_mid,
        new_m_mid,
        new_v_mid,
        new_bn,
        new_m_bn,
        new_v_bn,
    )


def solution(mesh):
    return jax.shard_map(
        shards,
        mesh=mesh,
        in_specs=(
            P("chan", "strip"),
            P("strip"),
            P(None, "chan", "strip", None),
            P(None, None, None, "chan"),
            P(None, None, None, "chan"),
            P(None, None, "chan", None),
            P(None, "chan"),
            P(None, "chan", "strip", None),
            P(None, None, None, "chan"),
            P(None, None, None, "chan"),
            P(None, None, None, "chan"),
            P(None, None, None, "chan"),
            P(None, None, "chan", None),
            P(None, None, "chan", None),
            P(None, "chan"),
            P(None, "chan"),
        ),
        out_specs=(
            P(None, "chan", "strip", None),
            P("chan", "strip"),
            P(None, "chan", "strip", None),
            P(),
            P(None, None, None, "chan"),
            P(None, None, None, "chan"),
            P(None, None, None, "chan"),
            P(None, None, None, "chan"),
            P(None, None, None, "chan"),
            P(None, None, None, "chan"),
            P(None, None, "chan", None),
            P(None, None, "chan", None),
            P(None, None, "chan", None),
            P(None, "chan"),
            P(None, "chan"),
            P(None, "chan"),
        ),
        check_vma=False,
    )
```

profile of v0, /device:TPU:0, one launch (start us, length us, event | category | flops | bytes accessed | tf_op | source)
XLA Modules:
  0.0 613.5 jit_solution(11605468252164425160)
XLA Ops:
  10.1 47.2 %while.23 = (s32[]{:T(128)}, f32[20,4096]{1,0:T(8,128)S(1)}, bf16[16,20,1024]{2,1,0:T(8,128)(2,1)S(1)}, s32[16,1024]{1,0:T(8,128)S(1)}, s32[]{:T(128)}, /*index=5*/s32[]{:T(128)}) while((s32[]{:T(128)}, f32[20,4096]{1,0:T(8,128)S(1)}, bf16[16,20,1024]{2,1,0:T(8,128)(2,1)S(1)}, s32[16,1024]{1,0:T(8,128)S(1)}, s32[]{:T(128)}, ...), condition=%wide.region_1.2_spmd.clone, body=%wide.region_0.1_spmd.clone.sunk | while | flops 172130304 | bytes 782423 | solution.py:158
  10.2 2.9 fusion.241
  13.1 2.9 fusion.241
  16.0 2.9 fusion.241
  19.0 2.9 fusion.241
  21.9 2.9 fusion.241
  24.9 2.9 fusion.241
  27.8 2.9 fusion.241
  30.8 2.9 fusion.241
  33.7 2.9 fusion.241
  36.7 2.9 fusion.241
  39.6 2.9 fusion.241
  42.6 2.9 fusion.241
  45.5 2.9 fusion.241
  48.5 2.9 fusion.241
  51.4 2.9 fusion.241
  54.4 2.9 fusion.241
  58.3 5.0 collective-permute-start
  64.7 13.2 %collective-permute-done = bf16[16,84,1,128]{3,0,2,1:T(8,128)(2,1)S(1)} collective-permute-done((bf16[16,84,1,128]{3,0,2,1:T(8,128)(2,1)S(1)}, bf16[16,84,1,128]{3,0,2,1:T(8,128)(2,1)S(1)}, u32[]{:S(2)}, u32[]{:S(2)}) %collective-permute-start) | collective-permute-done | bytes 344096 | tf_op jit(solution)/shard_map/ppermute | solution.py:29
  79.8 43.6 %all-gather.3.cloned.1.call-done = bf16[16,336,4,128]{3,0,2,1:T(8,128)(2,1)} async-done(((bf16[16,84,4,128]{3,0,2,1:T(8,128)(2,1)}), bf16[16,336,4,128]{3,0,2,1:T(8,128)(2,1)}) %all-gather.3.cloned.1.call-update) | async-done | bytes 5505040 | tf_op jit(solution)/shard_map/all_gather | solution.py:170
  125.0 3.6 slice.452
  142.5 21.4 %all-reduce.8 = (f32[64]{0:T(128)S(1)}, f32[64]{0:T(128)S(1)}) all-reduce(f32[64]{0:T(128)S(1)} %get-tuple-element.222, f32[64]{0:T(128)S(1)} %get-tuple-element.221), channel_id=1, replica_groups=mesh['strip'=8,'chan'=4] {'strip'}, use_global_device_ids=true, to_apply=%region_5.6 | all-reduce | flops 128 | bytes 1024 | tf_op jit(solution)/shard_map/psum | solution.py:189
  167.7 6.3 %collective-permute-done.2 = bf16[16,64,1,128]{3,1,2,0:T(8,128)(2,1)S(1)} collective-permute-done((bf16[16,64,1,128]{3,1,2,0:T(8,128)(2,1)S(1)}, bf16[16,64,1,128]{3,1,2,0:T(8,128)(2,1)S(1)}, u32[]{:S(2)}, u32[]{:S(2)}) %collective-permute-start.2) | collective-permute-done | bytes 262176 | tf_op jit(solution)/shard_map/ppermute | solution.py:29
  176.7 2.8 fusion.129
  182.2 2.8 fusion.120
  187.7 2.8 fusion.88
  190.4 12.4 %add_bitcast_fusion.1 = f32[16,256,2,128]{3,1,2,0:T(8,128)} fusion(f32[16,2,128,256]{2,3,1,0:T(8,128)} %fusion.88, f32[16,2,128,256]{2,3,1,0:T(8,128)} %fusion.120, f32[16,2,128,256]{2,3,1,0:T(8,128)S(1)} %fusion.123, f32[16,2,128,256]{2,3,1,0:T(8,128)S(1)} %fusion.139, f32[16,2,128,256]{2,3,1,0:T(8,128)S(1)} %fusion.126, f32[16,2,128,256]{2,3,1,0:T(8,128)} %fusion.129, ...), kind=kOutput, calls=%fused_computation.38 | convolution fusion | flops 142606336 | bytes 38305792 | tf_op jit(solution)/shard_map/gihw,io->gohw/dot_general | solution.py:56
  202.9 42.9 %reduce-scatter.3.cloned.1.call-done = f32[16,64,2,128]{3,1,2,0:T(8,128)} async-done(((f32[16,256,2,128]{3,1,2,0:T(8,128)}), f32[16,64,2,128]{3,1,2,0:T(8,128)}) %reduce-scatter.3.cloned.1.call-update) | async-done | bytes 1048592 | tf_op jit(solution)/shard_map/reduce_scatter | solution.py:201
  247.2 21.4 %all-reduce.7 = (f32[64]{0:T(128)S(1)}, f32[64]{0:T(128)S(1)}) all-reduce(f32[64]{0:T(128)S(1)} %get-tuple-element.220, f32[64]{0:T(128)S(1)} %get-tuple-element.219), channel_id=1, replica_groups=mesh['strip'=8,'chan'=4] {'strip'}, use_global_device_ids=true, to_apply=%region_10.11 | all-reduce | flops 128 | bytes 1024 | tf_op jit(solution)/shard_map/psum | solution.py:202
  269.1 3.8 fusion.197
  272.9 17.3 %all-reduce.6 = (f32[64]{0:T(128)S(1)}, f32[64]{0:T(128)S(1)}) all-reduce(f32[64]{0:T(128)S(1)} %get-tuple-element.218, f32[64]{0:T(128)S(1)} %get-tuple-element.217), channel_id=1, replica_groups=mesh['strip'=8,'chan'=4] {'strip'}, use_global_device_ids=true, to_apply=%region_14.15 | all-reduce | flops 128 | bytes 1024 | tf_op jit(solution)/shard_map/psum | solution.py:211
  292.2 4.0 collective-permute-start.4
  300.0 4.4 collective-permute-done.5
  305.6 31.3 %all-gather.5.cloned.1.call-done = bf16[16,256,4,128]{3,1,2,0:T(8,128)(2,1)} async-done(((bf16[16,64,4,128]{3,1,2,0:T(8,128)(2,1)}), bf16[16,256,4,128]{3,1,2,0:T(8,128)(2,1)}) %all-gather.5.cloned.1.call-update) | async-done | bytes 4194320 | tf_op jit(solution)/shard_map/all_gather | solution.py:219
  348.5 21.4 %all-reduce.5 = (f32[64]{0:T(128)S(1)}, f32[64]{0:T(128)S(1)}) all-reduce(f32[64]{0:T(128)S(1)} %get-tuple-element.216, f32[64]{0:T(128)S(1)} %get-tuple-element.215), channel_id=1, replica_groups=mesh['strip'=8,'chan'=4] {'strip'}, use_global_device_ids=true, to_apply=%region_18.19 | all-reduce | flops 128 | bytes 1024 | tf_op jit(solution)/shard_map/psum | solution.py:227
  386.6 3.6 fusion.137
  391.6 4.6 collective-permute-start.6
  411.6 2.8 fusion.107
  414.4 3.1 fusion.111
  417.5 3.2 fusion.96
  430.7 10.1 %add_bitcast_fusion = f32[16,256,2,128]{1,3,2,0:T(8,128)} fusion(f32[16,2,128,256]{3,2,1,0:T(8,128)} %fusion.85, f32[16,2,128,256]{3,2,1,0:T(8,128)} %fusion.96, f32[16,2,128,256]{3,2,1,0:T(8,128)S(1)} %fusion.100, f32[16,2,128,256]{3,2,1,0:T(8,128)S(1)} %copy-done.4, f32[16,2,128,256]{3,2,1,0:T(8,128)S(1)} %fusion.103, f32[16,2,128,256]{3,2,1,0:T(8,128)} %fusion.107, ...), kind=kOutput, calls=%fused_computation.37 | convolution fusion | flops 142606336 | bytes 38305792 | tf_op jit(solution)/shard_map/gohw,io->gihw/dot_general | solution.py:73
  440.8 5.4 copy.170
  446.2 2.9 pad_maximum_fusion
  449.1 5.6 copy.172
  456.1 33.9 %all-reduce.12.cloned.1.call-done = (f32[3,3,80,64]{2,3,1,0:T(8,128)}, f32[3,3,256,64]{2,3,1,0:T(8,128)}, f32[3,3,64,256]{3,2,1,0:T(8,128)}) async-done(((f32[3,3,80,64]{2,3,1,0:T(8,128)}, f32[3,3,256,64]{2,3,1,0:T(8,128)}, f32[3,3,64,256]{3,2,1,0:T(8,128)}), (f32[3,3,80,64]{2,3,1,0:T(8,128)}, f32[3,3,256,64]{2,3,1,0:T(8,128)}, f32[3,3,64,256]{3,2,1,0:T(8,128)})) %all-reduce.12.cloned.1.call-update) | async-done | bytes 1363984 | tf_op jit(solution)/shard_map/psum | solution.py:261
  499.9 7.9 %psum.95 = f32[]{:T(128)} all-reduce(f32[]{:T(128)S(6)} %add.420), channel_id=1, replica_groups=mesh['strip'=8,'chan'=4] {'chan'}, use_global_device_ids=true, to_apply=%region_29.30 | all-reduce | flops 1 | bytes 8 | tf_op jit(solution)/shard_map/psum | solution.py:269
  515.3 29.5 %reduce-scatter.5.cloned.1.call-done = f32[16,84,2,128]{3,0,2,1:T(8,128)} async-done(((f32[16,336,2,128]{3,0,2,1:T(8,128)}), f32[16,84,2,128]{3,0,2,1:T(8,128)}) %reduce-scatter.5.cloned.1.call-update) | async-done | bytes 1376272 | tf_op jit(solution)/shard_map/reduce_scatter | solution.py:251
  546.0 55.1 %while.22 = (s32[]{:T(128)}, f32[16,20,1024]{2,1,0:T(8,128)S(1)}, s32[16,1024]{1,0:T(8,128)}, bf16[20,4096]{1,0:T(8,128)(2,1)S(1)}, s32[]{:T(128)}) while((s32[]{:T(128)}, f32[16,20,1024]{2,1,0:T(8,128)S(1)}, s32[16,1024]{1,0:T(8,128)}, bf16[20,4096]{1,0:T(8,128)(2,1)S(1)}, s32[]{:T(128)}) %tuple.99), condition=%wide.region_21.22_spmd.clone, body=%wide.region_20.21_spmd.clone.sunk | while | flops 171966464 | bytes 307269 | solution.py:260
  (308 shorter events, 173.7 us)
Async XLA Ops:
  7.2 116.3 %all-gather.3.cloned.1.call-start = ((), (), s32[]{:S(2)}) async-start(), calls=%async_computation.2 | async-start | bytes 6881280 | tf_op jit(solution)/shard_map/all_gather | solution.py:170
  10.1 47.4 %copy-start.35 = (bf16[16,64,2,128]{3,2,1,0:T(2,128)(2,1)S(1)}, bf16[16,64,2,128]{3,2,1,0:T(2,128)(2,1)}, u32[]{:S(2)}) copy-start(bf16[16,64,2,128]{3,2,1,0:T(2,128)(2,1)} %param.22) | copy-start | bytes 1572868
  57.3 6.0 copy-start.36
  58.2 21.2 %copy-start.23 = (f32[3,3,80,64]{2,3,1,0:T(8,128)S(1)}, f32[3,3,80,64]{2,3,1,0:T(8,128)}, u32[]{:S(2)}) copy-start(f32[3,3,80,64]{2,3,1,0:T(8,128)} %param.23) | copy-start | bytes 552964
  58.3 19.7 %collective-permute-start = (bf16[16,84,1,128]{3,0,2,1:T(8,128)(2,1)S(1)}, bf16[16,84,1,128]{3,0,2,1:T(8,128)(2,1)S(1)}, u32[]{:S(2)}, u32[]{:S(2)}) collective-permute-start(bf16[16,84,1,128]{3,0,2,1:T(8,128)(2,1)S(1)} %get-tuple-element.264), channel_id=1, source_target_pairs={{0,4},{4,8},{8,12},{12,16},{16,20},{20,24},{24,28},{1,5},{5,9},{9,... | collective-permute-start | bytes 1032200 | tf_op jit(solution)/shard_map/ppermute | solution.py:29
  63.3 16.2 %copy-start.14 = (f32[3,3,256,64]{2,3,1,0:T(8,128)S(1)}, f32[3,3,256,64]{2,3,1,0:T(8,128)}, u32[]{:S(2)}) copy-start(f32[3,3,256,64]{2,3,1,0:T(8,128)} %param.24) | copy-start | bytes 1769476
  63.3 16.2 %copy-start.12 = (f32[3,3,64,256]{3,2,1,0:T(8,128)S(1)}, f32[3,3,64,256]{3,2,1,0:T(8,128)}, u32[]{:S(2)}) copy-start(f32[3,3,64,256]{3,2,1,0:T(8,128)} %param.25) | copy-start | bytes 1769476
  63.3 14.6 %collective-permute-start.1 = (bf16[16,84,1,128]{3,0,2,1:T(8,128)(2,1)S(1)}, bf16[16,84,1,128]{3,0,2,1:T(8,128)(2,1)S(1)}, u32[]{:S(2)}, u32[]{:S(2)}) collective-permute-start(bf16[16,84,1,128]{3,0,2,1:T(8,128)(2,1)S(1)} %get-tuple-element.265), channel_id=1, source_target_pairs={{4,0},{8,4},{12,8},{16,12},{20,16},{24,20},{28,24},{5,1},{9,5},{13... | collective-permute-start | bytes 1032200 | tf_op jit(solution)/shard_map/ppermute | solution.py:31
  79.2 166.6 %reduce-scatter.3.cloned.1.call-start = ((), (), s32[]{:S(2)}) async-start(), calls=%async_computation.3 | async-start | bytes 5242880 | tf_op jit(solution)/shard_map/reduce_scatter | solution.py:201
  79.5 61.9 %copy-start.10 = (bf16[3,3,256,64]{2,3,1,0:T(8,128)(2,1)}, bf16[3,3,256,64]{2,3,1,0:T(8,128)(2,1)S(1)}, u32[]{:S(2)}) copy-start(bf16[3,3,256,64]{2,3,1,0:T(8,128)(2,1)S(1)} %convert_element_type.47) | copy-start | bytes 884740
  125.0 9.5 %copy-start.7 = (bf16[16,4,20,4,128]{4,0,3,2,1:T(8,128)(2,1)}, bf16[16,4,20,4,128]{4,0,3,2,1:T(8,128)(2,1)S(1)}, u32[]{:S(2)}) copy-start(bf16[16,4,20,4,128]{4,0,3,2,1:T(8,128)(2,1)S(1)} %slice.439) | copy-start | bytes 3932164
  131.4 10.1 %copy-start = (bf16[16,4,64,4,128]{4,2,1,3,0:T(8,128)(2,1)}, bf16[16,4,64,4,128]{4,2,1,3,0:T(8,128)(2,1)S(1)}, u32[]{:S(2)}) copy-start(bf16[16,4,64,4,128]{4,2,1,3,0:T(8,128)(2,1)S(1)} %copy.158) | copy-start | bytes 12582916
  163.9 181.9 %copy-start.39 = (f32[64]{0:T(128)}, f32[64]{0:T(128)S(1)}, u32[]{:S(2)}) copy-start(f32[64]{0:T(128)S(1)} %get-tuple-element.280) | copy-start | bytes 772
  163.9 181.9 %copy-start.40 = (f32[64]{0:T(128)}, f32[64]{0:T(128)S(1)}, u32[]{:S(2)}) copy-start(f32[64]{0:T(128)S(1)} %get-tuple-element.281) | copy-start | bytes 772
  164.4 9.7 %collective-permute-start.2 = (bf16[16,64,1,128]{3,1,2,0:T(8,128)(2,1)S(1)}, bf16[16,64,1,128]{3,1,2,0:T(8,128)(2,1)S(1)}, u32[]{:S(2)}, u32[]{:S(2)}) collective-permute-start(bf16[16,64,1,128]{3,1,2,0:T(8,128)(2,1)S(1)} %get-tuple-element.270), channel_id=1, source_target_pairs={{0,4},{4,8},{8,12},{12,16},{16,20},{20,24},{24,28},{1,5},{5,9},{9,... | collective-permute-start | bytes 786440 | tf_op jit(solution)/shard_map/ppermute | solution.py:29
  165.7 8.4 %collective-permute-start.3 = (bf16[16,64,1,128]{3,1,2,0:T(8,128)(2,1)S(1)}, bf16[16,64,1,128]{3,1,2,0:T(8,128)(2,1)S(1)}, u32[]{:S(2)}, u32[]{:S(2)}) collective-permute-start(bf16[16,64,1,128]{3,1,2,0:T(8,128)(2,1)S(1)} %get-tuple-element.271), channel_id=1, source_target_pairs={{4,0},{8,4},{12,8},{16,12},{20,16},{24,20},{28,24},{5,1},{9,5},{13... | collective-permute-start | bytes 786440 | tf_op jit(solution)/shard_map/ppermute | solution.py:31
  174.1 10.9 %copy-start.28 = (bf16[16,64,1,128]{3,1,2,0:T(8,128)(2,1)}, bf16[16,64,1,128]{3,1,2,0:T(8,128)(2,1)S(1)}, u32[]{:S(2)}) copy-start(bf16[16,64,1,128]{3,1,2,0:T(8,128)(2,1)S(1)} %collective-permute-done.2) | copy-start | bytes 786436
  174.1 13.6 %copy-start.26 = (bf16[16,64,1,128]{3,1,2,0:T(8,128)(2,1)}, bf16[16,64,1,128]{3,1,2,0:T(8,128)(2,1)S(1)}, u32[]{:S(2)}) copy-start(bf16[16,64,1,128]{3,1,2,0:T(8,128)(2,1)S(1)} %collective-permute-done.3) | copy-start | bytes 786436
  175.2 7.0 %copy-start.5 = (bf16[16,64,4,130]{3,1,2,0:T(8,128)(2,1)}, bf16[16,64,4,130]{3,1,2,0:T(8,128)(2,1)S(1)}, u32[]{:S(2)}) copy-start(bf16[16,64,4,130]{3,1,2,0:T(8,128)(2,1)S(1)} %select_maximum_fusion.2) | copy-start | bytes 3194884
  202.8 134.0 %all-gather.5.cloned.1.call-start = ((), (), s32[]{:S(2)}) async-start(), calls=%async_computation.4 | async-start | bytes 5242880 | tf_op jit(solution)/shard_map/all_gather | solution.py:219
  290.2 15.3 %copy-start.41 = (f32[64]{0:T(128)}, f32[64]{0:T(128)S(1)}, u32[]{:S(2)}) copy-start(f32[64]{0:T(128)S(1)} %get-tuple-element.241) | copy-start | bytes 772
  290.2 15.3 %copy-start.43 = (f32[64]{0:T(128)}, f32[64]{0:T(128)S(1)}, u32[]{:S(2)}) copy-start(f32[64]{0:T(128)S(1)} %get-tuple-element.242) | copy-start | bytes 772
  292.2 7.9 %collective-permute-start.4 = (bf16[16,64,1,128]{3,1,2,0:T(8,128)(2,1)S(1)}, bf16[16,64,1,128]{3,1,2,0:T(8,128)(2,1)S(1)}, u32[]{:S(2)}, u32[]{:S(2)}) collective-permute-start(bf16[16,64,1,128]{3,1,2,0:T(8,128)(2,1)S(1)} %get-tuple-element.268), channel_id=1, source_target_pairs={{0,4},{4,8},{8,12},{12,16},{16,20},{20,24},{24,28},{1,5},{5,9},{9,... | collective-permute-start | bytes 786440 | tf_op jit(solution)/shard_map/ppermute | solution.py:29
  296.2 8.3 %collective-permute-start.5 = (bf16[16,64,1,128]{3,1,2,0:T(8,128)(2,1)S(1)}, bf16[16,64,1,128]{3,1,2,0:T(8,128)(2,1)S(1)}, u32[]{:S(2)}, u32[]{:S(2)}) collective-permute-start(bf16[16,64,1,128]{3,1,2,0:T(8,128)(2,1)S(1)} %get-tuple-element.269), channel_id=1, source_target_pairs={{4,0},{8,4},{12,8},{16,12},{20,16},{24,20},{28,24},{5,1},{9,5},{13... | collective-permute-start | bytes 786440 | tf_op jit(solution)/shard_map/ppermute | solution.py:31
  305.6 184.4 %all-reduce.12.cloned.1.call-start = ((), (), s32[]{:S(2)}) async-start(), calls=%async_computation.6 | async-start | bytes 2949120 | tf_op jit(solution)/shard_map/psum | solution.py:261
  336.9 4.3 copy-start.2
  371.9 2.8 copy-start.1
  386.5 9.7 %copy-start.3 = (bf16[16,256,4,128]{3,1,2,0:T(8,128)(2,1)S(1)}, bf16[16,256,4,128]{3,1,2,0:T(8,128)(2,1)}, u32[]{:S(2)}) copy-start(bf16[16,256,4,128]{3,1,2,0:T(8,128)(2,1)} %all-gather.5.cloned.1.call-done) | copy-start | bytes 12582916
  386.5 9.7 %copy-start.29 = (bf16[16,64,1,128]{3,1,2,0:T(8,128)(2,1)S(1)}, bf16[16,64,1,128]{3,1,2,0:T(8,128)(2,1)}, u32[]{:S(2)}) copy-start(bf16[16,64,1,128]{3,1,2,0:T(8,128)(2,1)} %copy-done.28) | copy-start | bytes 786436
  390.2 6.8 %copy-start.6 = (bf16[16,64,4,130]{3,1,2,0:T(8,128)(2,1)S(1)}, bf16[16,64,4,130]{3,1,2,0:T(8,128)(2,1)}, u32[]{:S(2)}) copy-start(bf16[16,64,4,130]{3,1,2,0:T(8,128)(2,1)} %copy-done.5) | copy-start | bytes 3194884
  390.2 16.5 %collective-permute-start.7 = (bf16[16,64,1,128]{3,1,2,0:T(8,128)(2,1)S(1)}, bf16[16,64,1,128]{3,1,2,0:T(8,128)(2,1)S(1)}, u32[]{:S(2)}, u32[]{:S(2)}) collective-permute-start(bf16[16,64,1,128]{3,1,2,0:T(8,128)(2,1)S(1)} %get-tuple-element.266), channel_id=1, source_target_pairs={{4,0},{8,4},{12,8},{16,12},{20,16},{24,20},{28,24},{5,1},{9,5},{13... | collective-permute-start | bytes 786440 | tf_op jit(solution)/shard_map/ppermute | solution.py:31
  391.6 15.1 %collective-permute-start.6 = (bf16[16,64,1,128]{3,1,2,0:T(8,128)(2,1)S(1)}, bf16[16,64,1,128]{3,1,2,0:T(8,128)(2,1)S(1)}, u32[]{:S(2)}, u32[]{:S(2)}) collective-permute-start(bf16[16,64,1,128]{3,1,2,0:T(8,128)(2,1)S(1)} %get-tuple-element.267), channel_id=1, source_target_pairs={{0,4},{4,8},{8,12},{12,16},{16,20},{20,24},{24,28},{1,5},{5,9},{9,... | collective-permute-start | bytes 786440 | tf_op jit(solution)/shard_map/ppermute | solution.py:29
  405.9 138.9 %reduce-scatter.5.cloned.1.call-start = ((), (), s32[]{:S(2)}) async-start(), calls=%async_computation.5 | async-start | bytes 6881280 | tf_op jit(solution)/shard_map/reduce_scatter | solution.py:251
  417.5 3.2 copy-start.19
  427.2 3.4 copy-start.4
  454.8 43.4 %copy-start.9 = (f32[16,64,2,128]{3,1,2,0:T(8,128)S(1)}, f32[16,64,2,128]{3,1,2,0:T(8,128)}, u32[]{:S(2)}) copy-start(f32[16,64,2,128]{3,1,2,0:T(8,128)} %get-tuple-element.263) | copy-start | bytes 3145732
  454.8 53.7 %copy-start.38 = (f32[4,64]{1,0:T(4,128)S(1)}, f32[4,64]{1,0:T(4,128)}, u32[]{:S(2)}) copy-start(f32[4,64]{1,0:T(4,128)} %param.26) | copy-start | bytes 3076
  454.8 53.7 %copy-start.45 = (f32[4,64]{1,0:T(4,128)S(1)}, f32[4,64]{1,0:T(4,128)}, u32[]{:S(2)}) copy-start(f32[4,64]{1,0:T(4,128)} %param.34) | copy-start | bytes 3076
  454.8 53.7 %copy-start.46 = (f32[4,64]{1,0:T(4,128)S(1)}, f32[4,64]{1,0:T(4,128)}, u32[]{:S(2)}) copy-start(f32[4,64]{1,0:T(4,128)} %param.35) | copy-start | bytes 3076
  454.8 54.4 %copy-start.24 = (f32[3,3,80,64]{2,3,1,0:T(8,128)S(1)}, f32[3,3,80,64]{2,3,1,0:T(8,128)}, u32[]{:S(2)}) copy-start(f32[3,3,80,64]{2,3,1,0:T(8,128)} %param.23) | copy-start | bytes 552964
  489.9 19.3 %copy-start.25 = (f32[3,3,80,64]{2,3,1,0:T(8,128)S(1)}, f32[3,3,80,64]{2,3,1,0:T(8,128)}, u32[]{:S(2)}) copy-start(f32[3,3,80,64]{2,3,1,0:T(8,128)} %get-tuple-element.247) | copy-start | bytes 552964
  496.6 14.7 %copy-start.13 = (f32[3,3,64,256]{3,2,1,0:T(8,128)S(1)}, f32[3,3,64,256]{3,2,1,0:T(8,128)}, u32[]{:S(2)}) copy-start(f32[3,3,64,256]{3,2,1,0:T(8,128)} %param.25) | copy-start | bytes 1769476
  496.6 14.7 %copy-start.17 = (f32[3,3,64,256]{3,2,1,0:T(8,128)S(1)}, f32[3,3,64,256]{3,2,1,0:T(8,128)}, u32[]{:S(2)}) copy-start(f32[3,3,64,256]{3,2,1,0:T(8,128)} %get-tuple-element.249) | copy-start | bytes 1769476
  496.6 14.7 %copy-start.30 = (f32[3,3,64,256]{3,2,1,0:T(8,128)S(1)}, f32[3,3,64,256]{3,2,1,0:T(8,128)}, u32[]{:S(2)}) copy-start(f32[3,3,64,256]{3,2,1,0:T(8,128)} %param.32) | copy-start | bytes 1769476
  499.9 11.4 %copy-start.31 = (f32[3,3,64,256]{3,2,1,0:T(8,128)S(1)}, f32[3,3,64,256]{3,2,1,0:T(8,128)}, u32[]{:S(2)}) copy-start(f32[3,3,64,256]{3,2,1,0:T(8,128)} %param.33) | copy-start | bytes 1769476
  511.3 2.3 copy-start.32
  511.3 2.5 copy-start.33
  513.8 32.2 %copy-start.22 = (f32[16,20,1024]{2,1,0:T(8,128)S(1)}, f32[16,20,1024]{2,1,0:T(8,128)}, u32[]{:S(2)}) copy-start(f32[16,20,1024]{2,1,0:T(8,128)} %custom-call.2) | copy-start | bytes 3932164
  (17 other events, 17.5 us)
Sparse Core Ops, SparseCore 0:
  79.3 44.1 all-gather.2
  203.0 42.7 reduce-scatter.2
  305.7 31.1 all-gather.4
  406.0 83.8 all-reduce.11
  492.3 52.4 reduce-scatter.4
where the time goes:
time: 620 us; the launch traced here: 614 us
  waiting for transfers between devices  208 us (34%)
  matrix products  194 us (31%)
  blocking collectives  89.3 us (14%)
  local copies, waits for them, and re-layouts  49.7 us (8%)
  other arithmetic  31.5 us (5%)
  starting transfers between devices  21.1 us (3%)
  between operations  19.9 us (3%)
    dot_general x16, matrix products, pool_step(): lax.dot_general(feature, table, (((1,), (1,)), ((), ())), preferred_eleme...  46.4 us
    dot_general x27, matrix products, conv_back_input(): jnp.einsum('gohw,io->gihw', window, kernel[row_tap, col_tap], preferred_e...  45.4 us
    all_gather x1, waiting for transfers between devices, gather_inputs(): gathered = lax.all_gather(rimmed, 'chan', axis=1, tiled=True)  43.6 us
    reduce_scatter x1, waiting for transfers between devices, shards(): lax.psum_scatter(partial_mid, 'chan', scatter_dimension=1, tiled=True)  42.9 us
    dot_general x16, matrix products, spread_block(): return jnp.dot(grad_pool, table, preferred_element_type=jnp.float32)  42.7 us
    dot_general x27, matrix products, conv_taps(): jnp.einsum('gihw,io->gohw', window, kernel[row_tap, col_tap], preferred_e...  38.5 us
    psum x1, waiting for transfers between devices, shards(): lax.psum((grad_wc_local, grad_wl_local, grad_mid_local), 'strip')  33.9 us
    all_gather x1, waiting for transfers between devices, shards(): grad_enc_all = lax.all_gather(grad_enc_rim, 'chan', axis=1, tiled=True)  31.3 us
  transfers between devices with their start and end apart: 13, of which 9 were waited for; matrix products, arithmetic and copies ran while one was open for 12% of the time, Pallas kernels for 0%

commit v1 on v0

v1 whole, which is shorter than its diff:
```python
import functools
import math

import jax
import jax.numpy as jnp
from jax import lax
from jax.experimental import pallas as pl
from jax.experimental.pallas import tpu as pltpu
from jax.sharding import PartitionSpec as P

STEP = 10


beta_one = 0.9
beta_two = 0.999
adam_eps = 1e-08
learn_rate = 0.02
norm_rate = 1.5
weight_decay = 0.01
norm_eps = 1e-05
clip_norm = 1.0

AXES = ("strip", "chan")
LANES = 128
VMEM_BYTES = 48 * 1024 * 1024

f32 = jnp.float32
bf16 = jnp.bfloat16


def round_up(value, step):
    return (value + step - 1) // step * step


def call(body, out_shape, scratch=(), smem=0, **options):
    def run(*operands):
        specs = [pl.BlockSpec(memory_space=pltpu.SMEM)] * smem
        specs += [pl.BlockSpec(memory_space=pltpu.VMEM)] * (len(operands) - smem)
        return pl.pallas_call(
            body,
            out_shape=out_shape,
            in_specs=specs,
            out_specs=jax.tree.map(lambda _: pl.BlockSpec(memory_space=pltpu.VMEM), out_shape),
            scratch_shapes=list(scratch),
            compiler_params=pltpu.CompilerParams(vmem_limit_bytes=VMEM_BYTES),
            **options,
        )(*operands)

    return run


def struct(shape, dtype):
    return jax.ShapeDtypeStruct(shape, dtype)


def cut(position):
    return slice(position * LANES, (position + 1) * LANES)


def sides(row):
    lane = lax.broadcasted_iota(jnp.int32, row.shape, 1)
    before = jnp.where(lane == 0, 0.0, pltpu.roll(row, 1, axis=1))
    after = jnp.where(lane == LANES - 1, 0.0, pltpu.roll(row, LANES - 1, axis=1))
    return before, after


def column_sums(parts):
    return jnp.concatenate([jnp.sum(part.T, axis=0, keepdims=True) for part in parts], axis=0)


def to_columns(rows):
    channels = rows[0].shape[1]
    rest = jnp.zeros((LANES - len(rows), channels), f32)
    return jnp.concatenate(list(rows) + [rest], axis=0).T


def matmul(left, right):
    return lax.dot_general(left, right, (((1,), (0,)), ((), ())), preferred_element_type=f32)


def matmul_nt(left, right):
    return lax.dot_general(left, right, (((1,), (1,)), ((), ())), preferred_element_type=f32)


def sigmoid(values):
    return 1.0 / (1.0 + jnp.exp(-values))


def moments(received, pixel_count):
    total = jnp.sum(received, axis=0)
    mean = total[0:1] / pixel_count
    variance = total[1:2] / pixel_count - mean * mean
    return mean, lax.rsqrt(variance + norm_eps)


def pool_body(grids, cells, chans, index_ref, feat_ref, out_ref, acc_ref):
    step = pl.program_id(0)
    rows = round_up(chans, 8)
    index = index_ref[...]
    high, low = index // cells, index % cells
    count = index.shape[1]
    feat = feat_ref[...].astype(f32)
    feat = jnp.concatenate([feat, jnp.zeros((rows - chans, count), f32)], axis=0)
    spread = jnp.concatenate(
        [jnp.where(high == grid, feat, 0.0) for grid in range(grids)], axis=0
    ).astype(bf16)
    table = (lax.broadcasted_iota(jnp.int32, (cells, count), 0) == low).astype(f32).astype(bf16)
    added = matmul_nt(spread, table)

    @pl.when(step == 0)
    def _():
        acc_ref[...] = added

    @pl.when(step > 0)
    def _():
        acc_ref[...] += added

    @pl.when(step == pl.num_programs(0) - 1)
    def _():
        out_ref[...] = acc_ref[...].reshape(grids, rows, cells)[:, :chans].astype(bf16)


def spread_body(grids, cells, chans, first, index_ref, grad_ref, out_ref):
    rows = round_up(chans, 8)
    index = index_ref[...]
    high, low = index // cells, index % cells
    count = index.shape[1]
    table = (lax.broadcasted_iota(jnp.int32, (cells, count), 0) == low).astype(f32).astype(bf16)
    grad = grad_ref[:, first : first + chans, :].astype(f32)
    grad = jnp.concatenate([grad, jnp.zeros((grids, rows - chans, cells), f32)], axis=1)
    picked = matmul(grad.reshape(grids * rows, cells).astype(bf16), table)
    total = jnp.zeros((rows, count), f32)
    for grid in range(grids):
        total = jnp.where(high == grid, picked[grid * rows : (grid + 1) * rows], total)
    out_ref[...] = total[:chans]


def pack_body(lid, cam, mid, one_width, lidar_ref, cam_ref, mid_ref, norm_ref, out_ref):
    rows = lidar_ref.shape[2]
    for a in range(3):
        base = a * one_width
        for b in range(3):
            out_ref[:, base + b * lid : base + (b + 1) * lid] = lidar_ref[a, b].astype(bf16)
        used = 3 * lid + 3 * cam
        rest = [cam_ref[a, b] for b in range(3)]
        if one_width > used:
            rest.append(jnp.zeros((rows, one_width - used), f32))
        out_ref[:, base + 3 * lid : base + one_width] = jnp.concatenate(rest, axis=1).astype(bf16)
        for b in range(3):
            start = 3 * one_width + (3 * a + b) * mid
            out_ref[:, start : start + mid] = mid_ref[a, b].astype(bf16)
    norm = norm_ref[...]
    high = norm.astype(bf16)
    left = norm - high.astype(f32)
    middle = left.astype(bf16)
    low = (left - middle.astype(f32)).astype(bf16)
    tail = jnp.concatenate(
        [high.astype(f32), middle.astype(f32), low.astype(f32), jnp.zeros((rows, LANES - 12), f32)],
        axis=1,
    )
    out_ref[:, 3 * one_width + 9 * mid :] = tail.astype(bf16)


def unpack_body(own, lid, cam, one_width, mid, masks, where_ref, *refs):
    parts, (one_ref, two_ref, one_t_ref, two_t_ref, norm_ref, all_ref) = refs[:-6], refs[-6:]
    chan = where_ref[0]
    place = 0
    for part in parts:
        for j in range(part.shape[0]):
            row = pl.multiple_of((chan ^ masks[place]) * own, own)
            all_ref[pl.ds(row, own), :] = part[j]
            place += 1
    one_ref[...] = all_ref[:, : 3 * one_width]
    two_t_ref[...] = all_ref[:, 3 * one_width : 3 * one_width + 9 * mid]
    tail = all_ref[:, 3 * one_width + 9 * mid :].astype(f32)
    norm = tail[:, 0:4] + tail[:, 4:8] + tail[:, 8:12]
    norm_ref[...] = jnp.concatenate([norm, jnp.zeros((norm.shape[0], LANES - 4), f32)], axis=1)
    outs = mid
    for a in range(3):
        for b in range(3):
            to = slice((3 * a + b) * outs, (3 * a + b + 1) * outs)
            start = a * one_width + b * lid
            one_t_ref[0:lid, to] = all_ref[:, start : start + lid].T
            start = 3 * one_width + (3 * a + b) * mid
            two_ref[:, to] = all_ref[:, start : start + mid].T
        start = a * one_width + 3 * lid
        turned = all_ref[:, start : start + one_width - 3 * lid].T
        for b in range(3):
            to = slice((3 * a + b) * outs, (3 * a + b + 1) * outs)
            one_t_ref[lid : lid + cam, to] = turned[b * cam : (b + 1) * cam]


def edge_rows(edge_ref, place_ref, groups, first, last):
    if groups == 2:
        edge_ref[0] = jnp.where(place_ref[1] == 0, last, first)
    else:
        edge_ref[0] = last
        edge_ref[1] = first


def first_body(
    cfg, place_ref, got_ref, above_ref, below_ref, kernel_ref,
    stack_ref, cot_ref, out_ref, sums_ref, edge_ref,
):
    nc, spg, rows, lid, cam, lid_own, cam_own, one_width, groups = cfg
    per_strip = rows // spg
    has_above = place_ref[1] > 0
    has_below = place_ref[1] < groups - 1
    cam_at = 2 * lid_own

    def take(p, first, count):
        if p == 0:
            pieces = [above_ref[c, first : first + count, :] for c in range(nc)]
        elif p == rows + 1:
            pieces = [below_ref[c, first : first + count, :] for c in range(nc)]
        else:
            s, r = (p - 1) // per_strip, (p - 1) % per_strip
            pieces = [got_ref[s * nc + c, first : first + count, cut(r)] for c in range(nc)]
        row = jnp.concatenate([piece.astype(f32) for piece in pieces], axis=0)
        if p == 0:
            row = jnp.where(has_above, row, 0.0)
        if p == rows + 1:
            row = jnp.where(has_below, row, 0.0)
        return row

    used = 3 * lid + 3 * cam
    if one_width > used:
        stack_ref[used:, :] = jnp.zeros((one_width - used, (rows + 2) * LANES), bf16)
    for p in range(rows + 2):
        row = take(p, 0, lid_own)
        for b, shifted in zip((0, 2, 1), (*sides(row), row), strict=True):
            stack_ref[b * lid : (b + 1) * lid, cut(p)] = shifted.astype(bf16)
        row = take(p, cam_at, cam_own)
        for b, shifted in zip((0, 2, 1), (*sides(row), row), strict=True):
            start = 3 * lid + b * cam
            stack_ref[start : start + cam, cut(p)] = shifted.astype(bf16)
        cot_ref[:, cut(p)] = take(p, lid_own, lid_own).astype(bf16)
    total = None
    for a in range(3):
        term = matmul(
            kernel_ref[:, a * one_width : (a + 1) * one_width],
            stack_ref[:, a * LANES : (a + rows) * LANES],
        )
        total = term if total is None else total + term
    finish_sums(total, rows, out_ref, sums_ref, edge_ref, place_ref, groups)


def finish_sums(total, rows, out_ref, sums_ref, edge_ref, place_ref, groups):
    out_ref[...] = total
    sums = squares = None
    for q in range(rows):
        row = total[:, cut(q)]
        sums = row if sums is None else sums + row
        squares = row * row if squares is None else squares + row * row
    sums_ref[...] = column_sums([sums, squares])
    edge_rows(edge_ref, place_ref, groups, total[:, cut(0)], total[:, cut(rows - 1)])


def second_body(
    cfg, place_ref, raw_ref, above_ref, below_ref, stats_ref, norm_ref, kernel_ref,
    out_ref, sums_ref, edge_ref, hidden_ref, means_ref, stack_ref,
):
    rows, chans, groups, pixel_count = cfg
    mean, inv = moments(stats_ref[...], pixel_count)
    columns = to_columns([mean, inv])
    means_ref[...] = columns
    mean, inv = columns[:, 0:1], columns[:, 1:2]
    gain, shift = norm_ref[:, 0:1], norm_ref[:, 1:2]
    for p in range(rows + 2):
        if p == 0:
            raw = above_ref[...]
        elif p == rows + 1:
            raw = below_ref[...]
        else:
            raw = raw_ref[:, cut(p - 1)]
        act = gain * ((raw - mean) * inv) + shift
        hidden = act * sigmoid(act)
        if p == 0:
            hidden = jnp.where(place_ref[1] > 0, hidden, 0.0)
        elif p == rows + 1:
            hidden = jnp.where(place_ref[1] < groups - 1, hidden, 0.0)
        else:
            hidden_ref[:, cut(p - 1)] = hidden
        for b, shifted in zip((0, 2, 1), (*sides(hidden), hidden), strict=True):
            stack_ref[b * chans : (b + 1) * chans, cut(p)] = shifted.astype(bf16)
    total = None
    for a in range(3):
        term = matmul(
            kernel_ref[:, a * 3 * chans : (a + 1) * 3 * chans],
            stack_ref[:, a * LANES : (a + rows) * LANES],
        )
        total = term if total is None else total + term
    finish_sums(total, rows, out_ref, sums_ref, edge_ref, place_ref, groups)


def slope_body(
    cfg, place_ref, raw_ref, above_ref, below_ref, stats_ref, norm_ref, cot_ref, hidden_ref,
    slope_ref, sums_ref, mixed_ref, means_ref,
):
    rows, chans, own, spg, nc, groups, pixel_count = cfg
    per_strip = rows // spg
    mean, inv = moments(stats_ref[...], pixel_count)
    columns = to_columns([mean, inv])
    means_ref[...] = columns
    mean, inv = columns[:, 0:1], columns[:, 1:2]
    gain, shift = norm_ref[:, 2:3], norm_ref[:, 3:4]
    shift_sum = gain_sum = None
    for p in range(rows + 2):
        if p == 0:
            raw = above_ref[...]
        elif p == rows + 1:
            raw = below_ref[...]
        else:
            raw = raw_ref[:, cut(p - 1)]
        centred = (raw - mean) * inv
        act = gain * centred + shift
        gate = sigmoid(act)
        slope = cot_ref[:, cut(p)].astype(f32) * (gate * (1.0 + act * (1.0 - gate)))
        slope_ref[:, cut(p)] = slope
        if 0 < p <= rows:
            shift_sum = slope if shift_sum is None else shift_sum + slope
            term = slope * centred
            gain_sum = term if gain_sum is None else gain_sum + term
            mixed = (hidden_ref[:, cut(p - 1)] + act * gate).astype(bf16)
            s, r = (p - 1) // per_strip, (p - 1) % per_strip
            for c in range(nc):
                mixed_ref[s * nc + c, :, cut(r)] = mixed[c * own : (c + 1) * own]
    sums_ref[...] = column_sums([shift_sum, gain_sum])


def mid_back_body(
    cfg, place_ref, slope_ref, raw_ref, above_ref, below_ref, means_two_ref, stats_ref, norm_ref,
    kernel_ref, raw_one_ref, means_one_ref, cot_ref, hidden_ref,
    out_ref, sums_ref, edge_ref, keep_ref, send_ref, grads_ref, stack_ref, order_ref,
):
    rows, chans, own, nc, groups, pixel_count = cfg
    total = jnp.sum(stats_ref[...], axis=0)
    grads_ref[...] = total
    columns = to_columns([total[0:1] / pixel_count, total[1:2] / pixel_count])
    shift_mean, gain_mean = columns[:, 0:1], columns[:, 1:2]
    mean, inv = means_two_ref[:, 0:1], means_two_ref[:, 1:2]
    scale = norm_ref[:, 2:3] * inv
    for p in range(rows + 2):
        if p == 0:
            raw = above_ref[...]
        elif p == rows + 1:
            raw = below_ref[...]
        else:
            raw = raw_ref[:, cut(p - 1)]
        centred = (raw - mean) * inv
        grad = scale * (slope_ref[:, cut(p)] - shift_mean - centred * gain_mean)
        if p == 0:
            grad = jnp.where(place_ref[1] > 0, grad, 0.0)
        elif p == rows + 1:
            grad = jnp.where(place_ref[1] < groups - 1, grad, 0.0)
        for b, shifted in zip((2, 0, 1), (*sides(grad), grad), strict=True):
            stack_ref[b * chans : (b + 1) * chans, cut(p)] = shifted.astype(bf16)
    back = None
    for a in range(3):
        term = matmul(
            kernel_ref[:, a * 3 * chans : (a + 1) * 3 * chans],
            stack_ref[:, (2 - a) * LANES : (2 - a + rows) * LANES],
        )
        back = term if back is None else back + term
    mean, inv = means_one_ref[:, 0:1], means_one_ref[:, 1:2]
    gain, shift = norm_ref[:, 0:1], norm_ref[:, 1:2]
    shift_sum = gain_sum = None
    slopes = []
    for q in range(rows):
        centred = (raw_one_ref[:, cut(q)] - mean) * inv
        act = gain * centred + shift
        gate = sigmoid(act)
        grad = back[:, cut(q)] + cot_ref[:, cut(q + 1)].astype(f32)
        slope = grad * (gate * (1.0 + act * (1.0 - gate)))
        out_ref[:, cut(q)] = slope
        if q in (0, rows - 1):
            slopes.append(slope)
        shift_sum = slope if shift_sum is None else shift_sum + slope
        term = slope * centred
        gain_sum = term if gain_sum is None else gain_sum + term
    sums_ref[...] = column_sums([shift_sum, gain_sum])
    edge_rows(edge_ref, place_ref, groups, slopes[0], slopes[-1])
    order_ref[...] = hidden_ref[...].astype(bf16)
    low = place_ref[0] & 1
    halves = []
    for side in (low, 1 - low):
        for pair in range(nc // 2):
            start = pl.multiple_of((2 * pair + side) * own, own)
            halves.append(order_ref[pl.ds(start, own), :])
    ordered = jnp.concatenate(halves, axis=0)
    half = chans // 2
    for a in range(3):
        grad = matmul_nt(ordered, stack_ref[:, (2 - a) * LANES : (2 - a + rows) * LANES])
        grad = grad.astype(bf16)
        to = slice(a * 3 * chans, (a + 1) * 3 * chans)
        keep_ref[:, to] = grad[:half]
        send_ref[:, to] = grad[half:]


def first_back_body(
    cfg, place_ref, slope_ref, slope_above_ref, slope_below_ref, raw_ref, above_ref, below_ref,
    means_ref, stats_ref, norm_ref, kernel_ref, cells_ref, mixed_ref, grads_two_ref,
    keep_ref, send_ref, back_ref, grads_ref, stack_ref,
):
    rows, chans, own, lid, cam, lid_own, cam_own, one_width, spg, nc, groups, pixel_count = cfg
    per_strip = rows // spg
    total = jnp.sum(stats_ref[...], axis=0)
    grads_ref[...] = jnp.concatenate(
        [total[1:2], total[0:1], grads_two_ref[1:2], grads_two_ref[0:1]], axis=0
    )
    columns = to_columns([total[0:1] / pixel_count, total[1:2] / pixel_count])
    shift_mean, gain_mean = columns[:, 0:1], columns[:, 1:2]
    mean, inv = means_ref[:, 0:1], means_ref[:, 1:2]
    scale = norm_ref[:, 0:1] * inv
    for p in range(rows + 2):
        if p == 0:
            raw, slope = above_ref[...], slope_above_ref[...]
        elif p == rows + 1:
            raw, slope = below_ref[...], slope_below_ref[...]
        else:
            raw, slope = raw_ref[:, cut(p - 1)], slope_ref[:, cut(p - 1)]
        grad = scale * (slope - shift_mean - (raw - mean) * inv * gain_mean)
        if p == 0:
            grad = jnp.where(place_ref[1] > 0, grad, 0.0)
        elif p == rows + 1:
            grad = jnp.where(place_ref[1] < groups - 1, grad, 0.0)
        for b, shifted in zip((2, 0, 1), (*sides(grad), grad), strict=True):
            stack_ref[b * chans : (b + 1) * chans, cut(p)] = shifted.astype(bf16)
    low = place_ref[0] & 1
    halves = []
    for side in (low, 1 - low):
        for pair in range(nc // 2):
            start = pl.multiple_of(chans + (2 * pair + side) * own, own)
            halves.append(stack_ref[pl.ds(start, own), LANES : (rows + 1) * LANES])
    ordered = jnp.concatenate(halves, axis=0)
    half = chans // 2
    for a in range(3):
        grad = matmul_nt(ordered, cells_ref[:, a * LANES : (a + rows) * LANES]).astype(bf16)
        to = slice(a * one_width, (a + 1) * one_width)
        keep_ref[:, to] = grad[:half]
        send_ref[:, to] = grad[half:]
    back = None
    for a in range(3):
        term = matmul(
            kernel_ref[:, a * 3 * chans : (a + 1) * 3 * chans],
            stack_ref[:, (2 - a) * LANES : (2 - a + rows) * LANES],
        )
        back = term if back is None else back + term
    for s in range(spg):
        cells = slice(s * per_strip * LANES, (s + 1) * per_strip * LANES)
        for c in range(nc):
            block = s * nc + c
            back_ref[block, 0:lid_own, :] = back[c * lid_own : (c + 1) * lid_own, cells].astype(bf16)
            back_ref[block, lid_own : 2 * lid_own, :] = mixed_ref[block]
            start = lid + c * cam_own
            back_ref[block, 2 * lid_own : 2 * lid_own + cam_own, :] = back[
                start : start + cam_own, cells
            ].astype(bf16)


def adam(weight, gradient, first, second, rate):
    first = beta_one * first + (1.0 - beta_one) * gradient
    second = beta_two * second + (1.0 - beta_two) * gradient * gradient
    fix_one = 1.0 - beta_one**STEP
    fix_two = 1.0 - beta_two**STEP
    stepped = first / fix_one / (jnp.sqrt(second / fix_two) + adam_eps)
    return weight - rate * (stepped + weight_decay * weight), first, second


def adam_body(lid, cam, mid, factor_ref, one_ref, two_ref, grad_ref, *refs):
    factor = factor_ref[0]
    ins, outs = refs[:12], refs[12:]
    (wc, mc, vc), (wl, ml, vl), (wm, mm, vm), (wb, mb, vb) = (ins[3 * i : 3 * i + 3] for i in range(4))
    oc, ol, om, ob = (outs[3 * i : 3 * i + 3] for i in range(4))

    def step(reads, writes, at, gradient, rate):
        weight, first, second = (ref[at] for ref in reads)
        for ref, value in zip(writes, adam(weight, factor * gradient, first, second, rate), strict=True):
            ref[at] = value

    for b in range(3):
        at = (0, b)
        step((wl, ml, vl), ol, at, one_ref[:, b * lid : (b + 1) * lid].astype(f32), learn_rate)
        step((wm, mm, vm), om, at, two_ref[:, b * mid : (b + 1) * mid].astype(f32), learn_rate)
    tail = one_ref[:, 3 * lid :].astype(f32)
    for b in range(3):
        step((wc, mc, vc), oc, (0, b), tail[:, b * cam : (b + 1) * cam], learn_rate)

    @pl.when(pl.program_id(0) == 0)
    def _():
        step((wb, mb, vb), ob, ..., grad_ref[...], norm_rate)


def shards(
    cam_feats,
    cell_index,
    lidar_bev,
    w_cam,
    w_lidar,
    w_mid,
    bn_params,
    cotangent,
    m_cam,
    v_cam,
    m_lidar,
    v_lidar,
    m_mid,
    v_mid,
    m_bn,
    v_bn,
):
    grids, lid_own, strip_rows, width = lidar_bev.shape
    cam_own, points = cam_feats.shape
    own = bn_params.shape[1]
    nc = lax.axis_size("chan")
    ns = lax.axis_size("strip")
    lid, cam, chans = nc * lid_own, nc * cam_own, nc * own
    spg = grids // nc
    groups = ns // spg
    members = spg * nc
    rows = spg * strip_rows
    cells = strip_rows * width
    pixel_count = float(grids * cells * ns)
    devices = ns * nc
    one_width = round_up(3 * lid + 3 * cam, 256)
    two_width = 3 * chans
    total_width = 3 * one_width + 3 * two_width
    chan = lax.axis_index("chan")
    group = lax.axis_index("strip") // spg
    place = jnp.stack([chan, group]).astype(jnp.int32)

    def within(member_of):
        return [member for g in range(groups) for member in member_of(g)]

    tile_groups = [[g * members + r for r in range(members)] for g in range(groups)]
    half_groups = [
        [(g * spg + s) * nc + 2 * pair + low for pair in range(nc // 2) for s in range(spg)]
        for g in range(groups)
        for low in range(2)
    ]
    strip_groups = [
        [(g * spg + s) * nc + c for s in range(spg)] for g in range(groups) for c in range(nc)
    ]

    def exchange(blocks, parts):
        return lax.all_to_all(blocks, AXES, 0, 0, axis_index_groups=parts, tiled=True)

    def everywhere(values):
        return lax.all_to_all(
            jnp.broadcast_to(values[None], (devices, *values.shape)), AXES, 0, 0, tiled=True
        )

    def chan_swap(values, bit):
        return lax.ppermute(values, "chan", [(c, c ^ bit) for c in range(nc)])

    def neighbours(edges):
        if groups == 1:
            return edges[0], edges[0]
        if groups == 2:
            pairs = [(i, (i + members) % devices) for i in range(devices)]
            other = lax.ppermute(edges[0], AXES, pairs)
            return other, other
        down = [(i, i + members) for i in range(devices - members)]
        up = [(i + members, i) for i in range(devices - members)]
        return lax.ppermute(edges[0], AXES, down), lax.ppermute(edges[1], AXES, up)

    edge_count = 2 if groups > 2 else 1

    turn = (0, 1, 3, 2)
    packed = call(
        functools.partial(pack_body, lid, cam, chans, one_width),
        struct((own, total_width + LANES), bf16),
    )(w_lidar.transpose(turn), w_cam.transpose(turn), w_mid, bn_params.T)
    parts, masks = [packed[None]], [0]
    bit = nc // 2
    while bit:
        stacked = parts[0] if len(parts) == 1 else jnp.concatenate(parts, axis=0)
        parts.append(chan_swap(stacked, bit))
        masks += [mask ^ bit for mask in masks]
        bit //= 2

    index_row = cell_index.reshape(1, points)
    block = math.gcd(points, 2048)
    pooled = pl.pallas_call(
        functools.partial(pool_body, grids, cells, cam_own),
        grid=(points // block,),
        in_specs=[
            pl.BlockSpec((1, block), lambda i: (0, i)),
            pl.BlockSpec((cam_own, block), lambda i: (0, i)),
        ],
        out_specs=pl.BlockSpec((grids, cam_own, cells), lambda i: (0, 0, 0)),
        out_shape=struct((grids, cam_own, cells), bf16),
        scratch_shapes=[pltpu.VMEM((grids * round_up(cam_own, 8), cells), f32)],
        compiler_params=pltpu.CompilerParams(vmem_limit_bytes=VMEM_BYTES),
    )(index_row, cam_feats)
    joined = jnp.concatenate(
        [
            lidar_bev.reshape(grids, lid_own, cells),
            cotangent.reshape(grids, own, cells),
            pooled,
        ],
        axis=1,
    )
    got = exchange(joined, tile_groups)
    depth = joined.shape[1]
    last = got[members - nc :, :, cells - width :]
    first = got[:nc, :, :width]
    if groups == 2:
        edges = jnp.where(group == 0, last, first)[None]
    else:
        edges = jnp.stack([last, first])
    above, below = neighbours(edges)

    kernel_one, kernel_two, kernel_one_t, kernel_two_t, norm = call(
        functools.partial(unpack_body, own, lid, cam, one_width, chans, masks),
        [
            struct((chans, 3 * one_width), bf16),
            struct((chans, 3 * two_width), bf16),
            struct((lid + cam, 3 * two_width), bf16),
            struct((chans, 3 * two_width), bf16),
            struct((chans, LANES), f32),
        ],
        scratch=[pltpu.VMEM((chans, total_width + LANES), bf16)],
        smem=1,
    )(place, *parts)

    area = rows * LANES
    wide = (rows + 2) * LANES
    cells_stack, cot, raw_one, sums_one, edges_one = call(
        functools.partial(
            first_body, (nc, spg, rows, lid, cam, lid_own, cam_own, one_width, groups)
        ),
        [
            struct((one_width, wide), bf16),
            struct((chans, wide), bf16),
            struct((chans, area), f32),
            struct((2, chans), f32),
            struct((edge_count, chans, LANES), f32),
        ],
        smem=1,
    )(place, got, above, below, kernel_one)

    above_one, below_one = neighbours(edges_one)
    stats_one = everywhere(sums_one)
    raw_two, sums_two, edges_two, hidden, means_one = call(
        functools.partial(second_body, (rows, chans, groups, pixel_count)),
        [
            struct((chans, area), f32),
            struct((2, chans), f32),
            struct((edge_count, chans, LANES), f32),
            struct((chans, area), f32),
            struct((chans, LANES), f32),
        ],
        scratch=[pltpu.VMEM((two_width, wide), bf16)],
        smem=1,
    )(place, raw_one, above_one, below_one, stats_one, norm, kernel_two)

    above_two, below_two = neighbours(edges_two)
    stats_two = everywhere(sums_two)
    slope_two, sums_three, mixed_blocks, means_two = call(
        functools.partial(slope_body, (rows, chans, own, spg, nc, groups, pixel_count)),
        [
            struct((chans, wide), f32),
            struct((2, chans), f32),
            struct((members, own, cells), bf16),
            struct((chans, LANES), f32),
        ],
        smem=1,
    )(place, raw_two, above_two, below_two, stats_two, norm, cot, hidden)

    stats_three = everywhere(sums_three)
    slope_one, sums_four, edges_four, keep_two, send_two, grads_two = call(
        functools.partial(mid_back_body, (rows, chans, own, nc, groups, pixel_count)),
        [
            struct((chans, area), f32),
            struct((2, chans), f32),
            struct((edge_count, chans, LANES), f32),
            struct((chans // 2, 3 * two_width), bf16),
            struct((chans // 2, 3 * two_width), bf16),
            struct((2, chans), f32),
        ],
        scratch=[pltpu.VMEM((two_width, wide), bf16), pltpu.VMEM((chans, area), bf16)],
        smem=1,
    )(
        place, slope_two, raw_two, above_two, below_two, means_two, stats_three, norm,
        kernel_two_t, raw_one, means_one, cot, hidden,
    )

    above_four, below_four = neighbours(edges_four)
    got_two = chan_swap(send_two, 1)
    stats_four = everywhere(sums_four)
    keep_one, send_one, back_blocks, grad_bn_all = call(
        functools.partial(
            first_back_body,
            (rows, chans, own, lid, cam, lid_own, cam_own, one_width, spg, nc, groups, pixel_count),
        ),
        [
            struct((chans // 2, 3 * one_width), bf16),
            struct((chans // 2, 3 * one_width), bf16),
            struct((members, depth, cells), bf16),
            struct((4, chans), f32),
        ],
        scratch=[pltpu.VMEM((two_width, wide), bf16)],
        smem=1,
    )(
        place, slope_one, above_four, below_four, raw_one, above_one, below_one, means_one,
        stats_four, norm, kernel_one_t, cells_stack, mixed_blocks, grads_two,
    )

    got_one = chan_swap(send_one, 1)
    halved = jnp.concatenate(
        [
            (keep_one.astype(f32) + got_one.astype(f32)).astype(bf16),
            (keep_two.astype(f32) + got_two.astype(f32)).astype(bf16),
        ],
        axis=1,
    )
    piece_rows = own // spg
    pieces = exchange(halved.reshape(members // 2, piece_rows, total_width), half_groups)
    piece = jnp.sum(pieces.astype(f32), axis=0)
    shift = members
    while shift < devices:
        pairs = [(i, i ^ shift) for i in range(devices)]
        sent = piece.astype(bf16)
        piece = sent.astype(f32) + lax.ppermute(sent, AXES, pairs).astype(f32)
        shift *= 2
    piece = piece.astype(bf16)
    own_grads = exchange(
        jnp.broadcast_to(piece[None], (spg, piece_rows, total_width)), strip_groups
    ).reshape(own, total_width)
    grad_bn = lax.dynamic_slice(grad_bn_all, (0, chan * own), (4, own))
    squares = jnp.sum(jnp.square(own_grads.astype(f32))) + jnp.sum(grad_bn * grad_bn)
    bit = 1
    while bit < nc:
        squares = squares + chan_swap(squares, bit)
        bit *= 2
    grad_norm = jnp.sqrt(squares)
    factor = jnp.minimum(1.0, clip_norm / (grad_norm + 1e-06))

    home = exchange(back_blocks, tile_groups)
    grad_lidar = home[:, :lid_own].astype(f32).reshape(lidar_bev.shape)
    mixed = home[:, lid_own : lid_own + own].astype(f32).reshape(cotangent.shape)
    grad_cam = pl.pallas_call(
        functools.partial(spread_body, grids, cells, cam_own, lid_own + own),
        grid=(points // block,),
        in_specs=[
            pl.BlockSpec((1, block), lambda i: (0, i)),
            pl.BlockSpec((grids, depth, cells), lambda i: (0, 0, 0)),
        ],
        out_specs=pl.BlockSpec((cam_own, block), lambda i: (0, i)),
        out_shape=struct((cam_own, points), f32),
        compiler_params=pltpu.CompilerParams(vmem_limit_bytes=VMEM_BYTES),
    )(index_row, home)

    tall = lambda array: array.transpose(turn)
    state = [
        *(tall(array) for array in (w_cam, m_cam, v_cam)),
        *(tall(array) for array in (w_lidar, m_lidar, v_lidar)),
        w_mid, m_mid, v_mid, bn_params, m_bn, v_bn,
    ]
    state_specs = [
        pl.BlockSpec((1, *array.shape[1:]), lambda a: (a, 0, 0, 0))
        if array.ndim == 4
        else pl.BlockSpec(array.shape, lambda a: (0, 0))
        for array in state
    ]
    updated = pl.pallas_call(
        functools.partial(adam_body, lid, cam, chans),
        grid=(3,),
        in_specs=[
            pl.BlockSpec(memory_space=pltpu.SMEM),
            pl.BlockSpec((own, one_width), lambda a: (0, a)),
            pl.BlockSpec((own, two_width), lambda a: (0, a)),
            pl.BlockSpec((4, own), lambda a: (0, 0)),
            *state_specs,
        ],
        out_specs=state_specs,
        out_shape=[struct(array.shape, f32) for array in state],
        compiler_params=pltpu.CompilerParams(vmem_limit_bytes=VMEM_BYTES),
    )(
        factor.reshape(1), own_grads[:, : 3 * one_width], own_grads[:, 3 * one_width :], grad_bn, *state
    )
    turned = [tall(array) for array in updated[:6]]
    return (mixed, grad_cam, grad_lidar, grad_norm, *turned, *updated[6:])


def solution(mesh):
    return jax.shard_map(
        shards,
        mesh=mesh,
        in_specs=(
            P("chan", "strip"),
            P("strip"),
            P(None, "chan", "strip", None),
            P(None, None, None, "chan"),
            P(None, None, None, "chan"),
            P(None, None, "chan", None),
            P(None, "chan"),
            P(None, "chan", "strip", None),
            P(None, None, None, "chan"),
            P(None, None, None, "chan"),
            P(None, None, None, "chan"),
            P(None, None, None, "chan"),
            P(None, None, "chan", None),
            P(None, None, "chan", None),
            P(None, "chan"),
            P(None, "chan"),
        ),
        out_specs=(
            P(None, "chan", "strip", None),
            P("chan", "strip"),
            P(None, "chan", "strip", None),
            P(),
            P(None, None, None, "chan"),
            P(None, None, None, "chan"),
            P(None, None, None, "chan"),
            P(None, None, None, "chan"),
            P(None, None, None, "chan"),
            P(None, None, None, "chan"),
            P(None, None, "chan", None),
            P(None, None, "chan", None),
            P(None, None, "chan", None),
            P(None, "chan"),
            P(None, "chan"),
            P(None, "chan"),
        ),
        check_vma=False,
    )
```

time: 620 us -> 207 us (0.33)
  matrix products: 194 us -> 0 us
  waiting for transfers between devices: 208 us -> 45.7 us
  Pallas kernels: 0 us -> 41.4 us
  local copies, waits for them, and re-layouts: 49.7 us -> 19.5 us
  other arithmetic: 31.5 us -> 7.02 us
  blocking collectives: 89.3 us -> 64.9 us
  between operations: 19.9 us -> 4.71 us
    dot_general x113 -> x0, matrix products: 194 us -> none  [the longest x16 46.4 us: pool_step(): lax.dot_general(feature, table, (((1,), (1,)), ((), ())), preferred_eleme...]
    psum x5 -> x0, blocking collectives: 89.3 us -> none  [the longest x1 21.4 us: shards(): lax.psum((jnp.sum(encoded, axis=(0, 2, 3)), jnp.sum(encoded * encoded, ax...]
    all_gather x2 -> x0, waiting for transfers between devices: 74.9 us -> none  [the longest x1 43.6 us: gather_inputs(): gathered = lax.all_gather(rimmed, 'chan', axis=1, tiled=True)]
    reduce_scatter x2 -> x0, waiting for transfers between devices: 72.3 us -> none  [the longest x1 42.9 us: shards(): lax.psum_scatter(partial_mid, 'chan', scatter_dimension=1, tiled=True)]
    all_to_all x0 -> x5, blocking collectives: none -> 64.9 us  [the longest x4 42.6 us: everywhere(): lax.all_to_all(jnp.broadcast_to(values[None], (devices, *values.shape)),...]
    pallas_call x0 -> x10, Pallas kernels: none -> 41.4 us  [the longest x7 26.2 us: run(): pl.pallas_call(body, out_shape=out_shape, in_specs=specs, out_specs=jax.t...]
    psum x1 -> x0, waiting for transfers between devices: 33.9 us -> none  [shards(): lax.psum((grad_wc_local, grad_wl_local, grad_mid_local), 'strip')]
    all_to_all x0 -> x3, waiting for transfers between devices: none -> 17.9 us  [exchange(): lax.all_to_all(blocks, AXES, 0, 0, axis_index_groups=parts, tiled=True)]
  transfers between devices with their start and end apart: 13 -> 14, of which waited for: 9 -> 8; matrix products, arithmetic and copies ran while one was open for 12% -> 5% of each run, Pallas kernels for 0% -> 11%
where the time goes in v1:
time: 207 us; the launch traced here: 206 us
  blocking collectives  64.9 us (31%)
  waiting for transfers between devices  45.7 us (22%)
  Pallas kernels  41.4 us (20%)
  starting transfers between devices  22.7 us (11%)
  local copies, waits for them, and re-layouts  19.5 us (9%)
  other arithmetic  7.02 us (3%)
  between operations  4.71 us (2%)
    all_to_all x4, blocking collectives, everywhere(): lax.all_to_all(jnp.broadcast_to(values[None], (devices, *values.shape)),...  42.6 us
    pallas_call x7, Pallas kernels, run(): pl.pallas_call(body, out_shape=out_shape, in_specs=specs, out_specs=jax.t...  26.2 us
    all_to_all x1, blocking collectives, exchange(): lax.all_to_all(blocks, AXES, 0, 0, axis_index_groups=parts, tiled=True)  22.4 us
    all_to_all x3, waiting for transfers between devices, exchange(): lax.all_to_all(blocks, AXES, 0, 0, axis_index_groups=parts, tiled=True)  17.9 us
    ppermute x1, waiting for transfers between devices, shards(): piece = sent.astype(f32) + lax.ppermute(sent, AXES, pairs).astype(f32)  16.9 us
    all_to_all x3, starting transfers between devices, exchange(): lax.all_to_all(blocks, AXES, 0, 0, axis_index_groups=parts, tiled=True)  12 us
    unnamed x45, local copies, waits for them, and re-layouts  10.4 us
    ppermute x6, waiting for transfers between devices, chan_swap(): return lax.ppermute(values, 'chan', [(c, c ^ bit) for c in range(nc)])  8.21 us
  transfers between devices with their start and end apart: 14, of which 8 were waited for; matrix products, arithmetic and copies ran while one was open for 5% of the time, Pallas kernels for 11%

profile of v1, /device:TPU:0, one launch (start us, length us, event | category | flops | bytes accessed | tf_op | source)
XLA Modules:
  0.0 205.9 jit_solution(4986548478584384365)
XLA Ops:
  1.4 1.1 copy-done.1
  2.5 1.1 copy-done.3
  3.5 1.0 copy-done.8
  4.6 3.0 %collective-permute-start.1 = (bf16[1,64,5504]{2,1,0:T(8,128)(2,1)S(1)}, bf16[1,64,5504]{2,1,0:T(8,128)(2,1)S(1)}, u32[]{:S(2)}, u32[]{:S(2)}) collective-permute-start(bf16[1,64,5504]{2,1,0:T(8,128)(2,1)S(1)} %bitcast.23), channel_id=1, source_target_pairs={{0,2},{1,3},{2,0},{3,1},{4,6},{5,7},{6,4},{7,5},{8,10},{9,11},{10,... | collective-permute-start | bytes 2113544 | tf_op jit(solution)/shard_map/ppermute | solution.py:554
  8.0 1.4 reshape.68
  9.4 5.5 %shard_map.279 = bf16[16,20,256]{2,1,0:T(8,128)(2,1)S(1)} custom-call(s32[1,16384]{1,0:T(1,128)S(1)} %bitcast.34, bf16[20,16384]{1,0:T(8,128)(2,1)S(1)} %copy-done.10), custom_call_target="tpu_custom_call" | custom-call | tf_op jit(solution)/shard_map/pallas_call | solution.py:584
  14.9 1.1 pad_maximum_fusion.2
  16.1 4.2 %all-to-all-start = ((bf16[16,148,256]{2,1,0:T(8,128)(2,1)}), bf16[16,148,256]{2,1,0:T(8,128)(2,1)S(1)}, u32[]{:S(2)}, u32[]{:S(2)}) async-start(bf16[16,148,256]{2,1,0:T(8,128)(2,1)} %pad_maximum_fusion.2), calls=%async_computation | async-start | bytes 2490368 | tf_op jit(solution)/shard_map/all_to_all | solution.py:546
  20.2 3.5 %collective-permute-done.1.refs_1_ = bf16[1,64,5504]{2,1,0:T(8,128)(2,1)S(1)} collective-permute-done((bf16[1,64,5504]{2,1,0:T(8,128)(2,1)S(1)}, bf16[1,64,5504]{2,1,0:T(8,128)(2,1)S(1)}, u32[]{:S(2)}, u32[]{:S(2)}) %collective-permute-start.1) | collective-permute-done | bytes 704544 | tf_op jit(solution)/shard_map/ppermute | solution.py:554
  23.7 1.2 pad_maximum_fusion
  25.0 14.0 %all-to-all-done.got_ref = bf16[16,148,256]{2,1,0:T(8,128)(2,1)S(1)} async-done(((bf16[16,148,256]{2,1,0:T(8,128)(2,1)}), bf16[16,148,256]{2,1,0:T(8,128)(2,1)S(1)}, u32[]{:S(2)}, u32[]{:S(2)}) %all-to-all-start) | async-done | bytes 1212448 | tf_op jit(solution)/shard_map/all_to_all | solution.py:546
  39.0 2.7 %collective-permute-start = (bf16[4,148,128]{2,1,0:T(8,128)(2,1)S(1)}, bf16[4,148,128]{2,1,0:T(8,128)(2,1)S(1)}, u32[]{:S(2)}, u32[]{:S(2)}) collective-permute-start(bf16[4,148,128]{2,1,0:T(8,128)(2,1)S(1)} %slice_select_fusion), channel_id=1, source_target_pairs={{0,16},{1,17},{2,18},{3,19},{4,20},{5,21},{6,22},{7,23},{8,24},{9,... | collective-permute-start | bytes 454664 | tf_op jit(solution)/shard_map/ppermute | solution.py:561
  41.7 4.1 %shard_map.281 = (bf16[256,3072]{1,0:T(8,128)(2,1)}, bf16[256,2304]{1,0:T(8,128)(2,1)S(1)}, bf16[336,2304]{1,0:T(8,128)(2,1)}, bf16[256,2304]{1,0:T(8,128)(2,1)S(1)}, f32[256,128]{1,0:T(8,128)S(1)}) custom-call(s32[2]{0:T(128)S(1)} %pad_add_fusion.where_ref.place_ref, bf16[1,64,5504]{2,1,0:T(8,128)(2,1)S(1)} %bitcast.25, ...), custom_call_target="tpu_custom_call" | custom-call | tf_op jit(solution)/shard_map/pallas_call | solution.py:39
  45.8 2.7 %collective-permute-done.above_ref.below_ref = bf16[4,148,128]{2,1,0:T(8,128)(2,1)S(1)} collective-permute-done((bf16[4,148,128]{2,1,0:T(8,128)(2,1)S(1)}, bf16[4,148,128]{2,1,0:T(8,128)(2,1)S(1)}, u32[]{:S(2)}, u32[]{:S(2)}) %collective-permute-start) | collective-permute-done | bytes 151584 | tf_op jit(solution)/shard_map/ppermute | solution.py:561
  48.4 1.4 copy-done.5
  49.8 4.2 %shard_map.282 = (bf16[1024,1280]{1,0:T(8,128)(2,1)}, bf16[256,1280]{1,0:T(8,128)(2,1)S(1)}, f32[256,1024]{1,0:T(8,128)S(1)}, f32[2,256]{1,0:T(2,128)S(1)}, f32[1,256,128]{2,1,0:T(8,128)S(1)}) custom-call(s32[2]{0:T(128)S(1)} %pad_add_fusion.where_ref.place_ref, bf16[16,148,256]{2,1,0:T(8,128)(2,1)S(1)} %all-to-all-done.got_ref, ...), custom_call_target="tpu_custom_call" | custom-call | tf_op jit(solution)/shard_map/pallas_call | solution.py:39
  54.0 12.6 %all_to_all.40.stats_ref = f32[32,2,256]{2,1,0:T(2,128)S(1)} all-to-all(f32[32,2,256]{2,1,0:T(2,128)S(1)} %broadcast_in_dim.13), channel_id=1, replica_groups=mesh['strip'=8,'chan'=4] {'strip','chan'}, dimensions={0} | all-to-all | bytes 131072 | tf_op jit(solution)/shard_map/all_to_all | solution.py:549
  66.6 2.8 %shard_map.283 = (f32[256,1024]{1,0:T(8,128)S(1)}, f32[2,256]{1,0:T(2,128)S(1)}, f32[1,256,128]{2,1,0:T(8,128)S(1)}, f32[256,1024]{1,0:T(8,128)S(1)}, f32[256,128]{1,0:T(8,128)S(1)}) custom-call(s32[2]{0:T(128)S(1)} %pad_add_fusion.where_ref.place_ref, f32[256,1024]{1,0:T(8,128)S(1)} %get-tuple-element.58.raw_ref.raw_one_ref, ...), custom_call_target="tpu_custom_call" | custom-call | tf_op jit(solution)/shard_map/pallas_call | solution.py:39
  70.3 10.0 %all_to_all.41.stats_ref = f32[32,2,256]{2,1,0:T(2,128)S(1)} all-to-all(f32[32,2,256]{2,1,0:T(2,128)S(1)} %broadcast_in_dim.14), channel_id=1, replica_groups=mesh['strip'=8,'chan'=4] {'strip','chan'}, dimensions={0} | all-to-all | bytes 131072 | tf_op jit(solution)/shard_map/all_to_all | solution.py:549
  80.3 1.8 shard_map.284
  82.2 1.0 copy-done.6
  83.2 9.6 %all_to_all.42.stats_ref = f32[32,2,256]{2,1,0:T(2,128)S(1)} all-to-all(f32[32,2,256]{2,1,0:T(2,128)S(1)} %broadcast_in_dim.15), channel_id=1, replica_groups=mesh['strip'=8,'chan'=4] {'strip','chan'}, dimensions={0} | all-to-all | bytes 131072 | tf_op jit(solution)/shard_map/all_to_all | solution.py:549
  92.8 5.7 %shard_map.285 = (f32[256,1024]{1,0:T(8,128)S(1)}, f32[2,256]{1,0:T(2,128)S(1)}, f32[1,256,128]{2,1,0:T(8,128)S(1)}, bf16[128,2304]{1,0:T(8,128)(2,1)S(1)}, bf16...) custom-call(s32[2]{0:T(128)S(1)} %pad_add_fusion.where_ref.place_ref, f32[256,1280]{1,0:T(8,128)} %copy-done.6, ...), custom_call_target="tpu_custom_call" | custom-call | tf_op jit(solution)/shard_map/pallas_call | solution.py:39
  99.4 10.3 %all_to_all.43.stats_ref = f32[32,2,256]{2,1,0:T(2,128)S(1)} all-to-all(f32[32,2,256]{2,1,0:T(2,128)S(1)} %broadcast_in_dim.16), channel_id=1, replica_groups=mesh['strip'=8,'chan'=4] {'strip','chan'}, dimensions={0} | all-to-all | bytes 131072 | tf_op jit(solution)/shard_map/all_to_all | solution.py:549
  109.7 7.5 %shard_map.286 = (bf16[128,3072]{1,0:T(8,128)(2,1)S(1)}, bf16[128,3072]{1,0:T(8,128)(2,1)S(1)}, bf16[16,148,256]{2,1,0:T(8,128)(2,1)}, f32[4,256]{1,0:T(4,128)S(1)}) custom-call(s32[2]{0:T(128)S(1)} %pad_add_fusion.where_ref.place_ref, f32[256,1024]{1,0:T(8,128)S(1)} %get-tuple-element.73.slope_ref, ...), custom_call_target="tpu_custom_call" | custom-call | tf_op jit(solution)/shard_map/pallas_call | solution.py:39
  117.4 2.1 collective-permute-done.6
  119.8 22.4 %all_to_all.44 = bf16[8,16,5376]{2,1,0:T(8,128)(2,1)S(1)} all-to-all(bf16[8,16,5376]{2,1,0:T(8,128)(2,1)S(1)} %bitcast.40), channel_id=1, replica_groups={{0,4,8,12,2,6,10,14},{1,5,9,13,3,7,11,15},{16,20,24,28,18,22,26,30},{17..., dimensions={0} | all-to-all | bytes 2752512 | tf_op jit(solution)/shard_map/all_to_all | solution.py:546
  142.1 3.7 %all-to-all-start.5 = ((bf16[16,148,256]{2,1,0:T(8,128)(2,1)}), bf16[16,148,256]{2,1,0:T(8,128)(2,1)S(1)}, u32[]{:S(2)}, u32[]{:S(2)}) async-start(bf16[16,148,256]{2,1,0:T(8,128)(2,1)} %get-tuple-element.80), calls=%async_computation.5 | async-start | bytes 2490368 | tf_op jit(solution)/shard_map/all_to_all | solution.py:546
  146.1 1.0 collective-permute-start.8
  147.0 16.9 %collective-permute-done.8 = bf16[16,5376]{1,0:T(8,128)(2,1)S(1)} collective-permute-done((bf16[16,5376]{1,0:T(8,128)(2,1)S(1)}, bf16[16,5376]{1,0:T(8,128)(2,1)S(1)}, u32[]{:S(2)}, u32[]{:S(2)}) %collective-permute-start.8) | collective-permute-done | bytes 172064 | tf_op jit(solution)/shard_map/ppermute | solution.py:725
  164.0 4.0 %all-to-all-done.5.grad_ref = bf16[16,148,256]{2,1,0:T(8,128)(2,1)S(1)} async-done(((bf16[16,148,256]{2,1,0:T(8,128)(2,1)}), bf16[16,148,256]{2,1,0:T(8,128)(2,1)S(1)}, u32[]{:S(2)}, u32[]{:S(2)}) %all-to-all-start.5) | async-done | bytes 1212448 | tf_op jit(solution)/shard_map/all_to_all | solution.py:546
  167.9 0.9 broadcast_in_dim.17
  168.9 4.2 %all-to-all-start.7 = ((bf16[4,16,5376]{2,1,0:T(8,128)(2,1)}), bf16[4,16,5376]{2,1,0:T(8,128)(2,1)}, u32[]{:S(2)}, u32[]{:S(2)}) async-start(bf16[4,16,5376]{2,1,0:T(8,128)(2,1)} %broadcast_in_dim.17), calls=%async_computation.7 | async-start | bytes 1376256 | tf_op jit(solution)/shard_map/all_to_all | solution.py:546
  173.7 1.1 slice_convert_fusion
  174.8 2.7 %reshape.80 = f32[16,64,2,128]{3,2,1,0:T(2,128)} reshape(f32[16,64,256]{2,1,0:T(8,128)} %get-tuple-element.100) | data formatting | bytes 2097152 | tf_op jit(solution)/shard_map/reshape | solution.py:741
  177.6 1.5 reshape.78
  179.0 6.3 %shard_map.287 = f32[20,16384]{1,0:T(8,128)} custom-call(s32[1,16384]{1,0:T(1,128)S(1)} %bitcast.35, bf16[16,148,256]{2,1,0:T(8,128)(2,1)S(1)} %all-to-all-done.5.grad_ref), custom_call_target="tpu_custom_call" | custom-call | tf_op jit(solution)/shard_map/pallas_call | solution.py:743
  185.4 1.1 slice.29.two_ref
  186.5 1.0 slice.28.one_ref
  187.5 2.1 multiply_reduce_fusion
  190.9 1.0 collective-permute-start.9
  192.8 1.4 collective-permute-start.10
  194.2 2.3 %collective-permute-done.10 = f32[]{:T(128)} collective-permute-done((f32[]{:T(128)}, f32[]{:T(128)}, u32[]{:S(2)}, u32[]{:S(2)}) %collective-permute-start.10) | collective-permute-done | bytes 36 | tf_op jit(solution)/shard_map/ppermute | solution.py:554
  197.3 1.1 copy-done.13
  198.4 1.1 copy-done.14
  199.5 1.0 copy-done.15
  200.4 1.0 copy-done.16
  201.4 3.4 %shard_map.288 = (f32[3,3,64,80]{3,2,1,0:T(8,128)}, f32[3,3,64,80]{3,2,1,0:T(8,128)}, f32[3,3,64,80]{3,2,1,0:T(8,128)}, f32[3,3,64,256]{3,2,1,0:T(8,128)}, f32[3...) custom-call(f32[1]{0:T(128)} %bitcast.11.factor_ref, ...), custom_call_target="tpu_custom_call" | custom-call | tf_op jit(solution)/shard_map/pallas_call | solution.py:767
  (63 shorter events, 4.8 us)
Async XLA Ops:
  1.4 1.1 copy-start.1
  2.5 1.1 copy-start.3
  3.5 1.0 copy-start.8
  4.5 3.2 %copy-start.21 = (bf16[16,64,2,128]{3,2,1,0:T(2,128)(2,1)S(1)}, bf16[16,64,2,128]{3,2,1,0:T(2,128)(2,1)}, u32[]{:S(2)}) copy-start(bf16[16,64,2,128]{3,2,1,0:T(2,128)(2,1)} %param.18) | copy-start | bytes 1572868
  4.6 4.8 %copy-start.10 = (bf16[20,16384]{1,0:T(8,128)(2,1)S(1)}, bf16[20,16384]{1,0:T(8,128)(2,1)}, u32[]{:S(2)}) copy-start(bf16[20,16384]{1,0:T(8,128)(2,1)} %feat_ref.1) | copy-start | bytes 1966084
  4.6 4.8 %copy-start.17 = (s32[16384]{0:T(1024)S(1)}, s32[16384]{0:T(1024)}, u32[]{:S(2)}) copy-start(s32[16384]{0:T(1024)} %param.17) | copy-start | bytes 196612
  4.6 19.1 %collective-permute-start.1 = (bf16[1,64,5504]{2,1,0:T(8,128)(2,1)S(1)}, bf16[1,64,5504]{2,1,0:T(8,128)(2,1)S(1)}, u32[]{:S(2)}, u32[]{:S(2)}) collective-permute-start(bf16[1,64,5504]{2,1,0:T(8,128)(2,1)S(1)} %bitcast.23), channel_id=1, source_target_pairs={{0,2},{1,3},{2,0},{3,1},{4,6},{5,7},{6,4},{7,5},{8,10},{9,11},{10,... | collective-permute-start | bytes 2113544 | tf_op jit(solution)/shard_map/ppermute | solution.py:554
  16.1 22.9 %all-to-all-start = ((bf16[16,148,256]{2,1,0:T(8,128)(2,1)}), bf16[16,148,256]{2,1,0:T(8,128)(2,1)S(1)}, u32[]{:S(2)}, u32[]{:S(2)}) async-start(bf16[16,148,256]{2,1,0:T(8,128)(2,1)} %pad_maximum_fusion.2), calls=%async_computation | async-start | bytes 2490368 | tf_op jit(solution)/shard_map/all_to_all | solution.py:546
  25.0 16.7 %collective-permute-start.2 = (bf16[2,64,5504]{2,1,0:T(8,128)(2,1)}, bf16[2,64,5504]{2,1,0:T(8,128)(2,1)}, u32[]{:S(2)}, u32[]{:S(2)}) collective-permute-start(bf16[2,64,5504]{2,1,0:T(8,128)(2,1)} %pad_maximum_fusion), channel_id=1, source_target_pairs={{0,1},{1,0},{2,3},{3,2},{4,5},{5,4},{6,7},{7,6},{8,9},{9,8},{10,11... | collective-permute-start | bytes 4227080 | tf_op jit(solution)/shard_map/ppermute | solution.py:554
  39.0 9.5 %collective-permute-start = (bf16[4,148,128]{2,1,0:T(8,128)(2,1)S(1)}, bf16[4,148,128]{2,1,0:T(8,128)(2,1)S(1)}, u32[]{:S(2)}, u32[]{:S(2)}) collective-permute-start(bf16[4,148,128]{2,1,0:T(8,128)(2,1)S(1)} %slice_select_fusion), channel_id=1, source_target_pairs={{0,16},{1,17},{2,18},{3,19},{4,20},{5,21},{6,22},{7,23},{8,24},{9,... | collective-permute-start | bytes 454664 | tf_op jit(solution)/shard_map/ppermute | solution.py:561
  45.8 8.2 %copy-start.7 = (bf16[256,2304]{1,0:T(8,128)(2,1)}, bf16[256,2304]{1,0:T(8,128)(2,1)S(1)}, u32[]{:S(2)}) copy-start(bf16[256,2304]{1,0:T(8,128)(2,1)S(1)} %get-tuple-element.71.kernel_ref) | copy-start | bytes 3538948
  48.4 1.4 copy-start.5
  54.0 12.6 %collective-permute-start.3 = (f32[256,128]{1,0:T(8,128)S(1)}, f32[256,128]{1,0:T(8,128)S(1)}, u32[]{:S(2)}, u32[]{:S(2)}) collective-permute-start(f32[256,128]{1,0:T(8,128)S(1)} %bitcast.38), channel_id=1, source_target_pairs={{0,16},{1,17},{2,18},{3,19},{4,20},{5,21},{6,22},{7,23},{8,24},{9,... | collective-permute-start | bytes 393224 | tf_op jit(solution)/shard_map/ppermute | solution.py:561
  69.5 12.7 %copy-start = (f32[256,1024]{1,0:T(8,128)}, f32[256,1024]{1,0:T(8,128)S(1)}, u32[]{:S(2)}) copy-start(f32[256,1024]{1,0:T(8,128)S(1)} %get-tuple-element.67.hidden_ref) | copy-start | bytes 3145732
  69.5 10.8 %collective-permute-start.4 = (f32[256,128]{1,0:T(8,128)S(1)}, f32[256,128]{1,0:T(8,128)S(1)}, u32[]{:S(2)}, u32[]{:S(2)}) collective-permute-start(f32[256,128]{1,0:T(8,128)S(1)} %bitcast.39), channel_id=1, source_target_pairs={{0,16},{1,17},{2,18},{3,19},{4,20},{5,21},{6,22},{7,23},{8,24},{9,... | collective-permute-start | bytes 393224 | tf_op jit(solution)/shard_map/ppermute | solution.py:561
  82.1 1.1 copy-start.6
  98.5 18.8 %collective-permute-start.7 = (bf16[128,2304]{1,0:T(8,128)(2,1)S(1)}, bf16[128,2304]{1,0:T(8,128)(2,1)S(1)}, u32[]{:S(2)}, u32[]{:S(2)}) collective-permute-start(bf16[128,2304]{1,0:T(8,128)(2,1)S(1)} %get-tuple-element.84), channel_id=1, source_target_pairs={{0,1},{1,0},{2,3},{3,2},{4,5},{5,4},{6,7},{7,6},{8,9},{9,8},{10,11... | collective-permute-start | bytes 1769480 | tf_op jit(solution)/shard_map/ppermute | solution.py:554
  98.7 11.0 %collective-permute-start.5 = (f32[256,128]{1,0:T(8,128)S(1)}, f32[256,128]{1,0:T(8,128)S(1)}, u32[]{:S(2)}, u32[]{:S(2)}) collective-permute-start(f32[256,128]{1,0:T(8,128)S(1)} %bitcast.37), channel_id=1, source_target_pairs={{0,16},{1,17},{2,18},{3,19},{4,20},{5,21},{6,22},{7,23},{8,24},{9,... | collective-permute-start | bytes 393224 | tf_op jit(solution)/shard_map/ppermute | solution.py:561
  117.2 2.3 %collective-permute-start.6 = (bf16[128,3072]{1,0:T(8,128)(2,1)S(1)}, bf16[128,3072]{1,0:T(8,128)(2,1)S(1)}, u32[]{:S(2)}, u32[]{:S(2)}) collective-permute-start(bf16[128,3072]{1,0:T(8,128)(2,1)S(1)} %get-tuple-element.82), channel_id=1, source_target_pairs={{0,1},{1,0},{2,3},{3,2},{4,5},{5,4},{6,7},{7,6},{8,9},{9,8},{10,11... | collective-permute-start | bytes 2359304 | tf_op jit(solution)/shard_map/ppermute | solution.py:554
  142.1 25.8 %all-to-all-start.5 = ((bf16[16,148,256]{2,1,0:T(8,128)(2,1)}), bf16[16,148,256]{2,1,0:T(8,128)(2,1)S(1)}, u32[]{:S(2)}, u32[]{:S(2)}) async-start(bf16[16,148,256]{2,1,0:T(8,128)(2,1)} %get-tuple-element.80), calls=%async_computation.5 | async-start | bytes 2490368 | tf_op jit(solution)/shard_map/all_to_all | solution.py:546
  146.1 17.8 %collective-permute-start.8 = (bf16[16,5376]{1,0:T(8,128)(2,1)S(1)}, bf16[16,5376]{1,0:T(8,128)(2,1)S(1)}, u32[]{:S(2)}, u32[]{:S(2)}) collective-permute-start(bf16[16,5376]{1,0:T(8,128)(2,1)S(1)} %reduce_sum.30), channel_id=1, source_target_pairs={{0,16},{1,17},{2,18},{3,19},{4,20},{5,21},{6,22},{7,23},{8,24},{9,... | collective-permute-start | bytes 516104 | tf_op jit(solution)/shard_map/ppermute | solution.py:725
  168.9 16.5 %all-to-all-start.7 = ((bf16[4,16,5376]{2,1,0:T(8,128)(2,1)}), bf16[4,16,5376]{2,1,0:T(8,128)(2,1)}, u32[]{:S(2)}, u32[]{:S(2)}) async-start(bf16[4,16,5376]{2,1,0:T(8,128)(2,1)} %broadcast_in_dim.17), calls=%async_computation.7 | async-start | bytes 1376256 | tf_op jit(solution)/shard_map/all_to_all | solution.py:546
  179.0 18.2 %copy-start.12 = (f32[3,3,256,64]{2,3,1,0:T(8,128)S(1)}, f32[3,3,256,64]{2,3,1,0:T(8,128)}, u32[]{:S(2)}) copy-start(f32[3,3,256,64]{2,3,1,0:T(8,128)} %param.27) | copy-start | bytes 1769476
  185.3 11.9 %copy-start.2 = (f32[3,3,256,64]{2,3,1,0:T(8,128)S(1)}, f32[3,3,256,64]{2,3,1,0:T(8,128)}, u32[]{:S(2)}) copy-start(f32[3,3,256,64]{2,3,1,0:T(8,128)} %param.20) | copy-start | bytes 1769476
  185.3 11.9 %copy-start.4 = (f32[3,3,64,256]{3,2,1,0:T(8,128)S(1)}, f32[3,3,64,256]{3,2,1,0:T(8,128)}, u32[]{:S(2)}) copy-start(f32[3,3,64,256]{3,2,1,0:T(8,128)} %refs_6_.1) | copy-start | bytes 1769476
  185.3 12.0 %copy-start.9 = (f32[3,3,80,64]{2,3,1,0:T(8,128)S(1)}, f32[3,3,80,64]{2,3,1,0:T(8,128)}, u32[]{:S(2)}) copy-start(f32[3,3,80,64]{2,3,1,0:T(8,128)} %param.19) | copy-start | bytes 552964
  185.3 12.0 %copy-start.11 = (f32[3,3,256,64]{2,3,1,0:T(8,128)S(1)}, f32[3,3,256,64]{2,3,1,0:T(8,128)}, u32[]{:S(2)}) copy-start(f32[3,3,256,64]{2,3,1,0:T(8,128)} %param.26) | copy-start | bytes 1769476
  185.3 12.0 %copy-start.18 = (f32[4,64]{1,0:T(4,128)S(1)}, f32[4,64]{1,0:T(4,128)}, u32[]{:S(2)}) copy-start(f32[4,64]{1,0:T(4,128)} %refs_9_.1) | copy-start | bytes 3076
  185.3 12.0 %copy-start.19 = (f32[4,64]{1,0:T(4,128)S(1)}, f32[4,64]{1,0:T(4,128)}, u32[]{:S(2)}) copy-start(f32[4,64]{1,0:T(4,128)} %refs_10_.1) | copy-start | bytes 3076
  185.3 12.0 %copy-start.20 = (f32[4,64]{1,0:T(4,128)S(1)}, f32[4,64]{1,0:T(4,128)}, u32[]{:S(2)}) copy-start(f32[4,64]{1,0:T(4,128)} %refs_11_.1) | copy-start | bytes 3076
  190.9 1.3 collective-permute-start.9
  192.8 3.7 %collective-permute-start.10 = (f32[]{:T(128)}, f32[]{:T(128)}, u32[]{:S(2)}, u32[]{:S(2)}) collective-permute-start(f32[]{:T(128)} %add.30), channel_id=1, source_target_pairs={{0,2},{1,3},{2,0},{3,1},{4,6},{5,7},{6,4},{7,5},{8,10},{9,11},{10,... | collective-permute-start | bytes 20 | tf_op jit(solution)/shard_map/ppermute | solution.py:554
  197.3 1.1 copy-start.13
  198.4 1.1 copy-start.14
  199.4 1.0 copy-start.15
  200.4 1.0 copy-start.16

commit v2 on v1

v2 whole, which is shorter than its diff:
```python
import functools
import math

import jax
import jax.numpy as jnp
from jax import lax
from jax.experimental import pallas as pl
from jax.experimental.pallas import tpu as pltpu
from jax.sharding import PartitionSpec as P

STEP = 10


beta_one = 0.9
beta_two = 0.999
adam_eps = 1e-08
learn_rate = 0.02
norm_rate = 1.5
weight_decay = 0.01
norm_eps = 1e-05
clip_norm = 1.0

AXES = ("strip", "chan")
LANES = 128
VMEM_BYTES = 24 * 1024 * 1024
VMEM_MOST = 60 * 1024 * 1024

f32 = jnp.float32
bf16 = jnp.bfloat16


def round_up(value, step):
    return (value + step - 1) // step * step


def call(body, out_shape, scratch=(), smem=0, after=(), **options):
    waits = len(after)

    def run(*operands):
        specs = [pl.BlockSpec(memory_space=pltpu.SMEM)] * smem
        specs += [pl.BlockSpec(memory_space=pltpu.VMEM)] * (len(operands) - smem)
        specs = [pl.BlockSpec(memory_space=pl.ANY)] * waits + specs
        return pl.pallas_call(
            lambda *refs: body(*refs[waits:]),
            out_shape=out_shape,
            in_specs=specs,
            out_specs=jax.tree.map(lambda _: pl.BlockSpec(memory_space=pltpu.VMEM), out_shape),
            scratch_shapes=list(scratch),
            compiler_params=pltpu.CompilerParams(vmem_limit_bytes=VMEM_BYTES),
            **options,
        )(*after, *operands)

    return run


def struct(shape, dtype):
    return jax.ShapeDtypeStruct(shape, dtype)


def cut(position):
    return slice(position * LANES, (position + 1) * LANES)


def sides(row):
    lane = lax.broadcasted_iota(jnp.int32, row.shape, 1)
    before = jnp.where(lane == 0, 0.0, pltpu.roll(row, 1, axis=1))
    after = jnp.where(lane == LANES - 1, 0.0, pltpu.roll(row, LANES - 1, axis=1))
    return before, after


def column_sums(parts):
    return jnp.concatenate([jnp.sum(part.T, axis=0, keepdims=True) for part in parts], axis=0)


def for_all(ref, values):
    ref[...] = jnp.broadcast_to(values[None], ref.shape)


def to_columns(rows):
    channels = rows[0].shape[1]
    rest = jnp.zeros((LANES - len(rows), channels), f32)
    return jnp.concatenate(list(rows) + [rest], axis=0).T


def matmul(left, right):
    return lax.dot_general(left, right, (((1,), (0,)), ((), ())), preferred_element_type=f32)


def matmul_nt(left, right):
    return lax.dot_general(left, right, (((1,), (1,)), ((), ())), preferred_element_type=f32)


def sigmoid(values):
    return 1.0 / (1.0 + jnp.exp(-values))


def moments(received, pixel_count):
    total = jnp.sum(received, axis=0)
    mean = total[0:1] / pixel_count
    variance = total[1:2] / pixel_count - mean * mean
    return mean, lax.rsqrt(variance + norm_eps)


def pool_body(grids, cells, chans, index_ref, feat_ref, out_ref, acc_ref):
    step = pl.program_id(0)
    rows = round_up(chans, 8)
    index = index_ref[...]
    high, low = index // cells, index % cells
    count = index.shape[1]
    feat = feat_ref[...].astype(f32)
    feat = jnp.concatenate([feat, jnp.zeros((rows - chans, count), f32)], axis=0)
    spread = jnp.concatenate(
        [jnp.where(high == grid, feat, 0.0) for grid in range(grids)], axis=0
    ).astype(bf16)
    table = (lax.broadcasted_iota(jnp.int32, (cells, count), 0) == low).astype(f32).astype(bf16)
    added = matmul_nt(spread, table)

    @pl.when(step == 0)
    def _():
        acc_ref[...] = added

    @pl.when(step > 0)
    def _():
        acc_ref[...] += added

    @pl.when(step == pl.num_programs(0) - 1)
    def _():
        out_ref[...] = acc_ref[...].reshape(grids, rows, cells)[:, :chans].astype(bf16)


def spread_body(grids, cells, chans, first, index_ref, grad_ref, out_ref):
    rows = round_up(chans, 8)
    index = index_ref[...]
    high, low = index // cells, index % cells
    count = index.shape[1]
    table = (lax.broadcasted_iota(jnp.int32, (cells, count), 0) == low).astype(f32).astype(bf16)
    grad = grad_ref[:, first : first + chans, :].astype(f32)
    grad = jnp.concatenate([grad, jnp.zeros((grids, rows - chans, cells), f32)], axis=1)
    picked = matmul(grad.reshape(grids * rows, cells).astype(bf16), table)
    total = jnp.zeros((rows, count), f32)
    for grid in range(grids):
        total = jnp.where(high == grid, picked[grid * rows : (grid + 1) * rows], total)
    out_ref[...] = total[:chans]


def pack_body(
    lid, cam, mid, one_width, norm_ref, lidar_far, cam_far, mid_far, out_ref,
    lidar_ref, cam_ref, mid_ref, sems,
):
    rows = lidar_ref.shape[2]
    pairs = ((lidar_far, lidar_ref), (cam_far, cam_ref), (mid_far, mid_ref))
    copies = [
        [pltpu.make_async_copy(far.at[a], near.at[a], sems.at[i, a]) for i, (far, near) in enumerate(pairs)]
        for a in range(3)
    ]
    for group in copies:
        for copy in group:
            copy.start()
    for a in range(3):
        for copy in copies[a]:
            copy.wait()
        base = a * one_width
        for b in range(3):
            out_ref[:, base + b * lid : base + (b + 1) * lid] = lidar_ref[a, b].astype(bf16)
        used = 3 * lid + 3 * cam
        rest = [cam_ref[a, b] for b in range(3)]
        if one_width > used:
            rest.append(jnp.zeros((rows, one_width - used), f32))
        out_ref[:, base + 3 * lid : base + one_width] = jnp.concatenate(rest, axis=1).astype(bf16)
        for b in range(3):
            start = 3 * one_width + (3 * a + b) * mid
            out_ref[:, start : start + mid] = mid_ref[a, b].astype(bf16)
    norm = norm_ref[...]
    norm = jnp.concatenate([norm, jnp.zeros((LANES - norm.shape[0], rows), f32)], axis=0)
    norm = jnp.concatenate([norm, jnp.zeros((LANES, LANES - rows), f32)], axis=1).T[:rows, :4]
    high = norm.astype(bf16)
    left = norm - high.astype(f32)
    middle = left.astype(bf16)
    low = (left - middle.astype(f32)).astype(bf16)
    tail = jnp.concatenate(
        [high.astype(f32), middle.astype(f32), low.astype(f32), jnp.zeros((rows, LANES - 12), f32)],
        axis=1,
    )
    out_ref[:, 3 * one_width + 9 * mid :] = tail.astype(bf16)


def place_rows(own, masks, chan, parts, all_ref):
    place = 0
    for part in parts:
        for j in range(part.shape[0]):
            row = pl.multiple_of((chan ^ masks[place]) * own, own)
            all_ref[pl.ds(row, own), :] = part[j]
            place += 1


def unpack_body(own, one_width, two_width, masks, place_ref, *refs):
    parts, (one_ref, two_ref, norm_ref, all_ref) = refs[:-4], refs[-4:]
    place_rows(own, masks, place_ref[0], parts, all_ref)
    one_ref[...] = all_ref[:, : 3 * one_width]
    two_ref[...] = all_ref[:, 3 * one_width : 3 * (one_width + two_width)]
    tail = all_ref[:, 3 * (one_width + two_width) :].astype(f32)
    norm = tail[:, 0:4] + tail[:, 4:8] + tail[:, 8:12]
    norm_ref[...] = jnp.concatenate([norm, jnp.zeros((norm.shape[0], LANES - 4), f32)], axis=1)


def turn_body(lid, cam, one_width, outs, one_ref, two_t_ref, one_t_ref, two_ref):
    for t in range(9):
        at = slice(t * outs, (t + 1) * outs)
        two_ref[:, at] = two_t_ref[:, at].T
    for a in range(3):
        for b in range(3):
            to = slice((3 * a + b) * outs, (3 * a + b + 1) * outs)
            start = a * one_width + b * lid
            one_t_ref[0:lid, to] = one_ref[:, start : start + lid].T
        start = a * one_width + 3 * lid
        turned = one_ref[:, start : start + one_width - 3 * lid].T
        for b in range(3):
            to = slice((3 * a + b) * outs, (3 * a + b + 1) * outs)
            one_t_ref[lid : lid + cam, to] = turned[b * cam : (b + 1) * cam]


def edge_rows(edge_ref, place_ref, groups, first, last):
    if groups == 2:
        edge_ref[0] = jnp.where(place_ref[1] == 0, last, first)
    else:
        edge_ref[0] = last
        edge_ref[1] = first


def fill_stack(stack_ref, base, order, p, row):
    count = row.shape[0]
    for b, shifted in zip(order, (*sides(row), row), strict=True):
        start = base + b * count
        stack_ref[start : start + count, cut(p)] = shifted.astype(bf16)


FORWARD = (0, 2, 1)
BACKWARD = (2, 0, 1)


def first_body(cfg, got_ref, kernel_ref, stack_ref, cot_ref, part_ref):
    nc, spg, rows, lid, cam, lid_own, cam_own, one_width = cfg
    per_strip = rows // spg

    def take(q, first, count):
        s, r = q // per_strip, q % per_strip
        pieces = [got_ref[s * nc + c, first : first + count, cut(r)] for c in range(nc)]
        return jnp.concatenate([piece.astype(f32) for piece in pieces], axis=0)

    used = 3 * (lid + cam)
    stack_ref[:, cut(0)] = jnp.zeros((one_width, LANES), bf16)
    stack_ref[:, cut(rows + 1)] = jnp.zeros((one_width, LANES), bf16)
    if one_width > used:
        stack_ref[used:, :] = jnp.zeros((one_width - used, (rows + 2) * LANES), bf16)
    for q in range(rows):
        fill_stack(stack_ref, 0, FORWARD, q + 1, take(q, 0, lid_own))
        fill_stack(stack_ref, 3 * lid, FORWARD, q + 1, take(q, 2 * lid_own, cam_own))
        cot_ref[:, cut(q)] = take(q, lid_own, lid_own).astype(bf16)
    total = None
    for a in range(3):
        term = matmul(
            kernel_ref[:, a * one_width : (a + 1) * one_width],
            stack_ref[:, a * LANES : (a + rows) * LANES],
        )
        total = term if total is None else total + term
    part_ref[...] = total


def first_halo_body(
    cfg, place_ref, part_ref, above_ref, below_ref, kernel_ref,
    halo_ref, cot_ref, out_ref, sums_ref, edge_ref,
):
    nc, rows, lid, cam, lid_own, cam_own, one_width, groups = cfg
    has_above = place_ref[1] > 0
    has_below = place_ref[1] < groups - 1
    used = 3 * (lid + cam)
    if one_width > used:
        halo_ref[used:, :] = jnp.zeros((one_width - used, 2 * LANES), bf16)
    for side, (ref, given) in enumerate(((above_ref, has_above), (below_ref, has_below))):
        row = jnp.concatenate([ref[c, :lid_own].astype(f32) for c in range(nc)], axis=0)
        fill_stack(halo_ref, 0, FORWARD, side, jnp.where(given, row, 0.0))
        row = jnp.concatenate([ref[c, 2 * lid_own :].astype(f32) for c in range(nc)], axis=0)
        fill_stack(halo_ref, 3 * lid, FORWARD, side, jnp.where(given, row, 0.0))
        cot_ref[:, cut(side)] = jnp.concatenate([ref[c, lid_own : 2 * lid_own] for c in range(nc)], axis=0)
    lines = [part_ref[:, cut(q)] for q in range(rows)]
    lines[0] = lines[0] + matmul(kernel_ref[:, :one_width], halo_ref[:, cut(0)])
    lines[-1] = lines[-1] + matmul(kernel_ref[:, 2 * one_width :], halo_ref[:, cut(1)])
    finish_sums(lines, out_ref, sums_ref, edge_ref, place_ref, groups)


def finish_sums(lines, out_ref, sums_ref, edge_ref, place_ref, groups):
    sums = squares = None
    for q, row in enumerate(lines):
        out_ref[:, cut(q)] = row
        sums = row if sums is None else sums + row
        squares = row * row if squares is None else squares + row * row
    for_all(sums_ref, column_sums([sums, squares]))
    edge_rows(edge_ref, place_ref, groups, lines[0], lines[-1])


def second_body(
    cfg, place_ref, raw_ref, above_ref, below_ref, stats_ref, norm_ref, kernel_ref,
    out_ref, sums_ref, edge_ref, hidden_ref, means_ref, stack_ref,
):
    rows, chans, groups, pixel_count = cfg
    mean, inv = moments(stats_ref[...], pixel_count)
    columns = to_columns([mean, inv])
    means_ref[...] = columns
    mean, inv = columns[:, 0:1], columns[:, 1:2]
    gain, shift = norm_ref[:, 0:1], norm_ref[:, 1:2]
    for p in range(rows + 2):
        if p == 0:
            raw = above_ref[...]
        elif p == rows + 1:
            raw = below_ref[...]
        else:
            raw = raw_ref[:, cut(p - 1)]
        act = gain * ((raw - mean) * inv) + shift
        hidden = act * sigmoid(act)
        if p == 0:
            hidden = jnp.where(place_ref[1] > 0, hidden, 0.0)
        elif p == rows + 1:
            hidden = jnp.where(place_ref[1] < groups - 1, hidden, 0.0)
        else:
            hidden_ref[:, cut(p - 1)] = hidden
        fill_stack(stack_ref, 0, FORWARD, p, hidden)
    total = None
    for a in range(3):
        term = matmul(
            kernel_ref[:, a * 3 * chans : (a + 1) * 3 * chans],
            stack_ref[:, a * LANES : (a + rows) * LANES],
        )
        total = term if total is None else total + term
    lines = [total[:, cut(q)] for q in range(rows)]
    finish_sums(lines, out_ref, sums_ref, edge_ref, place_ref, groups)


def slope_body(
    cfg, place_ref, raw_ref, above_ref, below_ref, stats_ref, norm_ref, cot_ref, cot_halo_ref, hidden_ref,
    slope_ref, sums_ref, means_ref, mixed_ref,
):
    rows, own, spg, nc, pixel_count = cfg
    per_strip = rows // spg
    mean, inv = moments(stats_ref[...], pixel_count)
    columns = to_columns([mean, inv])
    means_ref[...] = columns
    mean, inv = columns[:, 0:1], columns[:, 1:2]
    gain, shift = norm_ref[:, 2:3], norm_ref[:, 3:4]
    shift_sum = gain_sum = None
    for p in range(rows + 2):
        if p == 0:
            raw, cot = above_ref[...], cot_halo_ref[:, cut(0)]
        elif p == rows + 1:
            raw, cot = below_ref[...], cot_halo_ref[:, cut(1)]
        else:
            raw, cot = raw_ref[:, cut(p - 1)], cot_ref[:, cut(p - 1)]
        centred = (raw - mean) * inv
        act = gain * centred + shift
        gate = sigmoid(act)
        slope = cot.astype(f32) * (gate * (1.0 + act * (1.0 - gate)))
        slope_ref[:, cut(p)] = slope
        if 0 < p <= rows:
            shift_sum = slope if shift_sum is None else shift_sum + slope
            term = slope * centred
            gain_sum = term if gain_sum is None else gain_sum + term
            mixed = (hidden_ref[:, cut(p - 1)] + act * gate).astype(bf16)
            s, r = (p - 1) // per_strip, (p - 1) % per_strip
            for c in range(nc):
                mixed_ref[s * nc + c, :, cut(r)] = mixed[c * own : (c + 1) * own]
    for_all(sums_ref, column_sums([shift_sum, gain_sum]))


def mid_back_body(
    cfg, place_ref, slope_ref, raw_ref, above_ref, below_ref, means_two_ref, stats_ref, norm_ref,
    kernel_ref, raw_one_ref, means_one_ref, cot_ref,
    out_ref, sums_ref, edge_ref, stack_ref, grads_ref,
):
    rows, chans, groups, pixel_count = cfg
    total = jnp.sum(stats_ref[...], axis=0)
    grads_ref[...] = total
    columns = to_columns([total[0:1] / pixel_count, total[1:2] / pixel_count])
    shift_mean, gain_mean = columns[:, 0:1], columns[:, 1:2]
    mean, inv = means_two_ref[:, 0:1], means_two_ref[:, 1:2]
    scale = norm_ref[:, 2:3] * inv
    for p in range(rows + 2):
        if p == 0:
            raw = above_ref[...]
        elif p == rows + 1:
            raw = below_ref[...]
        else:
            raw = raw_ref[:, cut(p - 1)]
        centred = (raw - mean) * inv
        grad = scale * (slope_ref[:, cut(p)] - shift_mean - centred * gain_mean)
        if p == 0:
            grad = jnp.where(place_ref[1] > 0, grad, 0.0)
        elif p == rows + 1:
            grad = jnp.where(place_ref[1] < groups - 1, grad, 0.0)
        fill_stack(stack_ref, 0, BACKWARD, p, grad)
    back = None
    for a in range(3):
        term = matmul(
            kernel_ref[:, a * 3 * chans : (a + 1) * 3 * chans],
            stack_ref[:, (2 - a) * LANES : (2 - a + rows) * LANES],
        )
        back = term if back is None else back + term
    mean, inv = means_one_ref[:, 0:1], means_one_ref[:, 1:2]
    gain, shift = norm_ref[:, 0:1], norm_ref[:, 1:2]
    shift_sum = gain_sum = None
    slopes = []
    for q in range(rows):
        centred = (raw_one_ref[:, cut(q)] - mean) * inv
        act = gain * centred + shift
        gate = sigmoid(act)
        grad = back[:, cut(q)] + cot_ref[:, cut(q)].astype(f32)
        slope = grad * (gate * (1.0 + act * (1.0 - gate)))
        out_ref[:, cut(q)] = slope
        if q in (0, rows - 1):
            slopes.append(slope)
        shift_sum = slope if shift_sum is None else shift_sum + slope
        term = slope * centred
        gain_sum = term if gain_sum is None else gain_sum + term
    for_all(sums_ref, column_sums([shift_sum, gain_sum]))
    edge_rows(edge_ref, place_ref, groups, slopes[0], slopes[-1])


def halves(place_ref, own, nc, rows_at):
    low = place_ref[0] & 1
    found = []
    for side in (low, 1 - low):
        for pair in range(nc // 2):
            found.append(rows_at(pl.multiple_of((2 * pair + side) * own, own)))
    return jnp.concatenate(found, axis=0)


def first_back_body(
    cfg, place_ref, slope_ref, slope_above_ref, slope_below_ref, raw_ref, above_ref, below_ref,
    means_ref, stats_ref, norm_ref, grads_two_ref, own_ref, halo_ref, hidden_ref, stack_two_ref,
    keep_ref, send_ref, stack_ref, grads_ref, squares_ref, cells_ref,
):
    rows, chans, own, nc, one_width, groups, pixel_count = cfg
    wide = (rows + 2) * LANES
    total = jnp.sum(stats_ref[...], axis=0)
    grads = jnp.concatenate(
        [total[1:2], total[0:1], grads_two_ref[1:2], grads_two_ref[0:1]], axis=0
    )
    grads_ref[...] = grads
    squares_ref[...] = jnp.sum(grads * grads).reshape(1, 1)
    columns = to_columns([total[0:1] / pixel_count, total[1:2] / pixel_count])
    shift_mean, gain_mean = columns[:, 0:1], columns[:, 1:2]
    mean, inv = means_ref[:, 0:1], means_ref[:, 1:2]
    scale = norm_ref[:, 0:1] * inv
    for p in range(rows + 2):
        if p == 0:
            raw, slope = above_ref[...], slope_above_ref[...]
        elif p == rows + 1:
            raw, slope = below_ref[...], slope_below_ref[...]
        else:
            raw, slope = raw_ref[:, cut(p - 1)], slope_ref[:, cut(p - 1)]
        grad = scale * (slope - shift_mean - (raw - mean) * inv * gain_mean)
        if p == 0:
            grad = jnp.where(place_ref[1] > 0, grad, 0.0)
        elif p == rows + 1:
            grad = jnp.where(place_ref[1] < groups - 1, grad, 0.0)
        fill_stack(stack_ref, 0, BACKWARD, p, grad)
    cells_ref[:, :LANES] = halo_ref[:, :LANES]
    cells_ref[:, LANES : wide - LANES] = own_ref[:, LANES : wide - LANES]
    cells_ref[:, wide - LANES :] = halo_ref[:, LANES:]
    half = chans // 2
    ordered = halves(
        place_ref, own, nc,
        lambda start: stack_ref[pl.ds(chans + start, own), LANES : (rows + 1) * LANES],
    )
    hidden = halves(place_ref, own, nc, lambda start: hidden_ref[pl.ds(start, own), :]).astype(bf16)
    for a in range(3):
        grad = matmul_nt(ordered, cells_ref[:, a * LANES : (a + rows) * LANES]).astype(bf16)
        to = slice(a * one_width, (a + 1) * one_width)
        keep_ref[:, to] = grad[:half]
        send_ref[:, to] = grad[half:]
        grad = matmul_nt(hidden, stack_two_ref[:, (2 - a) * LANES : (2 - a + rows) * LANES]).astype(bf16)
        start = 3 * one_width + a * 3 * chans
        keep_ref[:, start : start + 3 * chans] = grad[:half]
        send_ref[:, start : start + 3 * chans] = grad[half:]


def inputs_back_body(cfg, stack_ref, kernel_ref, mixed_ref, back_ref):
    rows, chans, lid, lid_own, cam_own, spg, nc = cfg
    per_strip = rows // spg
    back = None
    for a in range(3):
        term = matmul(
            kernel_ref[:, a * 3 * chans : (a + 1) * 3 * chans],
            stack_ref[:, (2 - a) * LANES : (2 - a + rows) * LANES],
        )
        back = term if back is None else back + term
    for s in range(spg):
        cells = slice(s * per_strip * LANES, (s + 1) * per_strip * LANES)
        for c in range(nc):
            block = s * nc + c
            back_ref[block, 0:lid_own, :] = back[c * lid_own : (c + 1) * lid_own, cells].astype(bf16)
            back_ref[block, lid_own : 2 * lid_own, :] = mixed_ref[block]
            start = lid + c * cam_own
            back_ref[block, 2 * lid_own : 2 * lid_own + cam_own, :] = back[
                start : start + cam_own, cells
            ].astype(bf16)


def adam(weight, gradient, first, second, rate):
    first = beta_one * first + (1.0 - beta_one) * gradient
    second = beta_two * second + (1.0 - beta_two) * gradient * gradient
    fix_one = 1.0 - beta_one**STEP
    fix_two = 1.0 - beta_two**STEP
    stepped = first / fix_one / (jnp.sqrt(second / fix_two) + adam_eps)
    return weight - rate * (stepped + weight_decay * weight), first, second


def add_body(mine_ref, other_ref, out_ref):
    out_ref[...] = (mine_ref[...].astype(f32) + other_ref[...].astype(f32)).astype(bf16)


def sum_body(pieces_ref, out_ref):
    out_ref[...] = jnp.sum(pieces_ref[...].astype(f32), axis=0).astype(bf16)


def merge_body(copies, mine_ref, other_ref, out_ref):
    width = mine_ref.shape[1]
    piece = (mine_ref[...].astype(f32) + other_ref[...].astype(f32)).astype(bf16)
    values = piece.astype(f32)
    squares = jnp.sum(values * values).reshape(1, 1)
    high = squares.astype(bf16).astype(f32)
    middle = (squares - high).astype(bf16).astype(f32)
    low = squares - high - middle
    shape = (piece.shape[0], LANES)
    row = lax.broadcasted_iota(jnp.int32, shape, 0)
    lane = lax.broadcasted_iota(jnp.int32, shape, 1)
    terms = jnp.where(lane == 0, high, jnp.where(lane == 1, middle, jnp.where(lane == 2, low, 0.0)))
    terms = jnp.where(row == 0, terms, 0.0).astype(bf16)
    for copy in range(copies):
        out_ref[copy, :, :width] = piece
        out_ref[copy, :, width:] = terms


def adam_body(lid, cam, mid, squares_ref, norm_squares_ref, grads_ref, norm_grad_ref, *refs):
    norm_ins, fars, refs = refs[:3], refs[3:12], refs[12:]
    norm_outs, far_outs, norm_ref, refs = refs[:3], refs[3:12], refs[12], refs[13:]
    nears, ins, outs = refs[:9], refs[9], refs[10]
    one_width = round_up(3 * lid + 3 * cam, 256)
    reads = [
        [pltpu.make_async_copy(fars[i].at[a], nears[i].at[a], ins.at[i, a]) for i in range(9)]
        for a in range(3)
    ]
    writes = [
        [pltpu.make_async_copy(nears[i].at[a], far_outs[i].at[a], outs.at[i, a]) for i in range(9)]
        for a in range(3)
    ]
    for group in reads:
        for copy in group:
            copy.start()
    norm = jnp.sqrt(squares_ref[...] + norm_squares_ref[...])
    norm_ref[...] = norm
    factor = jnp.minimum(1.0, clip_norm / (norm + 1e-06))

    def step(refs, results, at, gradient, rate):
        weight, first, second = (ref[at] for ref in refs)
        for ref, value in zip(results, adam(weight, factor * gradient, first, second, rate), strict=True):
            ref[at] = value

    step(norm_ins, norm_outs, ..., norm_grad_ref[...], norm_rate)
    for a in range(3):
        for copy in reads[a]:
            copy.wait()
        base = a * one_width
        tail = grads_ref[:, base + 3 * lid : base + one_width].astype(f32)
        for b in range(3):
            given = (
                tail[:, b * cam : (b + 1) * cam],
                grads_ref[:, base + b * lid : base + (b + 1) * lid].astype(f32),
                grads_ref[
                    :, 3 * one_width + (3 * a + b) * mid : 3 * one_width + (3 * a + b + 1) * mid
                ].astype(f32),
            )
            for i, gradient in enumerate(given):
                state = nears[3 * i : 3 * i + 3]
                step(state, state, (a, b), gradient, learn_rate)
        for copy in writes[a]:
            copy.start()
    for group in writes:
        for copy in group:
            copy.wait()


def shards(
    cam_feats,
    cell_index,
    lidar_bev,
    w_cam,
    w_lidar,
    w_mid,
    bn_params,
    cotangent,
    m_cam,
    v_cam,
    m_lidar,
    v_lidar,
    m_mid,
    v_mid,
    m_bn,
    v_bn,
):
    grids, lid_own, strip_rows, width = lidar_bev.shape
    cam_own, points = cam_feats.shape
    own = bn_params.shape[1]
    nc = lax.axis_size("chan")
    ns = lax.axis_size("strip")
    lid, cam, chans = nc * lid_own, nc * cam_own, nc * own
    spg = grids // nc
    groups = ns // spg
    members = spg * nc
    rows = spg * strip_rows
    cells = strip_rows * width
    pixel_count = float(grids * cells * ns)
    devices = ns * nc
    one_width = round_up(3 * lid + 3 * cam, 256)
    two_width = 3 * chans
    total_width = 3 * one_width + 3 * two_width
    chan = lax.axis_index("chan")
    group = lax.axis_index("strip") // spg
    place = jnp.stack([chan, group]).astype(jnp.int32)

    tile_groups = [[g * members + r for r in range(members)] for g in range(groups)]
    half_groups = [
        [(g * spg + s) * nc + 2 * pair + low for pair in range(nc // 2) for s in range(spg)]
        for g in range(groups)
        for low in range(2)
    ]
    strip_groups = [
        [(g * spg + s) * nc + c for s in range(spg)] for g in range(groups) for c in range(nc)
    ]

    def exchange(blocks, parts):
        return lax.all_to_all(blocks, AXES, 0, 0, axis_index_groups=parts, tiled=True)

    def everywhere(copies):
        return lax.all_to_all(copies, AXES, 0, 0, tiled=True)

    def chan_swap(values, bit):
        return lax.ppermute(values, "chan", [(c, c ^ bit) for c in range(nc)])

    def neighbours(edges):
        if groups == 1:
            return edges[0], edges[0]
        if groups == 2:
            pairs = [(i, (i + members) % devices) for i in range(devices)]
            other = lax.ppermute(edges[0], AXES, pairs)
            return other, other
        down = [(i, i + members) for i in range(devices - members)]
        up = [(i + members, i) for i in range(devices - members)]
        return lax.ppermute(edges[0], AXES, down), lax.ppermute(edges[1], AXES, up)

    edge_count = 2 if groups > 2 else 1

    area = rows * LANES
    wide = (rows + 2) * LANES
    def from_all_channels(packed):
        parts, masks = [packed[None]], [0]
        bit = nc // 2
        while bit:
            stacked = parts[0] if len(parts) == 1 else jnp.concatenate(parts, axis=0)
            parts.append(chan_swap(stacked, bit))
            masks += [mask ^ bit for mask in masks]
            bit //= 2
        return parts, masks

    def edge_cells(got):
        last = got[members - nc :, :, cells - width :]
        first = got[:nc, :, :width]
        if groups == 2:
            return jnp.where(group == 0, last, first)[None]
        return jnp.stack([last, first])

    sums_struct = struct((devices, 2, chans), f32)
    packed_width = total_width + LANES

    index_row = cell_index.reshape(1, points)
    block = math.gcd(points, 2048)
    pooled = pl.pallas_call(
        functools.partial(pool_body, grids, cells, cam_own),
        grid=(points // block,),
        in_specs=[
            pl.BlockSpec((1, block), lambda i: (0, i)),
            pl.BlockSpec((cam_own, block), lambda i: (0, i)),
        ],
        out_specs=pl.BlockSpec((grids, cam_own, cells), lambda i: (0, 0, 0)),
        out_shape=struct((grids, cam_own, cells), bf16),
        scratch_shapes=[pltpu.VMEM((grids * round_up(cam_own, 8), cells), f32)],
        compiler_params=pltpu.CompilerParams(vmem_limit_bytes=VMEM_BYTES),
    )(index_row, cam_feats)
    joined = jnp.concatenate(
        [
            lidar_bev.reshape(grids, lid_own, cells),
            cotangent.reshape(grids, own, cells),
            pooled,
        ],
        axis=1,
    )
    got = exchange(joined, tile_groups)
    above, below = neighbours(edge_cells(got))

    turn = (0, 1, 3, 2)
    far = pl.BlockSpec(memory_space=pltpu.HBM)
    near = pl.BlockSpec(memory_space=pltpu.VMEM)
    weights = [w_lidar.transpose(turn), w_cam.transpose(turn), w_mid]
    packed = pl.pallas_call(
        functools.partial(pack_body, lid, cam, chans, one_width),
        in_specs=[near, far, far, far],
        out_specs=near,
        out_shape=struct((own, packed_width), bf16),
        scratch_shapes=[
            *(pltpu.VMEM(weight.shape, f32) for weight in weights),
            pltpu.SemaphoreType.DMA((3, 3)),
        ],
        compiler_params=pltpu.CompilerParams(vmem_limit_bytes=VMEM_MOST),
    )(bn_params, *weights)
    parts, masks = from_all_channels(packed)
    kernel_one, kernel_two_t, norm = call(
        functools.partial(unpack_body, own, one_width, two_width, masks),
        [
            struct((chans, 3 * one_width), bf16),
            struct((chans, 3 * two_width), bf16),
            struct((chans, LANES), f32),
        ],
        scratch=[pltpu.VMEM((chans, packed_width), bf16)],
        smem=1,
    )(place, *parts)

    kernel_one_t, kernel_two = call(
        functools.partial(turn_body, lid, cam, one_width, chans),
        [struct((lid + cam, 3 * two_width), bf16), struct((chans, 3 * two_width), bf16)],
    )(kernel_one, kernel_two_t)
    own_stack, cot, part_one = call(
        functools.partial(first_body, (nc, spg, rows, lid, cam, lid_own, cam_own, one_width)),
        [
            struct((one_width, wide), bf16),
            struct((chans, area), bf16),
            struct((chans, area), f32),
        ],
    )(got, kernel_one)
    halo_stack, cot_halo, raw_one, sums_one, edges_one = call(
        functools.partial(
            first_halo_body, (nc, rows, lid, cam, lid_own, cam_own, one_width, groups)
        ),
        [
            struct((one_width, 2 * LANES), bf16),
            struct((chans, 2 * LANES), bf16),
            struct((chans, area), f32),
            sums_struct,
            struct((edge_count, chans, LANES), f32),
        ],
        smem=1,
        after=(kernel_one_t, kernel_two),
    )(place, part_one, above, below, kernel_one)

    above_one, below_one = neighbours(edges_one)
    stats_one = everywhere(sums_one)
    raw_two, sums_two, edges_two, hidden, means_one = call(
        functools.partial(second_body, (rows, chans, groups, pixel_count)),
        [
            struct((chans, area), f32),
            sums_struct,
            struct((edge_count, chans, LANES), f32),
            struct((chans, area), f32),
            struct((chans, LANES), f32),
        ],
        scratch=[pltpu.VMEM((two_width, wide), bf16)],
        smem=1,
    )(place, raw_one, above_one, below_one, stats_one, norm, kernel_two)

    above_two, below_two = neighbours(edges_two)
    stats_two = everywhere(sums_two)
    slope_two, sums_three, means_two, mixed_blocks = call(
        functools.partial(slope_body, (rows, own, spg, nc, pixel_count)),
        [
            struct((chans, wide), f32),
            sums_struct,
            struct((chans, LANES), f32),
            struct((members, own, cells), bf16),
        ],
        smem=1,
    )(place, raw_two, above_two, below_two, stats_two, norm, cot, cot_halo, hidden)

    stats_three = everywhere(sums_three)
    slope_one, sums_four, edges_four, grad_stack, grads_two = call(
        functools.partial(mid_back_body, (rows, chans, groups, pixel_count)),
        [
            struct((chans, area), f32),
            sums_struct,
            struct((edge_count, chans, LANES), f32),
            struct((two_width, wide), bf16),
            struct((2, chans), f32),
        ],
        smem=1,
    )(
        place, slope_two, raw_two, above_two, below_two, means_two, stats_three, norm,
        kernel_two_t, raw_one, means_one, cot,
    )

    above_four, below_four = neighbours(edges_four)
    stats_four = everywhere(sums_four)
    keep, send, grad_stack_one, grad_bn_all, norm_squares = call(
        functools.partial(
            first_back_body, (rows, chans, own, nc, one_width, groups, pixel_count)
        ),
        [
            struct((chans // 2, total_width), bf16),
            struct((chans // 2, total_width), bf16),
            struct((two_width, wide), bf16),
            struct((4, chans), f32),
            struct((1, 1), f32),
        ],
        scratch=[pltpu.VMEM((one_width, wide), bf16)],
        smem=1,
    )(
        place, slope_one, above_four, below_four, raw_one, above_one, below_one, means_one,
        stats_four, norm, grads_two, own_stack, halo_stack, hidden, grad_stack,
    )
    back_blocks = call(
        functools.partial(inputs_back_body, (rows, chans, lid, lid_own, cam_own, spg, nc)),
        struct((members, lid_own + own + cam_own, cells), bf16),
    )(grad_stack_one, kernel_one_t, mixed_blocks)
    home = exchange(back_blocks, tile_groups)

    halved = call(add_body, struct(keep.shape, bf16), after=(back_blocks,))(keep, chan_swap(send, 1))
    piece_rows = own // spg
    pieces = exchange(halved.reshape(members // 2, piece_rows, total_width), half_groups)
    piece = call(sum_body, struct((piece_rows, total_width), bf16))(pieces)
    other = jnp.zeros_like(piece)
    shift = members
    while shift < devices:
        if shift > members:
            piece = (piece.astype(f32) + other.astype(f32)).astype(bf16)
        other = lax.ppermute(piece, AXES, [(i, i ^ shift) for i in range(devices)])
        shift *= 2
    merged = call(
        functools.partial(merge_body, spg), struct((spg, piece_rows, packed_width), bf16)
    )(piece, other)
    merged = exchange(merged, strip_groups)
    squares = jnp.sum(merged[:, 0, total_width : total_width + 3].astype(f32)).reshape(1, 1)
    own_grads = merged.reshape(own, packed_width)
    bit = 1
    while bit < nc:
        squares = squares + chan_swap(squares, bit)
        bit *= 2
    grad_bn = lax.dynamic_slice(grad_bn_all, (0, chan * own), (4, own))

    depth = back_blocks.shape[1]
    grad_lidar = home[:, :lid_own].astype(f32).reshape(lidar_bev.shape)
    mixed = home[:, lid_own : lid_own + own].astype(f32).reshape(cotangent.shape)
    grad_cam = pl.pallas_call(
        functools.partial(spread_body, grids, cells, cam_own, lid_own + own),
        grid=(points // block,),
        in_specs=[
            pl.BlockSpec((1, block), lambda i: (0, i)),
            pl.BlockSpec((grids, depth, cells), lambda i: (0, 0, 0)),
        ],
        out_specs=pl.BlockSpec((cam_own, block), lambda i: (0, i)),
        out_shape=struct((cam_own, points), f32),
        compiler_params=pltpu.CompilerParams(vmem_limit_bytes=VMEM_BYTES),
    )(index_row, home)

    tall = lambda array: array.transpose(turn)
    state = [
        *(tall(array) for array in (w_cam, m_cam, v_cam)),
        *(tall(array) for array in (w_lidar, m_lidar, v_lidar)),
        w_mid, m_mid, v_mid,
    ]
    norm_state = [bn_params, m_bn, v_bn]
    *updated, grad_norm = pl.pallas_call(
        functools.partial(adam_body, lid, cam, chans),
        in_specs=[near] * 7 + [far] * 9,
        out_specs=[near] * 3 + [far] * 9 + [near],
        out_shape=[struct(array.shape, f32) for array in norm_state + state] + [struct((1, 1), f32)],
        scratch_shapes=[
            *(pltpu.VMEM(array.shape, f32) for array in state),
            pltpu.SemaphoreType.DMA((9, 3)),
            pltpu.SemaphoreType.DMA((9, 3)),
        ],
        compiler_params=pltpu.CompilerParams(vmem_limit_bytes=VMEM_MOST),
    )(squares, norm_squares, own_grads, grad_bn, *norm_state, *state)
    turned = [tall(array) for array in updated[3:9]]
    return (mixed, grad_cam, grad_lidar, grad_norm.reshape(()), *turned, *updated[9:], *updated[:3])


def solution(mesh):
    return jax.shard_map(
        shards,
        mesh=mesh,
        in_specs=(
            P("chan", "strip"),
            P("strip"),
            P(None, "chan", "strip", None),
            P(None, None, None, "chan"),
            P(None, None, None, "chan"),
            P(None, None, "chan", None),
            P(None, "chan"),
            P(None, "chan", "strip", None),
            P(None, None, None, "chan"),
            P(None, None, None, "chan"),
            P(None, None, None, "chan"),
            P(None, None, None, "chan"),
            P(None, None, "chan", None),
            P(None, None, "chan", None),
            P(None, "chan"),
            P(None, "chan"),
        ),
        out_specs=(
            P(None, "chan", "strip", None),
            P("chan", "strip"),
            P(None, "chan", "strip", None),
            P(),
            P(None, None, None, "chan"),
            P(None, None, None, "chan"),
            P(None, None, None, "chan"),
            P(None, None, None, "chan"),
            P(None, None, None, "chan"),
            P(None, None, None, "chan"),
            P(None, None, "chan", None),
            P(None, None, "chan", None),
            P(None, None, "chan", None),
            P(None, "chan"),
            P(None, "chan"),
            P(None, "chan"),
        ),
        check_vma=False,
    )
```

time: 207 us -> 186 us (0.90)
  local copies, waits for them, and re-layouts: 19.5 us -> 4.31 us
  Pallas kernels: 41.4 us -> 44.8 us
  waiting for transfers between devices: 45.7 us -> 42.6 us
  other arithmetic: 7.02 us -> 4.02 us
    unnamed x45 -> x10, local copies, waits for them, and re-layouts: 10.4 us -> 0.02 us
    all_to_all x3, waiting for transfers between devices: 17.9 us -> 10.5 us  [exchange(): lax.all_to_all(blocks, AXES, 0, 0, axis_index_groups=parts, tiled=True)]
    ppermute x6 -> x5, waiting for transfers between devices: 8.21 us -> 12.9 us  [chan_swap(): return lax.ppermute(values, 'chan', [(c, c ^ bit) for c in range(nc)])]
    pallas_call x8 -> x14, Pallas kernels: 29.6 us -> 33 us  [the longest x12 23.1 us: run(): pl.pallas_call(lambda *refs: body(*refs[waits:]), out_shape=out_shape, in...]
    slice x2 -> x0, local copies, waits for them, and re-layouts: 2.14 us -> none  [the longest x1 1.12 us: shards(): own_grads[:, 3 * one_width:]]
    ppermute x6 -> x5, starting transfers between devices: 5.7 us -> 5.15 us  [chan_swap(): return lax.ppermute(values, 'chan', [(c, c ^ bit) for c in range(nc)])]
  transfers between devices with their start and end apart: 14 -> 13, of which waited for: 8 -> 8; matrix products, arithmetic and copies ran while one was open for 5% -> 4% of each run, Pallas kernels for 11% -> 11%
where the time goes in v2:
time: 186 us; the launch traced here: 185 us
  blocking collectives  64.1 us (34%)
  Pallas kernels  44.8 us (24%)
  waiting for transfers between devices  42.6 us (23%)
  starting transfers between devices  22.3 us (12%)
  local copies, waits for them, and re-layouts  4.31 us (2%)
  other arithmetic  4.02 us (2%)
  between operations  2.91 us (2%)
    all_to_all x4, blocking collectives, everywhere(): return lax.all_to_all(copies, AXES, 0, 0, tiled=True)  42.1 us
    pallas_call x12, Pallas kernels, run(): pl.pallas_call(lambda *refs: body(*refs[waits:]), out_shape=out_shape, in...  23.1 us
    all_to_all x1, blocking collectives, exchange(): lax.all_to_all(blocks, AXES, 0, 0, axis_index_groups=parts, tiled=True)  21.9 us
    ppermute x1, waiting for transfers between devices, shards(): other = lax.ppermute(piece, AXES, [(i, i ^ shift) for i in range(devices)])  16.8 us
    ppermute x5, waiting for transfers between devices, chan_swap(): return lax.ppermute(values, 'chan', [(c, c ^ bit) for c in range(nc)])  12.9 us
    all_to_all x3, starting transfers between devices, exchange(): lax.all_to_all(blocks, AXES, 0, 0, axis_index_groups=parts, tiled=True)  11.9 us
    all_to_all x3, waiting for transfers between devices, exchange(): lax.all_to_all(blocks, AXES, 0, 0, axis_index_groups=parts, tiled=True)  10.5 us
    pallas_call x1, Pallas kernels, shards(): pl.pallas_call(functools.partial(adam_body, lid, cam, chans), in_specs=[n...  6.65 us
  transfers between devices with their start and end apart: 13, of which 8 were waited for; matrix products, arithmetic and copies ran while one was open for 4% of the time, Pallas kernels for 11%

profile of v2, /device:TPU:0, one launch (start us, length us, event | category | flops | bytes accessed | tf_op | source)
XLA Modules:
  0.0 185.1 jit_solution(7591257401703424613)
XLA Ops:
  0.7 3.3 %shard_map.279 = bf16[64,5504]{1,0:T(8,128)(2,1)} custom-call(f32[4,64]{1,0:T(4,128)} %refs_0_.1, f32[3,3,64,256]{3,2,1,0:T(8,128)} %bitcast.32, f32[3,3,64,80]{3,2,1,0:T(8,128)} %bitcast.34, f32[3,3,64,256]{3,2,1,0:T(8,128)} %refs_9_.1), custom_call_target="tpu_custom_call" | custom-call | tf_op jit(solution)/shard_map/pallas_call | solution.py:712
  4.0 3.0 %collective-permute-start = (bf16[1,64,5504]{2,1,0:T(8,128)(2,1)}, bf16[1,64,5504]{2,1,0:T(8,128)(2,1)S(1)}, u32[]{:S(2)}, u32[]{:S(2)}) collective-permute-start(bf16[1,64,5504]{2,1,0:T(8,128)(2,1)} %bitcast.23), channel_id=1, source_target_pairs={{0,2},{1,3},{2,0},{3,1},{4,6},{5,7},{6,4},{7,5},{8,10},{9,11},{10,... | collective-permute-start | bytes 2113544 | tf_op jit(solution)/shard_map/ppermute | solution.py:646
  7.0 0.3 reshape.66
  7.4 0.3 reshape.67
  7.7 5.5 %shard_map.282 = bf16[16,20,256]{2,1,0:T(8,128)(2,1)S(1)} custom-call(s32[1,16384]{1,0:T(1,128)S(1)} %bitcast.27, bf16[20,16384]{1,0:T(8,128)(2,1)S(1)} %copy-done.1), custom_call_target="tpu_custom_call" | custom-call | tf_op jit(solution)/shard_map/pallas_call | solution.py:685
  13.2 1.1 pad_maximum_fusion.1
  14.4 4.0 %all-to-all-start = ((bf16[16,148,256]{2,1,0:T(8,128)(2,1)}), bf16[16,148,256]{2,1,0:T(8,128)(2,1)S(1)}, u32[]{:S(2)}, u32[]{:S(2)}) async-start(bf16[16,148,256]{2,1,0:T(8,128)(2,1)} %pad_maximum_fusion.1), calls=%async_computation | async-start | bytes 2490368 | tf_op jit(solution)/shard_map/all_to_all | solution.py:640
  18.4 9.9 %collective-permute-done.refs_2_ = bf16[1,64,5504]{2,1,0:T(8,128)(2,1)S(1)} collective-permute-done((bf16[1,64,5504]{2,1,0:T(8,128)(2,1)}, bf16[1,64,5504]{2,1,0:T(8,128)(2,1)S(1)}, u32[]{:S(2)}, u32[]{:S(2)}) %collective-permute-start) | collective-permute-done | bytes 704544 | tf_op jit(solution)/shard_map/ppermute | solution.py:646
  28.4 1.2 pad_maximum_fusion
  29.6 7.5 %all-to-all-done.refs_0_ = bf16[16,148,256]{2,1,0:T(8,128)(2,1)S(1)} async-done(((bf16[16,148,256]{2,1,0:T(8,128)(2,1)}), bf16[16,148,256]{2,1,0:T(8,128)(2,1)S(1)}, u32[]{:S(2)}, u32[]{:S(2)}) %all-to-all-start) | async-done | bytes 1212448 | tf_op jit(solution)/shard_map/all_to_all | solution.py:640
  37.2 2.7 %collective-permute-start.2 = (bf16[4,148,128]{2,1,0:T(8,128)(2,1)S(1)}, bf16[4,148,128]{2,1,0:T(8,128)(2,1)S(1)}, u32[]{:S(2)}, u32[]{:S(2)}) collective-permute-start(bf16[4,148,128]{2,1,0:T(8,128)(2,1)S(1)} %slice_select_fusion), channel_id=1, source_target_pairs={{0,16},{1,17},{2,18},{3,19},{4,20},{5,21},{6,22},{7,23},{8,24},{9,... | collective-permute-start | bytes 454664 | tf_op jit(solution)/shard_map/ppermute | solution.py:653
  39.9 1.7 shard_map.280
  41.6 0.8 shard_map.281
  42.4 2.2 %shard_map.283 = (bf16[1024,1280]{1,0:T(8,128)(2,1)S(1)}, bf16[256,1024]{1,0:T(8,128)(2,1)S(1)}, f32[256,1024]{1,0:T(8,128)S(1)}) custom-call(bf16[16,148,256]{2,1,0:T(8,128)(2,1)S(1)} %all-to-all-done.refs_0_, bf16[256,3072]{1,0:T(8,128)(2,1)S(1)} %get-tuple-element.61.refs_0_.refs_1_.refs_6_), custom_call_target="tpu_custom_call" | custom-call | tf_op jit(solution)/shard_map/pallas_call | solution.py:43
  44.6 2.4 %collective-permute-done.2.refs_4_.refs_5_ = bf16[4,148,128]{2,1,0:T(8,128)(2,1)S(1)} collective-permute-done((bf16[4,148,128]{2,1,0:T(8,128)(2,1)S(1)}, bf16[4,148,128]{2,1,0:T(8,128)(2,1)S(1)}, u32[]{:S(2)}, u32[]{:S(2)}) %collective-permute-start.2) | collective-permute-done | bytes 151584 | tf_op jit(solution)/shard_map/ppermute | solution.py:653
  47.0 1.3 shard_map.284
  48.4 12.4 %all_to_all.40.refs_4_ = f32[32,2,256]{2,1,0:T(2,128)S(1)} all-to-all(f32[32,2,256]{2,1,0:T(2,128)S(1)} %get-tuple-element.68), channel_id=1, replica_groups=mesh['strip'=8,'chan'=4] {'strip','chan'}, dimensions={0} | all-to-all | bytes 131072 | tf_op jit(solution)/shard_map/all_to_all | solution.py:643
  60.8 2.9 %shard_map.285 = (f32[256,1024]{1,0:T(8,128)S(1)}, f32[32,2,256]{2,1,0:T(2,128)S(1)}, f32[1,256,128]{2,1,0:T(8,128)S(1)}, f32[256,1024]{1,0:T(8,128)S(1)}, f32[256,128]{1,0:T(8,128)S(1)}) custom-call(s32[2]{0:T(128)S(1)} %pad_add_fusion.refs_0_.refs_2_, f32[256,1024]{1,0:T(8,128)S(1)} %get-tuple-element.66.refs_1_.refs_9_.refs_4_, ...), custom_call_target="tpu_custom_call" | custom-call | tf_op jit(solution)/shard_map/pallas_call | solution.py:43
  63.6 0.7 collective-permute-start.4
  64.4 10.0 %all_to_all.41.refs_4_ = f32[32,2,256]{2,1,0:T(2,128)S(1)} all-to-all(f32[32,2,256]{2,1,0:T(2,128)S(1)} %get-tuple-element.72), channel_id=1, replica_groups=mesh['strip'=8,'chan'=4] {'strip','chan'}, dimensions={0} | all-to-all | bytes 131072 | tf_op jit(solution)/shard_map/all_to_all | solution.py:643
  74.4 1.9 shard_map.286
  76.3 9.6 %all_to_all.42.refs_6_ = f32[32,2,256]{2,1,0:T(2,128)S(1)} all-to-all(f32[32,2,256]{2,1,0:T(2,128)S(1)} %get-tuple-element.78), channel_id=1, replica_groups=mesh['strip'=8,'chan'=4] {'strip','chan'}, dimensions={0} | all-to-all | bytes 131072 | tf_op jit(solution)/shard_map/all_to_all | solution.py:643
  85.9 3.0 %shard_map.287 = (f32[256,1024]{1,0:T(8,128)S(1)}, f32[32,2,256]{2,1,0:T(2,128)S(1)}, f32[1,256,128]{2,1,0:T(8,128)S(1)}, bf16[768,1280]{1,0:T(8,128)(2,1)S(1)}, f32[2,256]{1,0:T(2,128)S(1)}) custom-call(s32[2]{0:T(128)S(1)} %pad_add_fusion.refs_0_.refs_2_, f32[256,1280]{1,0:T(8,128)S(1)} %get-tuple-element.76.refs_1_, ...), custom_call_target="tpu_custom_call" | custom-call | tf_op jit(solution)/shard_map/pallas_call | solution.py:43
  88.9 0.7 collective-permute-start.5
  89.6 10.0 %all_to_all.43.refs_8_ = f32[32,2,256]{2,1,0:T(2,128)S(1)} all-to-all(f32[32,2,256]{2,1,0:T(2,128)S(1)} %get-tuple-element.82), channel_id=1, replica_groups=mesh['strip'=8,'chan'=4] {'strip','chan'}, dimensions={0} | all-to-all | bytes 131072 | tf_op jit(solution)/shard_map/all_to_all | solution.py:643
  99.7 5.0 %shard_map.288 = (bf16[128,5376]{1,0:T(8,128)(2,1)S(1)}, bf16[128,5376]{1,0:T(8,128)(2,1)S(1)}, bf16[768,1280]{1,0:T(8,128)(2,1)S(1)}, f32[4,256]{1,0:T(4,128)S(1)}, f32[1,1]{1,0:T(1,128)}) custom-call(s32[2]{0:T(128)S(1)} %pad_add_fusion.refs_0_.refs_2_, f32[256,1024]{1,0:T(8,128)S(1)} %get-tuple-element.80.refs_1_, ...), custom_call_target="tpu_custom_call" | custom-call | tf_op jit(solution)/shard_map/pallas_call | solution.py:43
  104.7 0.1 collective-permute-start.6
  104.9 2.8 %shard_map.289.refs_0_ = bf16[16,148,256]{2,1,0:T(8,128)(2,1)} custom-call(bf16[768,1280]{1,0:T(8,128)(2,1)S(1)} %get-tuple-element.87.refs_0_, bf16[336,2304]{1,0:T(8,128)(2,1)S(1)} %get-tuple-element.63.refs_0_.refs_1_, bf16[16,64,256]{2,1,0:T(8,128)(2,1)S(1)} %get-tuple-element.88.refs_2_), custom_call_target="tpu_custom_call" | custom-call | tf_op jit(solution)/shard_map/pallas_call | solution.py:43
  107.7 0.2 collective-permute-done.6.refs_2_
  107.9 0.3 shard_map.291
  108.2 21.9 %all_to_all.44.refs_0_ = bf16[8,16,5376]{2,1,0:T(8,128)(2,1)S(1)} all-to-all(bf16[8,16,5376]{2,1,0:T(8,128)(2,1)S(1)} %bitcast.26), channel_id=1, replica_groups={{0,4,8,12,2,6,10,14},{1,5,9,13,3,7,11,15},{16,20,24,28,18,22,26,30},{17..., dimensions={0} | all-to-all | bytes 2752512 | tf_op jit(solution)/shard_map/all_to_all | solution.py:640
  130.1 3.7 %all-to-all-start.5 = ((bf16[16,148,256]{2,1,0:T(8,128)(2,1)}), bf16[16,148,256]{2,1,0:T(8,128)(2,1)S(1)}, u32[]{:S(2)}, u32[]{:S(2)}) async-start(bf16[16,148,256]{2,1,0:T(8,128)(2,1)} %shard_map.289.refs_0_), calls=%async_computation.5 | async-start | bytes 2490368 | tf_op jit(solution)/shard_map/all_to_all | solution.py:640
  133.8 0.2 shard_map.292.refs_0_
  134.0 1.1 collective-permute-start.7
  135.1 16.8 %collective-permute-done.7.refs_1_ = bf16[16,5376]{1,0:T(8,128)(2,1)S(1)} collective-permute-done((bf16[16,5376]{1,0:T(8,128)(2,1)S(1)}, bf16[16,5376]{1,0:T(8,128)(2,1)S(1)}, u32[]{:S(2)}, u32[]{:S(2)}) %collective-permute-start.7) | collective-permute-done | bytes 172064 | tf_op jit(solution)/shard_map/ppermute | solution.py:840
  151.9 1.1 shard_map.293
  153.0 2.9 %all-to-all-done.5.grad_ref = bf16[16,148,256]{2,1,0:T(8,128)(2,1)S(1)} async-done(((bf16[16,148,256]{2,1,0:T(8,128)(2,1)}), bf16[16,148,256]{2,1,0:T(8,128)(2,1)S(1)}, u32[]{:S(2)}, u32[]{:S(2)}) %all-to-all-start.5) | async-done | bytes 1212448 | tf_op jit(solution)/shard_map/all_to_all | solution.py:640
  155.9 4.2 %all-to-all-start.7 = ((bf16[4,16,5504]{2,1,0:T(8,128)(2,1)}), bf16[4,16,5504]{2,1,0:T(8,128)(2,1)}, u32[]{:S(2)}, u32[]{:S(2)}) async-start(bf16[4,16,5504]{2,1,0:T(8,128)(2,1)} %shard_map.293), calls=%async_computation.7 | async-start | bytes 1409024 | tf_op jit(solution)/shard_map/all_to_all | solution.py:640
  160.1 0.6 constant_dynamic-slice_fusion.norm_grad_ref
  160.8 0.2 slice_convert_fusion
  161.0 1.5 reshape.80
  162.5 1.5 reshape.78
  164.0 6.3 %shard_map.290 = f32[20,16384]{1,0:T(8,128)} custom-call(s32[1,16384]{1,0:T(1,128)S(1)} %bitcast.28, bf16[16,148,256]{2,1,0:T(8,128)(2,1)S(1)} %all-to-all-done.5.grad_ref), custom_call_target="tpu_custom_call" | custom-call | tf_op jit(solution)/shard_map/pallas_call | solution.py:857
  170.3 1.3 fusion
  171.6 1.2 collective-permute-done.8
  174.1 2.0 %collective-permute-start.9 = (f32[1,1]{1,0:T(1,128)}, f32[1,1]{1,0:T(1,128)}, u32[]{:S(2)}, u32[]{:S(2)}) collective-permute-start(f32[1,1]{1,0:T(1,128)} %add.10), channel_id=1, source_target_pairs={{0,2},{1,3},{2,0},{3,1},{4,6},{5,7},{6,4},{7,5},{8,10},{9,11},{10,... | collective-permute-start | bytes 20 | tf_op jit(solution)/shard_map/ppermute | solution.py:646
  176.1 1.6 collective-permute-done.9
  178.3 6.7 %shard_map.294 = (f32[4,64]{1,0:T(4,128)}, f32[4,64]{1,0:T(4,128)}, f32[4,64]{1,0:T(4,128)}, f32[3,3,64,80]{3,2,1,0:T(8,128)}, f32[3,3,64,80]{3,2,1,0:T(8,128)},...) custom-call(f32[1,1]{1,0:T(1,128)S(6)} %add.11.squares_ref, ...), custom_call_target="tpu_custom_call" | custom-call | tf_op jit(solution)/shard_map/pallas_call | solution.py:876
  (20 shorter events, 0.2 us)
Async XLA Ops:
  0.6 6.4 %copy-start.3 = (bf16[16,64,2,128]{3,2,1,0:T(2,128)(2,1)S(1)}, bf16[16,64,2,128]{3,2,1,0:T(2,128)(2,1)}, u32[]{:S(2)}) copy-start(bf16[16,64,2,128]{3,2,1,0:T(2,128)(2,1)} %param.18) | copy-start | bytes 1572868
  0.7 6.7 %copy-start.4 = (bf16[16,64,2,128]{3,2,1,0:T(2,128)(2,1)S(1)}, bf16[16,64,2,128]{3,2,1,0:T(2,128)(2,1)}, u32[]{:S(2)}) copy-start(bf16[16,64,2,128]{3,2,1,0:T(2,128)(2,1)} %param.23) | copy-start | bytes 1572868
  4.0 3.7 %copy-start.1 = (bf16[20,16384]{1,0:T(8,128)(2,1)S(1)}, bf16[20,16384]{1,0:T(8,128)(2,1)}, u32[]{:S(2)}) copy-start(bf16[20,16384]{1,0:T(8,128)(2,1)} %feat_ref.1) | copy-start | bytes 1966084
  4.0 3.7 %copy-start.2 = (s32[16384]{0:T(1024)S(1)}, s32[16384]{0:T(1024)}, u32[]{:S(2)}) copy-start(s32[16384]{0:T(1024)} %param.17) | copy-start | bytes 196612
  4.0 24.3 %collective-permute-start = (bf16[1,64,5504]{2,1,0:T(8,128)(2,1)}, bf16[1,64,5504]{2,1,0:T(8,128)(2,1)S(1)}, u32[]{:S(2)}, u32[]{:S(2)}) collective-permute-start(bf16[1,64,5504]{2,1,0:T(8,128)(2,1)} %bitcast.23), channel_id=1, source_target_pairs={{0,2},{1,3},{2,0},{3,1},{4,6},{5,7},{6,4},{7,5},{8,10},{9,11},{10,... | collective-permute-start | bytes 2113544 | tf_op jit(solution)/shard_map/ppermute | solution.py:646
  14.4 14.0 %copy-start = (bf16[64,5504]{1,0:T(8,128)(2,1)S(1)}, bf16[64,5504]{1,0:T(8,128)(2,1)}, u32[]{:S(2)}) copy-start(bf16[64,5504]{1,0:T(8,128)(2,1)} %shard_map.279) | copy-start | bytes 2113540
  14.4 22.7 %all-to-all-start = ((bf16[16,148,256]{2,1,0:T(8,128)(2,1)}), bf16[16,148,256]{2,1,0:T(8,128)(2,1)S(1)}, u32[]{:S(2)}, u32[]{:S(2)}) async-start(bf16[16,148,256]{2,1,0:T(8,128)(2,1)} %pad_maximum_fusion.1), calls=%async_computation | async-start | bytes 2490368 | tf_op jit(solution)/shard_map/all_to_all | solution.py:640
  29.6 10.3 %collective-permute-start.1 = (bf16[2,64,5504]{2,1,0:T(8,128)(2,1)}, bf16[2,64,5504]{2,1,0:T(8,128)(2,1)}, u32[]{:S(2)}, u32[]{:S(2)}) collective-permute-start(bf16[2,64,5504]{2,1,0:T(8,128)(2,1)} %pad_maximum_fusion), channel_id=1, source_target_pairs={{0,1},{1,0},{2,3},{3,2},{4,5},{5,4},{6,7},{7,6},{8,9},{9,8},{10,11... | collective-permute-start | bytes 4227080 | tf_op jit(solution)/shard_map/ppermute | solution.py:646
  37.2 9.9 %collective-permute-start.2 = (bf16[4,148,128]{2,1,0:T(8,128)(2,1)S(1)}, bf16[4,148,128]{2,1,0:T(8,128)(2,1)S(1)}, u32[]{:S(2)}, u32[]{:S(2)}) collective-permute-start(bf16[4,148,128]{2,1,0:T(8,128)(2,1)S(1)} %slice_select_fusion), channel_id=1, source_target_pairs={{0,16},{1,17},{2,18},{3,19},{4,20},{5,21},{6,22},{7,23},{8,24},{9,... | collective-permute-start | bytes 454664 | tf_op jit(solution)/shard_map/ppermute | solution.py:653
  48.3 12.5 %collective-permute-start.3 = (f32[256,128]{1,0:T(8,128)S(1)}, f32[256,128]{1,0:T(8,128)S(1)}, u32[]{:S(2)}, u32[]{:S(2)}) collective-permute-start(f32[256,128]{1,0:T(8,128)S(1)} %bitcast.30), channel_id=1, source_target_pairs={{0,16},{1,17},{2,18},{3,19},{4,20},{5,21},{6,22},{7,23},{8,24},{9,... | collective-permute-start | bytes 393224 | tf_op jit(solution)/shard_map/ppermute | solution.py:653
  63.6 10.8 %collective-permute-start.4 = (f32[256,128]{1,0:T(8,128)S(1)}, f32[256,128]{1,0:T(8,128)S(1)}, u32[]{:S(2)}, u32[]{:S(2)}) collective-permute-start(f32[256,128]{1,0:T(8,128)S(1)} %bitcast.31), channel_id=1, source_target_pairs={{0,16},{1,17},{2,18},{3,19},{4,20},{5,21},{6,22},{7,23},{8,24},{9,... | collective-permute-start | bytes 393224 | tf_op jit(solution)/shard_map/ppermute | solution.py:653
  88.9 10.8 %collective-permute-start.5 = (f32[256,128]{1,0:T(8,128)S(1)}, f32[256,128]{1,0:T(8,128)S(1)}, u32[]{:S(2)}, u32[]{:S(2)}) collective-permute-start(f32[256,128]{1,0:T(8,128)S(1)} %bitcast.29), channel_id=1, source_target_pairs={{0,16},{1,17},{2,18},{3,19},{4,20},{5,21},{6,22},{7,23},{8,24},{9,... | collective-permute-start | bytes 393224 | tf_op jit(solution)/shard_map/ppermute | solution.py:653
  104.7 3.1 %collective-permute-start.6 = (bf16[128,5376]{1,0:T(8,128)(2,1)S(1)}, bf16[128,5376]{1,0:T(8,128)(2,1)S(1)}, u32[]{:S(2)}, u32[]{:S(2)}) collective-permute-start(bf16[128,5376]{1,0:T(8,128)(2,1)S(1)} %get-tuple-element.90), channel_id=1, source_target_pairs={{0,1},{1,0},{2,3},{3,2},{4,5},{5,4},{6,7},{7,6},{8,9},{9,8},{10,11... | collective-permute-start | bytes 4128776 | tf_op jit(solution)/shard_map/ppermute | solution.py:646
  130.1 25.8 %all-to-all-start.5 = ((bf16[16,148,256]{2,1,0:T(8,128)(2,1)}), bf16[16,148,256]{2,1,0:T(8,128)(2,1)S(1)}, u32[]{:S(2)}, u32[]{:S(2)}) async-start(bf16[16,148,256]{2,1,0:T(8,128)(2,1)} %shard_map.289.refs_0_), calls=%async_computation.5 | async-start | bytes 2490368 | tf_op jit(solution)/shard_map/all_to_all | solution.py:640
  134.0 17.9 %collective-permute-start.7 = (bf16[16,5376]{1,0:T(8,128)(2,1)S(1)}, bf16[16,5376]{1,0:T(8,128)(2,1)S(1)}, u32[]{:S(2)}, u32[]{:S(2)}) collective-permute-start(bf16[16,5376]{1,0:T(8,128)(2,1)S(1)} %shard_map.292.refs_0_), channel_id=1, source_target_pairs={{0,16},{1,17},{2,18},{3,19},{4,20},{5,21},{6,22},{7,23},{8,24},{9,... | collective-permute-start | bytes 516104 | tf_op jit(solution)/shard_map/ppermute | solution.py:840
  155.9 14.3 %all-to-all-start.7 = ((bf16[4,16,5504]{2,1,0:T(8,128)(2,1)}), bf16[4,16,5504]{2,1,0:T(8,128)(2,1)}, u32[]{:S(2)}, u32[]{:S(2)}) async-start(bf16[4,16,5504]{2,1,0:T(8,128)(2,1)} %shard_map.293), calls=%async_computation.7 | async-start | bytes 1409024 | tf_op jit(solution)/shard_map/all_to_all | solution.py:640
  171.6 1.2 collective-permute-start.8
  174.1 3.6 %collective-permute-start.9 = (f32[1,1]{1,0:T(1,128)}, f32[1,1]{1,0:T(1,128)}, u32[]{:S(2)}, u32[]{:S(2)}) collective-permute-start(f32[1,1]{1,0:T(1,128)} %add.10), channel_id=1, source_target_pairs={{0,2},{1,3},{2,0},{3,1},{4,6},{5,7},{6,4},{7,5},{8,10},{9,11},{10,... | collective-permute-start | bytes 20 | tf_op jit(solution)/shard_map/ppermute | solution.py:646

commit v3 on v2

--- a/solution.py
+++ b/solution.py
@@ -33,7 +33,7 @@
     return (value + step - 1) // step * step
 
 
-def call(body, out_shape, scratch=(), smem=0, after=(), **options):
+def call(body, out_shape, scratch=(), smem=0, after=()):
     waits = len(after)
 
     def run(*operands):
@@ -47,7 +47,6 @@
             out_specs=jax.tree.map(lambda _: pl.BlockSpec(memory_space=pltpu.VMEM), out_shape),
             scratch_shapes=list(scratch),
             compiler_params=pltpu.CompilerParams(vmem_limit_bytes=VMEM_BYTES),
-            **options,
         )(*after, *operands)
 
     return run
@@ -101,53 +100,79 @@
     return mean, lax.rsqrt(variance + norm_eps)
 
 
-def pool_body(grids, cells, chans, index_ref, feat_ref, out_ref, acc_ref):
-    step = pl.program_id(0)
+def one_hot(low, cells):
+    count = low.shape[1]
+    tile = 16
+    given = jnp.broadcast_to(low.astype(f32), (tile, count)).astype(bf16)
+    row = lax.broadcasted_iota(jnp.int32, (tile, count), 0).astype(f32).astype(bf16)
+    one, zero = jnp.ones((), bf16), jnp.zeros((), bf16)
+    return jnp.concatenate(
+        [
+            jnp.where(given - jnp.asarray(start, bf16) == row, one, zero)
+            for start in range(0, cells, tile)
+        ],
+        axis=0,
+    )
+
+
+def pool_body(block, index_ref, feat_ref, lidar_ref, cot_ref, out_ref):
+    grids, own, cells = lidar_ref.shape
+    chans, points = feat_ref.shape
+    out_ref[:, :own] = lidar_ref[...]
+    out_ref[:, own : 2 * own] = cot_ref[...]
     rows = round_up(chans, 8)
-    index = index_ref[...]
-    high, low = index // cells, index % cells
-    count = index.shape[1]
-    feat = feat_ref[...].astype(f32)
-    feat = jnp.concatenate([feat, jnp.zeros((rows - chans, count), f32)], axis=0)
-    spread = jnp.concatenate(
-        [jnp.where(high == grid, feat, 0.0) for grid in range(grids)], axis=0
-    ).astype(bf16)
-    table = (lax.broadcasted_iota(jnp.int32, (cells, count), 0) == low).astype(f32).astype(bf16)
-    added = matmul_nt(spread, table)
-
-    @pl.when(step == 0)
-    def _():
-        acc_ref[...] = added
-
-    @pl.when(step > 0)
-    def _():
-        acc_ref[...] += added
-
-    @pl.when(step == pl.num_programs(0) - 1)
-    def _():
-        out_ref[...] = acc_ref[...].reshape(grids, rows, cells)[:, :chans].astype(bf16)
-
-
-def spread_body(grids, cells, chans, first, index_ref, grad_ref, out_ref):
+    total = None
+    for start in range(0, points, block):
+        at = slice(start, start + block)
+        index = index_ref[:, at]
+        high, low = index // cells, index % cells
+        feat = feat_ref[:, at].astype(f32)
+        feat = jnp.concatenate([feat, jnp.zeros((rows - chans, block), f32)], axis=0)
+        spread = jnp.concatenate([jnp.where(high == grid, feat, 0.0) for grid in range(grids)], axis=0)
+        term = matmul_nt(spread.astype(bf16), one_hot(low, cells))
+        total = term if total is None else total + term
+    out_ref[:, 2 * own :] = total.reshape(grids, rows, cells)[:, :chans].astype(bf16)
+
+
+def home_body(
+    block, index_ref, home_ref, lidar_far, mixed_far, cam_far, token_ref,
+    lidar_ref, mixed_ref, cam_ref, sems,
+):
+    grids, own, _, _ = lidar_ref.shape
+    cells = home_ref.shape[2]
+    chans, points = cam_ref.shape
+    token_ref[...] = jnp.zeros(token_ref.shape, f32)
+    copies = []
+    for i, (near, far) in enumerate(((lidar_ref, lidar_far), (mixed_ref, mixed_far))):
+        near[...] = home_ref[:, i * own : (i + 1) * own, :].astype(f32).reshape(near.shape)
+        copies.append(pltpu.make_async_copy(near, far, sems.at[i]))
+        copies[-1].start()
     rows = round_up(chans, 8)
-    index = index_ref[...]
-    high, low = index // cells, index % cells
-    count = index.shape[1]
-    table = (lax.broadcasted_iota(jnp.int32, (cells, count), 0) == low).astype(f32).astype(bf16)
-    grad = grad_ref[:, first : first + chans, :].astype(f32)
+    grad = home_ref[:, 2 * own : 2 * own + chans, :].astype(f32)
     grad = jnp.concatenate([grad, jnp.zeros((grids, rows - chans, cells), f32)], axis=1)
-    picked = matmul(grad.reshape(grids * rows, cells).astype(bf16), table)
-    total = jnp.zeros((rows, count), f32)
-    for grid in range(grids):
-        total = jnp.where(high == grid, picked[grid * rows : (grid + 1) * rows], total)
-    out_ref[...] = total[:chans]
+    grad = grad.reshape(grids * rows, cells).astype(bf16)
+    for start in range(0, points, block):
+        at = slice(start, start + block)
+        index = index_ref[:, at]
+        high, low = index // cells, index % cells
+        picked = matmul(grad, one_hot(low, cells))
+        total = jnp.zeros((rows, block), f32)
+        for grid in range(grids):
+            total = jnp.where(high == grid, picked[grid * rows : (grid + 1) * rows], total)
+        cam_ref[:, at] = total[:chans]
+    copies.append(pltpu.make_async_copy(cam_ref, cam_far, sems.at[2]))
+    copies[-1].start()
+    for copy in copies:
+        copy.wait()
 
 
 def pack_body(
     lid, cam, mid, one_width, norm_ref, lidar_far, cam_far, mid_far, out_ref,
-    lidar_ref, cam_ref, mid_ref, sems,
+    near_ref, lidar_ref, cam_ref, mid_ref, norm_sem, sems,
 ):
     rows = lidar_ref.shape[2]
+    norm_copy = pltpu.make_async_copy(norm_ref, near_ref, norm_sem)
+    norm_copy.start()
     pairs = ((lidar_far, lidar_ref), (cam_far, cam_ref), (mid_far, mid_ref))
     copies = [
         [pltpu.make_async_copy(far.at[a], near.at[a], sems.at[i, a]) for i, (far, near) in enumerate(pairs)]
@@ -170,7 +195,8 @@
         for b in range(3):
             start = 3 * one_width + (3 * a + b) * mid
             out_ref[:, start : start + mid] = mid_ref[a, b].astype(bf16)
-    norm = norm_ref[...]
+    norm_copy.wait()
+    norm = near_ref[...]
     norm = jnp.concatenate([norm, jnp.zeros((LANES - norm.shape[0], rows), f32)], axis=0)
     norm = jnp.concatenate([norm, jnp.zeros((LANES, LANES - rows), f32)], axis=1).T[:rows, :4]
     high = norm.astype(bf16)
@@ -539,49 +565,70 @@
         out_ref[copy, :, width:] = terms
 
 
-def adam_body(lid, cam, mid, squares_ref, norm_squares_ref, grads_ref, norm_grad_ref, *refs):
-    norm_ins, fars, refs = refs[:3], refs[3:12], refs[12:]
-    norm_outs, far_outs, norm_ref, refs = refs[:3], refs[3:12], refs[12], refs[13:]
-    nears, ins, outs = refs[:9], refs[9], refs[10]
+def tail_body(width, pieces_ref, out_ref):
+    out_ref[...] = jnp.broadcast_to(jnp.sum(pieces_ref[:, :, width:].astype(f32)), out_ref.shape)
+
+
+def adam_body(lid, cam, mid, chans, smalls, *refs):
+    square_refs, grads_ref, refs = refs[:chans], refs[chans], refs[chans + 1 :]
+    small_fars, fars, refs = refs[:smalls], refs[smalls : smalls + 9], refs[smalls + 9 :]
+    small_outs, far_outs, refs = refs[:4], refs[4:13], refs[13:]
+    small_nears, nears, refs = refs[:smalls], refs[smalls : smalls + 9], refs[smalls + 9 :]
+    small_ins, ins, outs, norm_ref = refs
     one_width = round_up(3 * lid + 3 * cam, 256)
+    first = [
+        pltpu.make_async_copy(far, near, small_ins.at[i])
+        for i, (far, near) in enumerate(zip(small_fars, small_nears, strict=True))
+    ]
     reads = [
         [pltpu.make_async_copy(fars[i].at[a], nears[i].at[a], ins.at[i, a]) for i in range(9)]
         for a in range(3)
     ]
-    writes = [
-        [pltpu.make_async_copy(nears[i].at[a], far_outs[i].at[a], outs.at[i, a]) for i in range(9)]
-        for a in range(3)
-    ]
-    for group in reads:
+    for group in (first, *reads):
         for copy in group:
             copy.start()
-    norm = jnp.sqrt(squares_ref[...] + norm_squares_ref[...])
+    for copy in first:
+        copy.wait()
+    squares = [ref[0:1, 0:1] for ref in square_refs]
+    norm_squares_ref, norm_grad_ref, *norm_state = small_nears
+    while len(squares) > 1:
+        squares = [squares[i] + squares[i + 1] for i in range(0, len(squares), 2)]
+    norm = jnp.sqrt(squares[0] + norm_squares_ref[...])
     norm_ref[...] = norm
     factor = jnp.minimum(1.0, clip_norm / (norm + 1e-06))
 
-    def step(refs, results, at, gradient, rate):
-        weight, first, second = (ref[at] for ref in refs)
-        for ref, value in zip(results, adam(weight, factor * gradient, first, second, rate), strict=True):
+    def step(state, at, gradient, rate):
+        weight, first, second = (ref[at] for ref in state)
+        for ref, value in zip(state, adam(weight, factor * gradient, first, second, rate), strict=True):
             ref[at] = value
 
-    step(norm_ins, norm_outs, ..., norm_grad_ref[...], norm_rate)
+    step(norm_state, ..., norm_grad_ref[...], norm_rate)
+    writes = [
+        [
+            pltpu.make_async_copy(near, far, small_ins.at[i])
+            for i, (near, far) in enumerate(zip((*norm_state, norm_ref), small_outs, strict=True))
+        ]
+    ]
+    for copy in writes[0]:
+        copy.start()
     for a in range(3):
         for copy in reads[a]:
             copy.wait()
         base = a * one_width
         tail = grads_ref[:, base + 3 * lid : base + one_width].astype(f32)
         for b in range(3):
+            start = 3 * one_width + (3 * a + b) * mid
             given = (
                 tail[:, b * cam : (b + 1) * cam],
                 grads_ref[:, base + b * lid : base + (b + 1) * lid].astype(f32),
-                grads_ref[
-                    :, 3 * one_width + (3 * a + b) * mid : 3 * one_width + (3 * a + b + 1) * mid
-                ].astype(f32),
+                grads_ref[:, start : start + mid].astype(f32),
             )
             for i, gradient in enumerate(given):
-                state = nears[3 * i : 3 * i + 3]
-                step(state, state, (a, b), gradient, learn_rate)
-        for copy in writes[a]:
+                step(nears[3 * i : 3 * i + 3], (a, b), gradient, learn_rate)
+        writes.append(
+            [pltpu.make_async_copy(nears[i].at[a], far_outs[i].at[a], outs.at[i, a]) for i in range(9)]
+        )
+        for copy in writes[-1]:
             copy.start()
     for group in writes:
         for copy in group:
@@ -681,26 +728,12 @@
     packed_width = total_width + LANES
 
     index_row = cell_index.reshape(1, points)
-    block = math.gcd(points, 2048)
-    pooled = pl.pallas_call(
-        functools.partial(pool_body, grids, cells, cam_own),
-        grid=(points // block,),
-        in_specs=[
-            pl.BlockSpec((1, block), lambda i: (0, i)),
-            pl.BlockSpec((cam_own, block), lambda i: (0, i)),
-        ],
-        out_specs=pl.BlockSpec((grids, cam_own, cells), lambda i: (0, 0, 0)),
-        out_shape=struct((grids, cam_own, cells), bf16),
-        scratch_shapes=[pltpu.VMEM((grids * round_up(cam_own, 8), cells), f32)],
-        compiler_params=pltpu.CompilerParams(vmem_limit_bytes=VMEM_BYTES),
-    )(index_row, cam_feats)
-    joined = jnp.concatenate(
-        [
-            lidar_bev.reshape(grids, lid_own, cells),
-            cotangent.reshape(grids, own, cells),
-            pooled,
-        ],
-        axis=1,
+    block = math.gcd(points, 1024)
+    joined = call(
+        functools.partial(pool_body, block), struct((grids, lid_own + own + cam_own, cells), bf16)
+    )(
+        index_row, cam_feats, lidar_bev.reshape(grids, lid_own, cells),
+        cotangent.reshape(grids, own, cells),
     )
     got = exchange(joined, tile_groups)
     above, below = neighbours(edge_cells(got))
@@ -711,11 +744,12 @@
     weights = [w_lidar.transpose(turn), w_cam.transpose(turn), w_mid]
     packed = pl.pallas_call(
         functools.partial(pack_body, lid, cam, chans, one_width),
-        in_specs=[near, far, far, far],
+        in_specs=[far] * 4,
         out_specs=near,
         out_shape=struct((own, packed_width), bf16),
         scratch_shapes=[
-            *(pltpu.VMEM(weight.shape, f32) for weight in weights),
+            *(pltpu.VMEM(weight.shape, f32) for weight in (bn_params, *weights)),
+            pltpu.SemaphoreType.DMA,
             pltpu.SemaphoreType.DMA((3, 3)),
         ],
         compiler_params=pltpu.CompilerParams(vmem_limit_bytes=VMEM_MOST),
@@ -840,53 +874,56 @@
         other = lax.ppermute(piece, AXES, [(i, i ^ shift) for i in range(devices)])
         shift *= 2
     merged = call(
-        functools.partial(merge_body, spg), struct((spg, piece_rows, packed_width), bf16)
+        functools.partial(merge_body, spg), struct((spg, piece_rows, packed_width), bf16), after=(home,)
     )(piece, other)
     merged = exchange(merged, strip_groups)
-    squares = jnp.sum(merged[:, 0, total_width : total_width + 3].astype(f32)).reshape(1, 1)
     own_grads = merged.reshape(own, packed_width)
-    bit = 1
-    while bit < nc:
-        squares = squares + chan_swap(squares, bit)
-        bit *= 2
-    grad_bn = lax.dynamic_slice(grad_bn_all, (0, chan * own), (4, own))
-
-    depth = back_blocks.shape[1]
-    grad_lidar = home[:, :lid_own].astype(f32).reshape(lidar_bev.shape)
-    mixed = home[:, lid_own : lid_own + own].astype(f32).reshape(cotangent.shape)
-    grad_cam = pl.pallas_call(
-        functools.partial(spread_body, grids, cells, cam_own, lid_own + own),
-        grid=(points // block,),
-        in_specs=[
-            pl.BlockSpec((1, block), lambda i: (0, i)),
-            pl.BlockSpec((grids, depth, cells), lambda i: (0, 0, 0)),
-        ],
-        out_specs=pl.BlockSpec((cam_own, block), lambda i: (0, i)),
-        out_shape=struct((cam_own, points), f32),
+    images = [struct(lidar_bev.shape, f32), struct(cotangent.shape, f32), struct((cam_own, points), f32)]
+    grad_lidar, mixed, grad_cam, token = pl.pallas_call(
+        functools.partial(home_body, block),
+        in_specs=[near] * 2,
+        out_specs=[far] * 3 + [near],
+        out_shape=[*images, struct((8, LANES), f32)],
+        scratch_shapes=[
+            *(pltpu.VMEM(image.shape, f32) for image in images),
+            pltpu.SemaphoreType.DMA((3,)),
+        ],
         compiler_params=pltpu.CompilerParams(vmem_limit_bytes=VMEM_BYTES),
     )(index_row, home)
-
     tall = lambda array: array.transpose(turn)
     state = [
         *(tall(array) for array in (w_cam, m_cam, v_cam)),
         *(tall(array) for array in (w_lidar, m_lidar, v_lidar)),
         w_mid, m_mid, v_mid,
     ]
+    squares = call(
+        functools.partial(tail_body, total_width),
+        struct((8, LANES), f32),
+        after=(token,),
+    )(merged)
+    squares = [squares] + [
+        lax.ppermute(squares, "chan", [(c, c ^ mask) for c in range(nc)]) for mask in range(1, nc)
+    ]
+    grad_bn = lax.dynamic_slice(grad_bn_all, (0, chan * own), (4, own))
     norm_state = [bn_params, m_bn, v_bn]
-    *updated, grad_norm = pl.pallas_call(
-        functools.partial(adam_body, lid, cam, chans),
-        in_specs=[near] * 7 + [far] * 9,
-        out_specs=[near] * 3 + [far] * 9 + [near],
-        out_shape=[struct(array.shape, f32) for array in norm_state + state] + [struct((1, 1), f32)],
+    small = [norm_squares, grad_bn, *norm_state]
+    results = [*norm_state, norm_squares, *state]
+    updated = pl.pallas_call(
+        functools.partial(adam_body, lid, cam, chans, nc, len(small)),
+        in_specs=[near] * (nc + 1) + [far] * (len(small) + 9),
+        out_specs=[far] * 13,
+        out_shape=[struct(array.shape, f32) for array in results],
         scratch_shapes=[
-            *(pltpu.VMEM(array.shape, f32) for array in state),
+            *(pltpu.VMEM(array.shape, f32) for array in small + state),
+            pltpu.SemaphoreType.DMA((len(small),)),
             pltpu.SemaphoreType.DMA((9, 3)),
             pltpu.SemaphoreType.DMA((9, 3)),
+            pltpu.VMEM((1, 1), f32),
         ],
         compiler_params=pltpu.CompilerParams(vmem_limit_bytes=VMEM_MOST),
-    )(squares, norm_squares, own_grads, grad_bn, *norm_state, *state)
-    turned = [tall(array) for array in updated[3:9]]
-    return (mixed, grad_cam, grad_lidar, grad_norm.reshape(()), *turned, *updated[9:], *updated[:3])
+    )(*squares, own_grads, *small, *state)
+    turned = [tall(array) for array in updated[4:10]]
+    return (mixed, grad_cam, grad_lidar, updated[3].reshape(()), *turned, *updated[10:], *updated[:3])
 
 
 def solution(mesh):

time: 186 us -> 183 us (0.984)
  waiting for transfers between devices: 42.6 us -> 48.6 us
  other arithmetic: 4.02 us -> 1.33 us
  local copies, waits for them, and re-layouts: 4.31 us -> 1.91 us
  Pallas kernels: 44.8 us -> 42.8 us
    ppermute x1, waiting for transfers between devices: 16.8 us -> 0.01 us  [shards(): other = lax.ppermute(piece, AXES, [(i, i ^ shift) for i in range(devices)])]
    all_to_all x3, waiting for transfers between devices: 10.5 us -> 26.2 us  [exchange(): lax.all_to_all(blocks, AXES, 0, 0, axis_index_groups=parts, tiled=True)]
    pallas_call x3 -> x2, Pallas kernels: 18.4 us -> 12.2 us  [the longest x1 6.81 us: shards(): pl.pallas_call(functools.partial(adam_body, lid, cam, chans, nc, len(smal...]
    pallas_call x12 -> x14, Pallas kernels: 23.1 us -> 27.9 us  [run(): pl.pallas_call(lambda *refs: body(*refs[waits:]), out_shape=out_shape, in...]
    ppermute x5 -> x3, waiting for transfers between devices: 12.9 us -> 17.5 us  [chan_swap(): return lax.ppermute(values, 'chan', [(c, c ^ bit) for c in range(nc)])]
    reshape x2 -> x0, local copies, waits for them, and re-layouts: 2.98 us -> none  [the longest x1 1.49 us: shards(): grad_lidar = home[:, :lid_own].astype(f32).reshape(lidar_bev.shape)]
    ppermute x5 -> x3, starting transfers between devices: 5.15 us -> 3.15 us  [chan_swap(): return lax.ppermute(values, 'chan', [(c, c ^ bit) for c in range(nc)])]
    ppermute x0 -> x3, starting transfers between devices: none -> 1.93 us  [shards(): lax.ppermute(squares, 'chan', [(c, c ^ mask) for c in range(nc)])]
  transfers between devices with their start and end apart: 13 -> 14, of which waited for: 8 -> 8; matrix products, arithmetic and copies ran while one was open for 4% -> 1% of each run, Pallas kernels for 11% -> 10%
where the time goes in v3:
time: 183 us; the launch traced here: 182 us
  blocking collectives  65 us (36%)
  waiting for transfers between devices  48.6 us (27%)
  Pallas kernels  42.8 us (23%)
  starting transfers between devices  21.8 us (12%)
  local copies, waits for them, and re-layouts  1.91 us (1%)
    all_to_all x4, blocking collectives, everywhere(): return lax.all_to_all(copies, AXES, 0, 0, tiled=True)  43 us
    pallas_call x14, Pallas kernels, run(): pl.pallas_call(lambda *refs: body(*refs[waits:]), out_shape=out_shape, in...  27.9 us
    all_to_all x3, waiting for transfers between devices, exchange(): lax.all_to_all(blocks, AXES, 0, 0, axis_index_groups=parts, tiled=True)  26.2 us
    all_to_all x1, blocking collectives, exchange(): lax.all_to_all(blocks, AXES, 0, 0, axis_index_groups=parts, tiled=True)  21.9 us
    ppermute x3, waiting for transfers between devices, chan_swap(): return lax.ppermute(values, 'chan', [(c, c ^ bit) for c in range(nc)])  17.5 us
    all_to_all x3, starting transfers between devices, exchange(): lax.all_to_all(blocks, AXES, 0, 0, axis_index_groups=parts, tiled=True)  11.4 us
    pallas_call x1, Pallas kernels, shards(): pl.pallas_call(functools.partial(adam_body, lid, cam, chans, nc, len(smal...  6.81 us
    pallas_call x1, Pallas kernels, shards(): pl.pallas_call(functools.partial(home_body, block), in_specs=[near] * 2,...  5.37 us
  transfers between devices with their start and end apart: 14, of which 8 were waited for; matrix products, arithmetic and copies ran while one was open for 1% of the time, Pallas kernels for 10%

profile of v3, /device:TPU:0, one launch (start us, length us, event | category | flops | bytes accessed | tf_op | source)
XLA Modules:
  0.0 182.4 jit_solution(18443511194936134169)
XLA Ops:
  0.7 2.7 %shard_map.279 = bf16[64,5504]{1,0:T(8,128)(2,1)} custom-call(f32[4,64]{1,0:T(4,128)} %refs_7_.1, f32[3,3,64,256]{3,2,1,0:T(8,128)} %bitcast.32, f32[3,3,64,80]{3,2,1,0:T(8,128)} %bitcast.34, f32[3,3,64,256]{3,2,1,0:T(8,128)} %refs_16_.1), custom_call_target="tpu_custom_call" | custom-call | tf_op jit(solution)/shard_map/pallas_call | solution.py:745
  3.4 3.0 %collective-permute-start = (bf16[1,64,5504]{2,1,0:T(8,128)(2,1)}, bf16[1,64,5504]{2,1,0:T(8,128)(2,1)S(1)}, u32[]{:S(2)}, u32[]{:S(2)}) collective-permute-start(bf16[1,64,5504]{2,1,0:T(8,128)(2,1)} %bitcast.22), channel_id=1, source_target_pairs={{0,2},{1,3},{2,0},{3,1},{4,6},{5,7},{6,4},{7,5},{8,10},{9,11},{10,... | collective-permute-start | bytes 2113544 | tf_op jit(solution)/shard_map/ppermute | solution.py:693
  6.5 0.3 reshape.51.refs_2_
  6.8 0.3 reshape.52.refs_3_
  7.2 4.5 %shard_map.282 = bf16[16,148,256]{2,1,0:T(8,128)(2,1)} custom-call(s32[1,16384]{1,0:T(1,128)S(1)} %bitcast.27, bf16[20,16384]{1,0:T(8,128)(2,1)S(1)} %copy-done.2, bf16[16,64,256]{2,1,0:T(8,128)(2,1)S(1)} %reshape.51.refs_2_, bf16[16,64,256]{2,1,0:T(8,128)(2,1)S(1)} %reshape.52.refs_3_), custom_call_target="tpu_custom_call" | custom-call | tf_op jit(solution)/shard_map/pallas_call | solution.py:43
  11.7 4.0 %all-to-all-start = ((bf16[16,148,256]{2,1,0:T(8,128)(2,1)}), bf16[16,148,256]{2,1,0:T(8,128)(2,1)S(1)}, u32[]{:S(2)}, u32[]{:S(2)}) async-start(bf16[16,148,256]{2,1,0:T(8,128)(2,1)} %shard_map.282), calls=%async_computation | async-start | bytes 2490368 | tf_op jit(solution)/shard_map/all_to_all | solution.py:687
  15.7 17.3 %collective-permute-done.refs_2_ = bf16[1,64,5504]{2,1,0:T(8,128)(2,1)S(1)} collective-permute-done((bf16[1,64,5504]{2,1,0:T(8,128)(2,1)}, bf16[1,64,5504]{2,1,0:T(8,128)(2,1)S(1)}, u32[]{:S(2)}, u32[]{:S(2)}) %collective-permute-start) | collective-permute-done | bytes 704544 | tf_op jit(solution)/shard_map/ppermute | solution.py:693
  33.0 1.2 pad_maximum_fusion
  34.2 0.9 all-to-all-done.refs_0_
  35.2 2.7 %collective-permute-start.2 = (bf16[4,148,128]{2,1,0:T(8,128)(2,1)S(1)}, bf16[4,148,128]{2,1,0:T(8,128)(2,1)S(1)}, u32[]{:S(2)}, u32[]{:S(2)}) collective-permute-start(bf16[4,148,128]{2,1,0:T(8,128)(2,1)S(1)} %slice_select_fusion), channel_id=1, source_target_pairs={{0,16},{1,17},{2,18},{3,19},{4,20},{5,21},{6,22},{7,23},{8,24},{9,... | collective-permute-start | bytes 454664 | tf_op jit(solution)/shard_map/ppermute | solution.py:700
  37.9 0.1 pad_add_fusion.refs_0_.refs_2_
  37.9 1.7 shard_map.280
  39.7 0.8 shard_map.281
  40.5 2.2 %shard_map.283 = (bf16[1024,1280]{1,0:T(8,128)(2,1)S(1)}, bf16[256,1024]{1,0:T(8,128)(2,1)S(1)}, f32[256,1024]{1,0:T(8,128)S(1)}) custom-call(bf16[16,148,256]{2,1,0:T(8,128)(2,1)S(1)} %all-to-all-done.refs_0_, bf16[256,3072]{1,0:T(8,128)(2,1)S(1)} %get-tuple-element.65.refs_0_.refs_1_.refs_6_), custom_call_target="tpu_custom_call" | custom-call | tf_op jit(solution)/shard_map/pallas_call | solution.py:43
  42.7 3.4 %collective-permute-done.2.refs_4_.refs_5_ = bf16[4,148,128]{2,1,0:T(8,128)(2,1)S(1)} collective-permute-done((bf16[4,148,128]{2,1,0:T(8,128)(2,1)S(1)}, bf16[4,148,128]{2,1,0:T(8,128)(2,1)S(1)}, u32[]{:S(2)}, u32[]{:S(2)}) %collective-permute-start.2) | collective-permute-done | bytes 151584 | tf_op jit(solution)/shard_map/ppermute | solution.py:700
  46.0 1.2 shard_map.284
  47.4 13.3 %all_to_all.40.refs_4_ = f32[32,2,256]{2,1,0:T(2,128)S(1)} all-to-all(f32[32,2,256]{2,1,0:T(2,128)S(1)} %get-tuple-element.72), channel_id=1, replica_groups=mesh['strip'=8,'chan'=4] {'strip','chan'}, dimensions={0} | all-to-all | bytes 131072 | tf_op jit(solution)/shard_map/all_to_all | solution.py:690
  60.7 2.9 %shard_map.285 = (f32[256,1024]{1,0:T(8,128)S(1)}, f32[32,2,256]{2,1,0:T(2,128)S(1)}, f32[1,256,128]{2,1,0:T(8,128)S(1)}, f32[256,1024]{1,0:T(8,128)S(1)}, f32[256,128]{1,0:T(8,128)S(1)}) custom-call(s32[2]{0:T(128)S(1)} %pad_add_fusion.refs_0_.refs_2_, f32[256,1024]{1,0:T(8,128)S(1)} %get-tuple-element.70.refs_1_.refs_9_.refs_4_, ...), custom_call_target="tpu_custom_call" | custom-call | tf_op jit(solution)/shard_map/pallas_call | solution.py:43
  63.5 0.7 collective-permute-start.4
  64.3 10.0 %all_to_all.41.refs_4_ = f32[32,2,256]{2,1,0:T(2,128)S(1)} all-to-all(f32[32,2,256]{2,1,0:T(2,128)S(1)} %get-tuple-element.76), channel_id=1, replica_groups=mesh['strip'=8,'chan'=4] {'strip','chan'}, dimensions={0} | all-to-all | bytes 131072 | tf_op jit(solution)/shard_map/all_to_all | solution.py:690
  74.3 1.9 %shard_map.286 = (f32[256,1280]{1,0:T(8,128)S(1)}, f32[32,2,256]{2,1,0:T(2,128)S(1)}, f32[256,128]{1,0:T(8,128)S(1)}, bf16[16,64,256]{2,1,0:T(8,128)(2,1)S(1)}) custom-call(s32[2]{0:T(128)S(1)} %pad_add_fusion.refs_0_.refs_2_, f32[256,1024]{1,0:T(8,128)S(1)} %get-tuple-element.74.refs_1_.refs_2_, ...), custom_call_target="tpu_custom_call" | custom-call | tf_op jit(solution)/shard_map/pallas_call | solution.py:43
  76.2 9.6 %all_to_all.42.refs_6_ = f32[32,2,256]{2,1,0:T(2,128)S(1)} all-to-all(f32[32,2,256]{2,1,0:T(2,128)S(1)} %get-tuple-element.82), channel_id=1, replica_groups=mesh['strip'=8,'chan'=4] {'strip','chan'}, dimensions={0} | all-to-all | bytes 131072 | tf_op jit(solution)/shard_map/all_to_all | solution.py:690
  85.8 3.1 %shard_map.287 = (f32[256,1024]{1,0:T(8,128)S(1)}, f32[32,2,256]{2,1,0:T(2,128)S(1)}, f32[1,256,128]{2,1,0:T(8,128)S(1)}, bf16[768,1280]{1,0:T(8,128)(2,1)S(1)}, f32[2,256]{1,0:T(2,128)S(1)}) custom-call(s32[2]{0:T(128)S(1)} %pad_add_fusion.refs_0_.refs_2_, f32[256,1280]{1,0:T(8,128)S(1)} %get-tuple-element.80.refs_1_, ...), custom_call_target="tpu_custom_call" | custom-call | tf_op jit(solution)/shard_map/pallas_call | solution.py:43
  88.9 0.7 collective-permute-start.5
  89.6 10.0 %all_to_all.43.refs_8_ = f32[32,2,256]{2,1,0:T(2,128)S(1)} all-to-all(f32[32,2,256]{2,1,0:T(2,128)S(1)} %get-tuple-element.86), channel_id=1, replica_groups=mesh['strip'=8,'chan'=4] {'strip','chan'}, dimensions={0} | all-to-all | bytes 131072 | tf_op jit(solution)/shard_map/all_to_all | solution.py:690
  99.7 5.1 %shard_map.288 = (bf16[128,5376]{1,0:T(8,128)(2,1)S(1)}, bf16[128,5376]{1,0:T(8,128)(2,1)S(1)}, bf16[768,1280]{1,0:T(8,128)(2,1)S(1)}, f32[4,256]{1,0:T(4,128)S(1)}, f32[1,1]{1,0:T(1,128)}) custom-call(s32[2]{0:T(128)S(1)} %pad_add_fusion.refs_0_.refs_2_, f32[256,1024]{1,0:T(8,128)S(1)} %get-tuple-element.84.refs_1_, ...), custom_call_target="tpu_custom_call" | custom-call | tf_op jit(solution)/shard_map/pallas_call | solution.py:43
  104.7 0.1 collective-permute-start.6
  104.9 2.8 %shard_map.289.refs_0_ = bf16[16,148,256]{2,1,0:T(8,128)(2,1)} custom-call(bf16[768,1280]{1,0:T(8,128)(2,1)S(1)} %get-tuple-element.91.refs_0_, bf16[336,2304]{1,0:T(8,128)(2,1)S(1)} %get-tuple-element.67.refs_0_.refs_1_, bf16[16,64,256]{2,1,0:T(8,128)(2,1)S(1)} %get-tuple-element.92.refs_2_), custom_call_target="tpu_custom_call" | custom-call | tf_op jit(solution)/shard_map/pallas_call | solution.py:43
  107.7 0.2 collective-permute-done.6.refs_2_
  107.9 0.3 shard_map.291
  108.2 21.9 %all_to_all.44.refs_0_ = bf16[8,16,5376]{2,1,0:T(8,128)(2,1)S(1)} all-to-all(bf16[8,16,5376]{2,1,0:T(8,128)(2,1)S(1)} %bitcast.26), channel_id=1, replica_groups={{0,4,8,12,2,6,10,14},{1,5,9,13,3,7,11,15},{16,20,24,28,18,22,26,30},{17..., dimensions={0} | all-to-all | bytes 2752512 | tf_op jit(solution)/shard_map/all_to_all | solution.py:687
  130.1 3.7 %all-to-all-start.5 = ((bf16[16,148,256]{2,1,0:T(8,128)(2,1)}), bf16[16,148,256]{2,1,0:T(8,128)(2,1)S(1)}, u32[]{:S(2)}, u32[]{:S(2)}) async-start(bf16[16,148,256]{2,1,0:T(8,128)(2,1)} %shard_map.289.refs_0_), calls=%async_computation.5 | async-start | bytes 2490368 | tf_op jit(solution)/shard_map/all_to_all | solution.py:687
  133.8 0.2 shard_map.292.refs_1_
  134.0 1.1 collective-permute-start.7
  135.1 20.8 %all-to-all-done.5.home_ref.refs_0_ = bf16[16,148,256]{2,1,0:T(8,128)(2,1)S(1)} async-done(((bf16[16,148,256]{2,1,0:T(8,128)(2,1)}), bf16[16,148,256]{2,1,0:T(8,128)(2,1)S(1)}, u32[]{:S(2)}, u32[]{:S(2)}) %all-to-all-start.5) | async-done | bytes 1212448 | tf_op jit(solution)/shard_map/all_to_all | solution.py:687
  155.9 1.1 shard_map.293
  157.0 3.7 %all-to-all-start.7 = ((bf16[4,16,5504]{2,1,0:T(8,128)(2,1)}), bf16[4,16,5504]{2,1,0:T(8,128)(2,1)S(1)}, u32[]{:S(2)}, u32[]{:S(2)}) async-start(bf16[4,16,5504]{2,1,0:T(8,128)(2,1)} %shard_map.293), calls=%async_computation.7 | async-start | bytes 1409024 | tf_op jit(solution)/shard_map/all_to_all | solution.py:687
  160.8 5.4 %shard_map.290 = (f32[16,64,2,128]{3,2,1,0:T(2,128)}, f32[16,64,2,128]{3,2,1,0:T(2,128)}, f32[20,16384]{1,0:T(8,128)}, f32[8,128]{1,0:T(8,128)S(1)}) custom-call(s32[1,16384]{1,0:T(1,128)S(1)} %bitcast.28, bf16[16,148,256]{2,1,0:T(8,128)(2,1)S(1)} %all-to-all-done.5.home_ref.refs_0_), custom_call_target="tpu_custom_call" | custom-call | tf_op jit(solution)/shard_map/pallas_call | solution.py:882
  166.1 4.4 %all-to-all-done.7.refs_1_ = bf16[4,16,5504]{2,1,0:T(8,128)(2,1)S(1)} async-done(((bf16[4,16,5504]{2,1,0:T(8,128)(2,1)}), bf16[4,16,5504]{2,1,0:T(8,128)(2,1)S(1)}, u32[]{:S(2)}, u32[]{:S(2)}) %all-to-all-start.7) | async-done | bytes 704544 | tf_op jit(solution)/shard_map/all_to_all | solution.py:687
  170.5 0.1 shard_map.294.refs_0_
  170.7 0.5 collective-permute-start.10
  171.2 0.4 collective-permute-start.9
  171.6 1.0 collective-permute-start.8
  172.6 0.6 constant_dynamic-slice_fusion.refs_6_
  173.3 0.5 collective-permute-done.10.refs_3_
  173.8 1.0 collective-permute-done.9.refs_2_
  174.8 0.6 copy-done.8
  175.4 6.8 %shard_map.295 = (f32[4,64]{1,0:T(4,128)}, f32[4,64]{1,0:T(4,128)}, f32[4,64]{1,0:T(4,128)}, f32[1,1]{1,0:T(1,128)}, f32[3,3,64,80]{3,2,1,0:T(8,128)}, /*index=5...) custom-call(f32[8,128]{1,0:T(8,128)} %copy-done.4, ...), custom_call_target="tpu_custom_call" | custom-call | tf_op jit(solution)/shard_map/pallas_call | solution.py:911
  (28 shorter events, 0.2 us)
Async XLA Ops:
  0.6 5.8 %copy-start.5 = (bf16[16,64,2,128]{3,2,1,0:T(2,128)(2,1)S(1)}, bf16[16,64,2,128]{3,2,1,0:T(2,128)(2,1)}, u32[]{:S(2)}) copy-start(bf16[16,64,2,128]{3,2,1,0:T(2,128)(2,1)} %param.18) | copy-start | bytes 1572868
  0.7 6.1 %copy-start.6 = (bf16[16,64,2,128]{3,2,1,0:T(2,128)(2,1)S(1)}, bf16[16,64,2,128]{3,2,1,0:T(2,128)(2,1)}, u32[]{:S(2)}) copy-start(bf16[16,64,2,128]{3,2,1,0:T(2,128)(2,1)} %param.23) | copy-start | bytes 1572868
  3.4 3.7 %copy-start.2 = (bf16[20,16384]{1,0:T(8,128)(2,1)S(1)}, bf16[20,16384]{1,0:T(8,128)(2,1)}, u32[]{:S(2)}) copy-start(bf16[20,16384]{1,0:T(8,128)(2,1)} %refs_1_.1) | copy-start | bytes 1966084
  3.4 3.7 %copy-start.3 = (s32[16384]{0:T(1024)S(1)}, s32[16384]{0:T(1024)}, u32[]{:S(2)}) copy-start(s32[16384]{0:T(1024)} %param.17) | copy-start | bytes 196612
  3.4 29.5 %collective-permute-start = (bf16[1,64,5504]{2,1,0:T(8,128)(2,1)}, bf16[1,64,5504]{2,1,0:T(8,128)(2,1)S(1)}, u32[]{:S(2)}, u32[]{:S(2)}) collective-permute-start(bf16[1,64,5504]{2,1,0:T(8,128)(2,1)} %bitcast.22), channel_id=1, source_target_pairs={{0,2},{1,3},{2,0},{3,1},{4,6},{5,7},{6,4},{7,5},{8,10},{9,11},{10,... | collective-permute-start | bytes 2113544 | tf_op jit(solution)/shard_map/ppermute | solution.py:693
  11.7 21.3 %copy-start = (bf16[64,5504]{1,0:T(8,128)(2,1)S(1)}, bf16[64,5504]{1,0:T(8,128)(2,1)}, u32[]{:S(2)}) copy-start(bf16[64,5504]{1,0:T(8,128)(2,1)} %shard_map.279) | copy-start | bytes 2113540
  11.7 23.5 %all-to-all-start = ((bf16[16,148,256]{2,1,0:T(8,128)(2,1)}), bf16[16,148,256]{2,1,0:T(8,128)(2,1)S(1)}, u32[]{:S(2)}, u32[]{:S(2)}) async-start(bf16[16,148,256]{2,1,0:T(8,128)(2,1)} %shard_map.282), calls=%async_computation | async-start | bytes 2490368 | tf_op jit(solution)/shard_map/all_to_all | solution.py:687
  34.2 3.7 %collective-permute-start.1 = (bf16[2,64,5504]{2,1,0:T(8,128)(2,1)}, bf16[2,64,5504]{2,1,0:T(8,128)(2,1)}, u32[]{:S(2)}, u32[]{:S(2)}) collective-permute-start(bf16[2,64,5504]{2,1,0:T(8,128)(2,1)} %pad_maximum_fusion), channel_id=1, source_target_pairs={{0,1},{1,0},{2,3},{3,2},{4,5},{5,4},{6,7},{7,6},{8,9},{9,8},{10,11... | collective-permute-start | bytes 4227080 | tf_op jit(solution)/shard_map/ppermute | solution.py:693
  35.2 10.9 %collective-permute-start.2 = (bf16[4,148,128]{2,1,0:T(8,128)(2,1)S(1)}, bf16[4,148,128]{2,1,0:T(8,128)(2,1)S(1)}, u32[]{:S(2)}, u32[]{:S(2)}) collective-permute-start(bf16[4,148,128]{2,1,0:T(8,128)(2,1)S(1)} %slice_select_fusion), channel_id=1, source_target_pairs={{0,16},{1,17},{2,18},{3,19},{4,20},{5,21},{6,22},{7,23},{8,24},{9,... | collective-permute-start | bytes 454664 | tf_op jit(solution)/shard_map/ppermute | solution.py:700
  47.3 13.4 %collective-permute-start.3 = (f32[256,128]{1,0:T(8,128)S(1)}, f32[256,128]{1,0:T(8,128)S(1)}, u32[]{:S(2)}, u32[]{:S(2)}) collective-permute-start(f32[256,128]{1,0:T(8,128)S(1)} %bitcast.30), channel_id=1, source_target_pairs={{0,16},{1,17},{2,18},{3,19},{4,20},{5,21},{6,22},{7,23},{8,24},{9,... | collective-permute-start | bytes 393224 | tf_op jit(solution)/shard_map/ppermute | solution.py:700
  63.5 10.8 %collective-permute-start.4 = (f32[256,128]{1,0:T(8,128)S(1)}, f32[256,128]{1,0:T(8,128)S(1)}, u32[]{:S(2)}, u32[]{:S(2)}) collective-permute-start(f32[256,128]{1,0:T(8,128)S(1)} %bitcast.31), channel_id=1, source_target_pairs={{0,16},{1,17},{2,18},{3,19},{4,20},{5,21},{6,22},{7,23},{8,24},{9,... | collective-permute-start | bytes 393224 | tf_op jit(solution)/shard_map/ppermute | solution.py:700
  88.9 10.8 %collective-permute-start.5 = (f32[256,128]{1,0:T(8,128)S(1)}, f32[256,128]{1,0:T(8,128)S(1)}, u32[]{:S(2)}, u32[]{:S(2)}) collective-permute-start(f32[256,128]{1,0:T(8,128)S(1)} %bitcast.29), channel_id=1, source_target_pairs={{0,16},{1,17},{2,18},{3,19},{4,20},{5,21},{6,22},{7,23},{8,24},{9,... | collective-permute-start | bytes 393224 | tf_op jit(solution)/shard_map/ppermute | solution.py:700
  104.7 3.1 %collective-permute-start.6 = (bf16[128,5376]{1,0:T(8,128)(2,1)S(1)}, bf16[128,5376]{1,0:T(8,128)(2,1)S(1)}, u32[]{:S(2)}, u32[]{:S(2)}) collective-permute-start(bf16[128,5376]{1,0:T(8,128)(2,1)S(1)} %get-tuple-element.98), channel_id=1, source_target_pairs={{0,1},{1,0},{2,3},{3,2},{4,5},{5,4},{6,7},{7,6},{8,9},{9,8},{10,11... | collective-permute-start | bytes 4128776 | tf_op jit(solution)/shard_map/ppermute | solution.py:693
  130.1 25.8 %all-to-all-start.5 = ((bf16[16,148,256]{2,1,0:T(8,128)(2,1)}), bf16[16,148,256]{2,1,0:T(8,128)(2,1)S(1)}, u32[]{:S(2)}, u32[]{:S(2)}) async-start(bf16[16,148,256]{2,1,0:T(8,128)(2,1)} %shard_map.289.refs_0_), calls=%async_computation.5 | async-start | bytes 2490368 | tf_op jit(solution)/shard_map/all_to_all | solution.py:687
  134.0 21.9 %collective-permute-start.7 = (bf16[16,5376]{1,0:T(8,128)(2,1)S(1)}, bf16[16,5376]{1,0:T(8,128)(2,1)S(1)}, u32[]{:S(2)}, u32[]{:S(2)}) collective-permute-start(bf16[16,5376]{1,0:T(8,128)(2,1)S(1)} %shard_map.292.refs_1_), channel_id=1, source_target_pairs={{0,16},{1,17},{2,18},{3,19},{4,20},{5,21},{6,22},{7,23},{8,24},{9,... | collective-permute-start | bytes 516104 | tf_op jit(solution)/shard_map/ppermute | solution.py:874
  157.0 13.5 %all-to-all-start.7 = ((bf16[4,16,5504]{2,1,0:T(8,128)(2,1)}), bf16[4,16,5504]{2,1,0:T(8,128)(2,1)S(1)}, u32[]{:S(2)}, u32[]{:S(2)}) async-start(bf16[4,16,5504]{2,1,0:T(8,128)(2,1)} %shard_map.293), calls=%async_computation.7 | async-start | bytes 1409024 | tf_op jit(solution)/shard_map/all_to_all | solution.py:687
  170.5 4.3 %copy-start.1 = (bf16[4,16,5504]{2,1,0:T(8,128)(2,1)}, bf16[4,16,5504]{2,1,0:T(8,128)(2,1)S(1)}, u32[]{:S(2)}) copy-start(bf16[4,16,5504]{2,1,0:T(8,128)(2,1)S(1)} %all-to-all-done.7.refs_1_) | copy-start | bytes 2113540
  170.7 4.2 %copy-start.4 = (f32[8,128]{1,0:T(8,128)}, f32[8,128]{1,0:T(8,128)S(1)}, u32[]{:S(2)}) copy-start(f32[8,128]{1,0:T(8,128)S(1)} %shard_map.294.refs_0_) | copy-start | bytes 12292
  170.7 3.1 %collective-permute-start.10 = (f32[8,128]{1,0:T(8,128)S(1)}, f32[8,128]{1,0:T(8,128)S(1)}, u32[]{:S(2)}, u32[]{:S(2)}) collective-permute-start(f32[8,128]{1,0:T(8,128)S(1)} %shard_map.294.refs_0_), channel_id=1, source_target_pairs={{0,3},{1,2},{2,1},{3,0},{4,7},{5,6},{6,5},{7,4},{8,11},{9,10},{10,... | collective-permute-start | bytes 12296 | tf_op jit(solution)/shard_map/ppermute | solution.py:905
  171.2 3.6 %collective-permute-start.9 = (f32[8,128]{1,0:T(8,128)S(1)}, f32[8,128]{1,0:T(8,128)S(1)}, u32[]{:S(2)}, u32[]{:S(2)}) collective-permute-start(f32[8,128]{1,0:T(8,128)S(1)} %shard_map.294.refs_0_), channel_id=1, source_target_pairs={{0,2},{1,3},{2,0},{3,1},{4,6},{5,7},{6,4},{7,5},{8,10},{9,11},{10,... | collective-permute-start | bytes 12296 | tf_op jit(solution)/shard_map/ppermute | solution.py:905
  171.6 3.3 %collective-permute-start.8 = (f32[8,128]{1,0:T(8,128)S(1)}, f32[8,128]{1,0:T(8,128)S(1)}, u32[]{:S(2)}, u32[]{:S(2)}) collective-permute-start(f32[8,128]{1,0:T(8,128)S(1)} %shard_map.294.refs_0_), channel_id=1, source_target_pairs={{0,1},{1,0},{2,3},{3,2},{4,5},{5,4},{6,7},{7,6},{8,9},{9,8},{10,11... | collective-permute-start | bytes 12296 | tf_op jit(solution)/shard_map/ppermute | solution.py:905
  173.8 1.1 copy-start.7
  174.8 0.6 copy-start.8
  174.8 0.6 copy-start.9

commit v4 on v3

--- a/solution.py
+++ b/solution.py
@@ -113,6 +113,13 @@
         ],
         axis=0,
     )
+
+
+def split_body(place_ref, got_ref, keep_ref, send_ref):
+    low = place_ref[0] & 1
+    for pair in range(keep_ref.shape[0]):
+        keep_ref[pair] = got_ref[2 * pair + low]
+        send_ref[pair] = got_ref[2 * pair + 1 - low]
 
 
 def pool_body(block, index_ref, feat_ref, lidar_ref, cot_ref, out_ref):
@@ -135,30 +142,33 @@
 
 
 def home_body(
-    block, index_ref, home_ref, lidar_far, mixed_far, cam_far, token_ref,
+    block, place_ref, index_ref, keep_ref, got_ref, lidar_far, mixed_far, cam_far, token_ref,
     lidar_ref, mixed_ref, cam_ref, sems,
 ):
     grids, own, _, _ = lidar_ref.shape
-    cells = home_ref.shape[2]
+    cells = keep_ref.shape[2]
     chans, points = cam_ref.shape
+    low = place_ref[0] & 1
+    blocks = [(ref, pair, 2 * pair + parity) for ref, parity in ((keep_ref, low), (got_ref, 1 - low)) for pair in range(grids // 2)]
     token_ref[...] = jnp.zeros(token_ref.shape, f32)
     copies = []
     for i, (near, far) in enumerate(((lidar_ref, lidar_far), (mixed_ref, mixed_far))):
-        near[...] = home_ref[:, i * own : (i + 1) * own, :].astype(f32).reshape(near.shape)
+        for ref, pair, grid in blocks:
+            near[grid] = ref[pair, i * own : (i + 1) * own, :].astype(f32).reshape(near.shape[1:])
         copies.append(pltpu.make_async_copy(near, far, sems.at[i]))
         copies[-1].start()
     rows = round_up(chans, 8)
-    grad = home_ref[:, 2 * own : 2 * own + chans, :].astype(f32)
-    grad = jnp.concatenate([grad, jnp.zeros((grids, rows - chans, cells), f32)], axis=1)
+    grad = jnp.concatenate([ref[:, 2 * own : 2 * own + chans, :] for ref in (keep_ref, got_ref)], axis=0)
+    grad = jnp.concatenate([grad.astype(f32), jnp.zeros((grids, rows - chans, cells), f32)], axis=1)
     grad = grad.reshape(grids * rows, cells).astype(bf16)
     for start in range(0, points, block):
         at = slice(start, start + block)
         index = index_ref[:, at]
-        high, low = index // cells, index % cells
-        picked = matmul(grad, one_hot(low, cells))
+        high, low_part = index // cells, index % cells
+        picked = matmul(grad, one_hot(low_part, cells))
         total = jnp.zeros((rows, block), f32)
-        for grid in range(grids):
-            total = jnp.where(high == grid, picked[grid * rows : (grid + 1) * rows], total)
+        for i, (_, _, grid) in enumerate(blocks):
+            total = jnp.where(high == grid, picked[i * rows : (i + 1) * rows], total)
         cam_ref[:, at] = total[:chans]
     copies.append(pltpu.make_async_copy(cam_ref, cam_far, sems.at[2]))
     copies[-1].start()
@@ -679,6 +689,11 @@
         for g in range(groups)
         for low in range(2)
     ]
+    core_groups = [
+        [(g * spg + s) * nc + 2 * pair + low for s in range(spg) for pair in range(nc // 2)]
+        for g in range(groups)
+        for low in range(2)
+    ]
     strip_groups = [
         [(g * spg + s) * nc + c for s in range(spg)] for g in range(groups) for c in range(nc)
     ]
@@ -860,7 +875,7 @@
         functools.partial(inputs_back_body, (rows, chans, lid, lid_own, cam_own, spg, nc)),
         struct((members, lid_own + own + cam_own, cells), bf16),
     )(grad_stack_one, kernel_one_t, mixed_blocks)
-    home = exchange(back_blocks, tile_groups)
+    home = exchange(back_blocks, core_groups)
 
     halved = call(add_body, struct(keep.shape, bf16), after=(back_blocks,))(keep, chan_swap(send, 1))
     piece_rows = own // spg
@@ -878,10 +893,13 @@
     )(piece, other)
     merged = exchange(merged, strip_groups)
     own_grads = merged.reshape(own, packed_width)
+    keep_home, send_home = call(
+        split_body, [struct((members // 2, *home.shape[1:]), bf16)] * 2, smem=1
+    )(place, home)
     images = [struct(lidar_bev.shape, f32), struct(cotangent.shape, f32), struct((cam_own, points), f32)]
     grad_lidar, mixed, grad_cam, token = pl.pallas_call(
         functools.partial(home_body, block),
-        in_specs=[near] * 2,
+        in_specs=[pl.BlockSpec(memory_space=pltpu.SMEM)] + [near] * 3,
         out_specs=[far] * 3 + [near],
         out_shape=[*images, struct((8, LANES), f32)],
         scratch_shapes=[
@@ -889,7 +907,7 @@
             pltpu.SemaphoreType.DMA((3,)),
         ],
         compiler_params=pltpu.CompilerParams(vmem_limit_bytes=VMEM_BYTES),
-    )(index_row, home)
+    )(place, index_row, keep_home, chan_swap(send_home, 1))
     tall = lambda array: array.transpose(turn)
     state = [
         *(tall(array) for array in (w_cam, m_cam, v_cam)),

time: 183 us -> 179 us (0.978)
  waiting for transfers between devices: 48.6 us -> 43.4 us
    all_to_all x3, waiting for transfers between devices: 26.2 us -> 18.6 us  [exchange(): lax.all_to_all(blocks, AXES, 0, 0, axis_index_groups=parts, tiled=True)]
    ppermute x3 -> x4, waiting for transfers between devices: 17.5 us -> 19.5 us  [chan_swap(): return lax.ppermute(values, 'chan', [(c, c ^ bit) for c in range(nc)])]
    pallas_call x14 -> x15, Pallas kernels: 27.9 us -> 28.5 us  [run(): pl.pallas_call(lambda *refs: body(*refs[waits:]), out_shape=out_shape, in...]
  transfers between devices with their start and end apart: 14 -> 15, of which waited for: 8 -> 9; matrix products, arithmetic and copies ran while one was open for 1% -> 2% of each run, Pallas kernels for 10% -> 10%
where the time goes in v4:
time: 179 us
  blocking collectives  64.9 us (36%)
  Pallas kernels  43.8 us (24%)
  waiting for transfers between devices  43.4 us (24%)
  starting transfers between devices  21.7 us (12%)
  local copies, waits for them, and re-layouts  2.17 us (1%)
    all_to_all x4, blocking collectives, everywhere(): return lax.all_to_all(copies, AXES, 0, 0, tiled=True)  43 us
    pallas_call x15, Pallas kernels, run(): pl.pallas_call(lambda *refs: body(*refs[waits:]), out_shape=out_shape, in...  28.5 us
    all_to_all x1, blocking collectives, exchange(): lax.all_to_all(blocks, AXES, 0, 0, axis_index_groups=parts, tiled=True)  21.9 us
    ppermute x4, waiting for transfers between devices, chan_swap(): return lax.ppermute(values, 'chan', [(c, c ^ bit) for c in range(nc)])  19.5 us
    all_to_all x3, waiting for transfers between devices, exchange(): lax.all_to_all(blocks, AXES, 0, 0, axis_index_groups=parts, tiled=True)  18.6 us
    all_to_all x3, starting transfers between devices, exchange(): lax.all_to_all(blocks, AXES, 0, 0, axis_index_groups=parts, tiled=True)  11.3 us
    pallas_call x1, Pallas kernels, shards(): pl.pallas_call(functools.partial(adam_body, lid, cam, chans, nc, len(smal...  6.85 us
    pallas_call x1, Pallas kernels, shards(): pl.pallas_call(functools.partial(home_body, block), in_specs=[pl.BlockSpe...  5.77 us
  transfers between devices with their start and end apart: 15, of which 9 were waited for; matrix products, arithmetic and copies ran while one was open for 2% of the time, Pallas kernels for 10%

profile of v4, /device:TPU:0, one launch (start us, length us, event | category | flops | bytes accessed | tf_op | source)
XLA Modules:
  0.0 178.5 jit_solution(17183980964699481825)
XLA Ops:
  0.7 2.7 %shard_map.279 = bf16[64,5504]{1,0:T(8,128)(2,1)} custom-call(f32[4,64]{1,0:T(4,128)} %refs_7_.1, f32[3,3,64,256]{3,2,1,0:T(8,128)} %bitcast.32, f32[3,3,64,80]{3,2,1,0:T(8,128)} %bitcast.34, f32[3,3,64,256]{3,2,1,0:T(8,128)} %refs_16_.1), custom_call_target="tpu_custom_call" | custom-call | tf_op jit(solution)/shard_map/pallas_call | solution.py:760
  3.4 3.0 %collective-permute-start = (bf16[1,64,5504]{2,1,0:T(8,128)(2,1)}, bf16[1,64,5504]{2,1,0:T(8,128)(2,1)S(1)}, u32[]{:S(2)}, u32[]{:S(2)}) collective-permute-start(bf16[1,64,5504]{2,1,0:T(8,128)(2,1)} %bitcast.22), channel_id=1, source_target_pairs={{0,2},{1,3},{2,0},{3,1},{4,6},{5,7},{6,4},{7,5},{8,10},{9,11},{10,... | collective-permute-start | bytes 2113544 | tf_op jit(solution)/shard_map/ppermute | solution.py:708
  6.5 0.3 reshape.51.refs_2_
  6.8 0.3 reshape.52.refs_3_
  7.2 4.5 %shard_map.282 = bf16[16,148,256]{2,1,0:T(8,128)(2,1)} custom-call(s32[1,16384]{1,0:T(1,128)S(1)} %bitcast.27, bf16[20,16384]{1,0:T(8,128)(2,1)S(1)} %copy-done.2, bf16[16,64,256]{2,1,0:T(8,128)(2,1)S(1)} %reshape.51.refs_2_, bf16[16,64,256]{2,1,0:T(8,128)(2,1)S(1)} %reshape.52.refs_3_), custom_call_target="tpu_custom_call" | custom-call | tf_op jit(solution)/shard_map/pallas_call | solution.py:43
  11.7 4.0 %all-to-all-start = ((bf16[16,148,256]{2,1,0:T(8,128)(2,1)}), bf16[16,148,256]{2,1,0:T(8,128)(2,1)S(1)}, u32[]{:S(2)}, u32[]{:S(2)}) async-start(bf16[16,148,256]{2,1,0:T(8,128)(2,1)} %shard_map.282), calls=%async_computation | async-start | bytes 2490368 | tf_op jit(solution)/shard_map/all_to_all | solution.py:702
  15.7 17.3 %collective-permute-done.refs_2_ = bf16[1,64,5504]{2,1,0:T(8,128)(2,1)S(1)} collective-permute-done((bf16[1,64,5504]{2,1,0:T(8,128)(2,1)}, bf16[1,64,5504]{2,1,0:T(8,128)(2,1)S(1)}, u32[]{:S(2)}, u32[]{:S(2)}) %collective-permute-start) | collective-permute-done | bytes 704544 | tf_op jit(solution)/shard_map/ppermute | solution.py:708
  33.0 1.2 pad_maximum_fusion
  34.2 0.9 all-to-all-done.refs_0_
  35.2 2.7 %collective-permute-start.2 = (bf16[4,148,128]{2,1,0:T(8,128)(2,1)S(1)}, bf16[4,148,128]{2,1,0:T(8,128)(2,1)S(1)}, u32[]{:S(2)}, u32[]{:S(2)}) collective-permute-start(bf16[4,148,128]{2,1,0:T(8,128)(2,1)S(1)} %slice_select_fusion), channel_id=1, source_target_pairs={{0,16},{1,17},{2,18},{3,19},{4,20},{5,21},{6,22},{7,23},{8,24},{9,... | collective-permute-start | bytes 454664 | tf_op jit(solution)/shard_map/ppermute | solution.py:715
  37.9 1.7 shard_map.280
  39.7 0.8 shard_map.281
  40.5 2.2 %shard_map.283 = (bf16[1024,1280]{1,0:T(8,128)(2,1)S(1)}, bf16[256,1024]{1,0:T(8,128)(2,1)S(1)}, f32[256,1024]{1,0:T(8,128)S(1)}) custom-call(bf16[16,148,256]{2,1,0:T(8,128)(2,1)S(1)} %all-to-all-done.refs_0_, bf16[256,3072]{1,0:T(8,128)(2,1)S(1)} %get-tuple-element.67.refs_0_.refs_1_.refs_6_), custom_call_target="tpu_custom_call" | custom-call | tf_op jit(solution)/shard_map/pallas_call | solution.py:43
  42.7 3.4 %collective-permute-done.2.refs_4_.refs_5_ = bf16[4,148,128]{2,1,0:T(8,128)(2,1)S(1)} collective-permute-done((bf16[4,148,128]{2,1,0:T(8,128)(2,1)S(1)}, bf16[4,148,128]{2,1,0:T(8,128)(2,1)S(1)}, u32[]{:S(2)}, u32[]{:S(2)}) %collective-permute-start.2) | collective-permute-done | bytes 151584 | tf_op jit(solution)/shard_map/ppermute | solution.py:715
  46.0 1.2 shard_map.284
  47.4 13.3 %all_to_all.40.refs_4_ = f32[32,2,256]{2,1,0:T(2,128)S(1)} all-to-all(f32[32,2,256]{2,1,0:T(2,128)S(1)} %get-tuple-element.74), channel_id=1, replica_groups=mesh['strip'=8,'chan'=4] {'strip','chan'}, dimensions={0} | all-to-all | bytes 131072 | tf_op jit(solution)/shard_map/all_to_all | solution.py:705
  60.7 2.9 %shard_map.285 = (f32[256,1024]{1,0:T(8,128)S(1)}, f32[32,2,256]{2,1,0:T(2,128)S(1)}, f32[1,256,128]{2,1,0:T(8,128)S(1)}, f32[256,1024]{1,0:T(8,128)S(1)}, f32[256,128]{1,0:T(8,128)S(1)}) custom-call(s32[2]{0:T(128)S(1)} %pad_add_fusion.refs_0_.refs_2_.place_ref, f32[256,1024]{1,0:T(8,128)S(1)} %get-tuple-element.72.refs_1_.refs_9_.refs_4_, ...), custom_call_target="tpu_custom_call" | custom-call | tf_op jit(solution)/shard_map/pallas_call | solution.py:43
  63.5 0.7 collective-permute-start.4
  64.3 10.0 %all_to_all.41.refs_4_ = f32[32,2,256]{2,1,0:T(2,128)S(1)} all-to-all(f32[32,2,256]{2,1,0:T(2,128)S(1)} %get-tuple-element.78), channel_id=1, replica_groups=mesh['strip'=8,'chan'=4] {'strip','chan'}, dimensions={0} | all-to-all | bytes 131072 | tf_op jit(solution)/shard_map/all_to_all | solution.py:705
  74.3 1.9 %shard_map.286 = (f32[256,1280]{1,0:T(8,128)S(1)}, f32[32,2,256]{2,1,0:T(2,128)S(1)}, f32[256,128]{1,0:T(8,128)S(1)}, bf16[16,64,256]{2,1,0:T(8,128)(2,1)S(1)}) custom-call(s32[2]{0:T(128)S(1)} %pad_add_fusion.refs_0_.refs_2_.place_ref, f32[256,1024]{1,0:T(8,128)S(1)} %get-tuple-element.76.refs_1_.refs_2_, ...), custom_call_target="tpu_custom_call" | custom-call | tf_op jit(solution)/shard_map/pallas_call | solution.py:43
  76.2 9.6 %all_to_all.42.refs_6_ = f32[32,2,256]{2,1,0:T(2,128)S(1)} all-to-all(f32[32,2,256]{2,1,0:T(2,128)S(1)} %get-tuple-element.84), channel_id=1, replica_groups=mesh['strip'=8,'chan'=4] {'strip','chan'}, dimensions={0} | all-to-all | bytes 131072 | tf_op jit(solution)/shard_map/all_to_all | solution.py:705
  85.8 3.1 %shard_map.287 = (f32[256,1024]{1,0:T(8,128)S(1)}, f32[32,2,256]{2,1,0:T(2,128)S(1)}, f32[1,256,128]{2,1,0:T(8,128)S(1)}, bf16[768,1280]{1,0:T(8,128)(2,1)S(1)}, f32[2,256]{1,0:T(2,128)S(1)}) custom-call(s32[2]{0:T(128)S(1)} %pad_add_fusion.refs_0_.refs_2_.place_ref, f32[256,1280]{1,0:T(8,128)S(1)} %get-tuple-element.82.refs_1_, ...), custom_call_target="tpu_custom_call" | custom-call | tf_op jit(solution)/shard_map/pallas_call | solution.py:43
  88.9 0.7 collective-permute-start.5
  89.6 10.0 %all_to_all.43.refs_8_ = f32[32,2,256]{2,1,0:T(2,128)S(1)} all-to-all(f32[32,2,256]{2,1,0:T(2,128)S(1)} %get-tuple-element.88), channel_id=1, replica_groups=mesh['strip'=8,'chan'=4] {'strip','chan'}, dimensions={0} | all-to-all | bytes 131072 | tf_op jit(solution)/shard_map/all_to_all | solution.py:705
  99.7 5.1 %shard_map.288 = (bf16[128,5376]{1,0:T(8,128)(2,1)S(1)}, bf16[128,5376]{1,0:T(8,128)(2,1)S(1)}, bf16[768,1280]{1,0:T(8,128)(2,1)S(1)}, f32[4,256]{1,0:T(4,128)S(1)}, f32[1,1]{1,0:T(1,128)}) custom-call(s32[2]{0:T(128)S(1)} %pad_add_fusion.refs_0_.refs_2_.place_ref, f32[256,1024]{1,0:T(8,128)S(1)} %get-tuple-element.86.refs_1_, ...), custom_call_target="tpu_custom_call" | custom-call | tf_op jit(solution)/shard_map/pallas_call | solution.py:43
  104.9 2.8 %shard_map.289.refs_0_ = bf16[16,148,256]{2,1,0:T(8,128)(2,1)} custom-call(bf16[768,1280]{1,0:T(8,128)(2,1)S(1)} %get-tuple-element.93.refs_0_, bf16[336,2304]{1,0:T(8,128)(2,1)S(1)} %get-tuple-element.69.refs_0_.refs_1_, bf16[16,64,256]{2,1,0:T(8,128)(2,1)S(1)} %get-tuple-element.94.refs_2_), custom_call_target="tpu_custom_call" | custom-call | tf_op jit(solution)/shard_map/pallas_call | solution.py:43
  107.7 0.2 collective-permute-done.7.refs_2_
  107.9 0.3 shard_map.292
  108.2 21.9 %all_to_all.44.refs_0_ = bf16[8,16,5376]{2,1,0:T(8,128)(2,1)S(1)} all-to-all(bf16[8,16,5376]{2,1,0:T(8,128)(2,1)S(1)} %bitcast.26), channel_id=1, replica_groups={{0,4,8,12,2,6,10,14},{1,5,9,13,3,7,11,15},{16,20,24,28,18,22,26,30},{17..., dimensions={0} | all-to-all | bytes 2752512 | tf_op jit(solution)/shard_map/all_to_all | solution.py:702
  130.1 3.6 %all-to-all-start.5 = ((bf16[16,148,256]{2,1,0:T(8,128)(2,1)}), bf16[16,148,256]{2,1,0:T(8,128)(2,1)S(1)}, u32[]{:S(2)}, u32[]{:S(2)}) async-start(bf16[16,148,256]{2,1,0:T(8,128)(2,1)} %shard_map.289.refs_0_), calls=%async_computation.5 | async-start | bytes 2490368 | tf_op jit(solution)/shard_map/all_to_all | solution.py:702
  133.7 0.2 shard_map.293.refs_1_
  133.9 1.1 collective-permute-start.8
  135.0 17.3 %all-to-all-done.5.refs_1_.refs_0_ = bf16[16,148,256]{2,1,0:T(8,128)(2,1)S(1)} async-done(((bf16[16,148,256]{2,1,0:T(8,128)(2,1)}), bf16[16,148,256]{2,1,0:T(8,128)(2,1)S(1)}, u32[]{:S(2)}, u32[]{:S(2)}) %all-to-all-start.5) | async-done | bytes 1212448 | tf_op jit(solution)/shard_map/all_to_all | solution.py:702
  152.3 1.1 shard_map.294
  153.4 3.7 %all-to-all-start.7 = ((bf16[4,16,5504]{2,1,0:T(8,128)(2,1)}), bf16[4,16,5504]{2,1,0:T(8,128)(2,1)S(1)}, u32[]{:S(2)}, u32[]{:S(2)}) async-start(bf16[4,16,5504]{2,1,0:T(8,128)(2,1)} %shard_map.294), calls=%async_computation.7 | async-start | bytes 1409024 | tf_op jit(solution)/shard_map/all_to_all | solution.py:702
  157.1 0.6 shard_map.290
  158.0 2.0 %collective-permute-done.6 = bf16[8,148,256]{2,0,1:T(8,128)(2,1)S(1)} collective-permute-done((bf16[8,148,256]{2,0,1:T(8,128)(2,1)S(1)}, bf16[8,148,256]{2,0,1:T(8,128)(2,1)S(1)}, u32[]{:S(2)}, u32[]{:S(2)}) %collective-permute-start.6) | collective-permute-done | bytes 606240 | tf_op jit(solution)/shard_map/ppermute | solution.py:708
  160.1 5.8 %shard_map.291 = (f32[16,64,2,128]{3,2,1,0:T(2,128)}, f32[16,64,2,128]{3,2,1,0:T(2,128)}, f32[20,16384]{1,0:T(8,128)}, f32[8,128]{1,0:T(8,128)S(1)}) custom-call(s32[2]{0:T(128)S(1)} %pad_add_fusion.refs_0_.refs_2_.place_ref, s32[1,16384]{1,0:T(1,128)S(1)} %bitcast.28, bf16[8,148,256]{2,1,0:T(8,128)(2,1)S(1)} %get-tuple-element.95.keep_ref, ...), custom_call_target="tpu_custom_call" | custom-call | tf_op jit(solution)/shard_map/pallas_call | solution.py:900
  165.9 0.4 all-to-all-done.7.refs_1_
  166.2 0.1 shard_map.295.refs_0_
  166.4 0.9 collective-permute-start.11
  167.3 0.6 collective-permute-start.10
  167.9 0.4 collective-permute-start.9
  168.3 0.7 constant_dynamic-slice_fusion.refs_6_
  169.0 0.5 collective-permute-done.11.refs_3_
  169.5 1.4 collective-permute-done.10.refs_2_
  170.9 0.6 copy-done.8
  171.5 6.8 %shard_map.296 = (f32[4,64]{1,0:T(4,128)}, f32[4,64]{1,0:T(4,128)}, f32[4,64]{1,0:T(4,128)}, f32[1,1]{1,0:T(1,128)}, f32[3,3,64,80]{3,2,1,0:T(8,128)}, /*index=5...) custom-call(f32[8,128]{1,0:T(8,128)} %copy-done.4, ...), custom_call_target="tpu_custom_call" | custom-call | tf_op jit(solution)/shard_map/pallas_call | solution.py:929
  (33 shorter events, 0.7 us)
Async XLA Ops:
  0.6 5.8 %copy-start.5 = (bf16[16,64,2,128]{3,2,1,0:T(2,128)(2,1)S(1)}, bf16[16,64,2,128]{3,2,1,0:T(2,128)(2,1)}, u32[]{:S(2)}) copy-start(bf16[16,64,2,128]{3,2,1,0:T(2,128)(2,1)} %param.18) | copy-start | bytes 1572868
  0.7 6.1 %copy-start.6 = (bf16[16,64,2,128]{3,2,1,0:T(2,128)(2,1)S(1)}, bf16[16,64,2,128]{3,2,1,0:T(2,128)(2,1)}, u32[]{:S(2)}) copy-start(bf16[16,64,2,128]{3,2,1,0:T(2,128)(2,1)} %param.23) | copy-start | bytes 1572868
  3.4 3.7 %copy-start.2 = (bf16[20,16384]{1,0:T(8,128)(2,1)S(1)}, bf16[20,16384]{1,0:T(8,128)(2,1)}, u32[]{:S(2)}) copy-start(bf16[20,16384]{1,0:T(8,128)(2,1)} %refs_1_.1) | copy-start | bytes 1966084
  3.4 3.7 %copy-start.3 = (s32[16384]{0:T(1024)S(1)}, s32[16384]{0:T(1024)}, u32[]{:S(2)}) copy-start(s32[16384]{0:T(1024)} %param.17) | copy-start | bytes 196612
  3.4 29.5 %collective-permute-start = (bf16[1,64,5504]{2,1,0:T(8,128)(2,1)}, bf16[1,64,5504]{2,1,0:T(8,128)(2,1)S(1)}, u32[]{:S(2)}, u32[]{:S(2)}) collective-permute-start(bf16[1,64,5504]{2,1,0:T(8,128)(2,1)} %bitcast.22), channel_id=1, source_target_pairs={{0,2},{1,3},{2,0},{3,1},{4,6},{5,7},{6,4},{7,5},{8,10},{9,11},{10,... | collective-permute-start | bytes 2113544 | tf_op jit(solution)/shard_map/ppermute | solution.py:708
  11.7 21.3 %copy-start = (bf16[64,5504]{1,0:T(8,128)(2,1)S(1)}, bf16[64,5504]{1,0:T(8,128)(2,1)}, u32[]{:S(2)}) copy-start(bf16[64,5504]{1,0:T(8,128)(2,1)} %shard_map.279) | copy-start | bytes 2113540
  11.7 23.5 %all-to-all-start = ((bf16[16,148,256]{2,1,0:T(8,128)(2,1)}), bf16[16,148,256]{2,1,0:T(8,128)(2,1)S(1)}, u32[]{:S(2)}, u32[]{:S(2)}) async-start(bf16[16,148,256]{2,1,0:T(8,128)(2,1)} %shard_map.282), calls=%async_computation | async-start | bytes 2490368 | tf_op jit(solution)/shard_map/all_to_all | solution.py:702
  34.2 3.7 %collective-permute-start.1 = (bf16[2,64,5504]{2,1,0:T(8,128)(2,1)}, bf16[2,64,5504]{2,1,0:T(8,128)(2,1)}, u32[]{:S(2)}, u32[]{:S(2)}) collective-permute-start(bf16[2,64,5504]{2,1,0:T(8,128)(2,1)} %pad_maximum_fusion), channel_id=1, source_target_pairs={{0,1},{1,0},{2,3},{3,2},{4,5},{5,4},{6,7},{7,6},{8,9},{9,8},{10,11... | collective-permute-start | bytes 4227080 | tf_op jit(solution)/shard_map/ppermute | solution.py:708
  35.2 10.9 %collective-permute-start.2 = (bf16[4,148,128]{2,1,0:T(8,128)(2,1)S(1)}, bf16[4,148,128]{2,1,0:T(8,128)(2,1)S(1)}, u32[]{:S(2)}, u32[]{:S(2)}) collective-permute-start(bf16[4,148,128]{2,1,0:T(8,128)(2,1)S(1)} %slice_select_fusion), channel_id=1, source_target_pairs={{0,16},{1,17},{2,18},{3,19},{4,20},{5,21},{6,22},{7,23},{8,24},{9,... | collective-permute-start | bytes 454664 | tf_op jit(solution)/shard_map/ppermute | solution.py:715
  47.3 13.4 %collective-permute-start.3 = (f32[256,128]{1,0:T(8,128)S(1)}, f32[256,128]{1,0:T(8,128)S(1)}, u32[]{:S(2)}, u32[]{:S(2)}) collective-permute-start(f32[256,128]{1,0:T(8,128)S(1)} %bitcast.30), channel_id=1, source_target_pairs={{0,16},{1,17},{2,18},{3,19},{4,20},{5,21},{6,22},{7,23},{8,24},{9,... | collective-permute-start | bytes 393224 | tf_op jit(solution)/shard_map/ppermute | solution.py:715
  63.5 10.8 %collective-permute-start.4 = (f32[256,128]{1,0:T(8,128)S(1)}, f32[256,128]{1,0:T(8,128)S(1)}, u32[]{:S(2)}, u32[]{:S(2)}) collective-permute-start(f32[256,128]{1,0:T(8,128)S(1)} %bitcast.31), channel_id=1, source_target_pairs={{0,16},{1,17},{2,18},{3,19},{4,20},{5,21},{6,22},{7,23},{8,24},{9,... | collective-permute-start | bytes 393224 | tf_op jit(solution)/shard_map/ppermute | solution.py:715
  88.9 10.8 %collective-permute-start.5 = (f32[256,128]{1,0:T(8,128)S(1)}, f32[256,128]{1,0:T(8,128)S(1)}, u32[]{:S(2)}, u32[]{:S(2)}) collective-permute-start(f32[256,128]{1,0:T(8,128)S(1)} %bitcast.29), channel_id=1, source_target_pairs={{0,16},{1,17},{2,18},{3,19},{4,20},{5,21},{6,22},{7,23},{8,24},{9,... | collective-permute-start | bytes 393224 | tf_op jit(solution)/shard_map/ppermute | solution.py:715
  104.7 3.1 %collective-permute-start.7 = (bf16[128,5376]{1,0:T(8,128)(2,1)S(1)}, bf16[128,5376]{1,0:T(8,128)(2,1)S(1)}, u32[]{:S(2)}, u32[]{:S(2)}) collective-permute-start(bf16[128,5376]{1,0:T(8,128)(2,1)S(1)} %get-tuple-element.102), channel_id=1, source_target_pairs={{0,1},{1,0},{2,3},{3,2},{4,5},{5,4},{6,7},{7,6},{8,9},{9,8},{10,11... | collective-permute-start | bytes 4128776 | tf_op jit(solution)/shard_map/ppermute | solution.py:708
  130.1 22.2 %all-to-all-start.5 = ((bf16[16,148,256]{2,1,0:T(8,128)(2,1)}), bf16[16,148,256]{2,1,0:T(8,128)(2,1)S(1)}, u32[]{:S(2)}, u32[]{:S(2)}) async-start(bf16[16,148,256]{2,1,0:T(8,128)(2,1)} %shard_map.289.refs_0_), calls=%async_computation.5 | async-start | bytes 2490368 | tf_op jit(solution)/shard_map/all_to_all | solution.py:702
  133.9 18.4 %collective-permute-start.8 = (bf16[16,5376]{1,0:T(8,128)(2,1)S(1)}, bf16[16,5376]{1,0:T(8,128)(2,1)S(1)}, u32[]{:S(2)}, u32[]{:S(2)}) collective-permute-start(bf16[16,5376]{1,0:T(8,128)(2,1)S(1)} %shard_map.293.refs_1_), channel_id=1, source_target_pairs={{0,16},{1,17},{2,18},{3,19},{4,20},{5,21},{6,22},{7,23},{8,24},{9,... | collective-permute-start | bytes 516104 | tf_op jit(solution)/shard_map/ppermute | solution.py:889
  153.4 12.8 %all-to-all-start.7 = ((bf16[4,16,5504]{2,1,0:T(8,128)(2,1)}), bf16[4,16,5504]{2,1,0:T(8,128)(2,1)S(1)}, u32[]{:S(2)}, u32[]{:S(2)}) async-start(bf16[4,16,5504]{2,1,0:T(8,128)(2,1)} %shard_map.294), calls=%async_computation.7 | async-start | bytes 1409024 | tf_op jit(solution)/shard_map/all_to_all | solution.py:702
  157.9 2.1 %collective-permute-start.6 = (bf16[8,148,256]{2,0,1:T(8,128)(2,1)S(1)}, bf16[8,148,256]{2,0,1:T(8,128)(2,1)S(1)}, u32[]{:S(2)}, u32[]{:S(2)}) collective-permute-start(bf16[8,148,256]{2,0,1:T(8,128)(2,1)S(1)} %copy.32), channel_id=1, source_target_pairs={{0,1},{1,0},{2,3},{3,2},{4,5},{5,4},{6,7},{7,6},{8,9},{9,8},{10,11... | collective-permute-start | bytes 1818632 | tf_op jit(solution)/shard_map/ppermute | solution.py:708
  166.2 4.7 %copy-start.1 = (bf16[4,16,5504]{2,1,0:T(8,128)(2,1)}, bf16[4,16,5504]{2,1,0:T(8,128)(2,1)S(1)}, u32[]{:S(2)}) copy-start(bf16[4,16,5504]{2,1,0:T(8,128)(2,1)S(1)} %all-to-all-done.7.refs_1_) | copy-start | bytes 2113540
  166.4 4.5 %copy-start.4 = (f32[8,128]{1,0:T(8,128)}, f32[8,128]{1,0:T(8,128)S(1)}, u32[]{:S(2)}) copy-start(f32[8,128]{1,0:T(8,128)S(1)} %shard_map.295.refs_0_) | copy-start | bytes 12292
  166.4 3.1 %collective-permute-start.11 = (f32[8,128]{1,0:T(8,128)S(1)}, f32[8,128]{1,0:T(8,128)S(1)}, u32[]{:S(2)}, u32[]{:S(2)}) collective-permute-start(f32[8,128]{1,0:T(8,128)S(1)} %shard_map.295.refs_0_), channel_id=1, source_target_pairs={{0,3},{1,2},{2,1},{3,0},{4,7},{5,6},{6,5},{7,4},{8,11},{9,10},{10,... | collective-permute-start | bytes 12296 | tf_op jit(solution)/shard_map/ppermute | solution.py:923
  167.3 3.6 %collective-permute-start.10 = (f32[8,128]{1,0:T(8,128)S(1)}, f32[8,128]{1,0:T(8,128)S(1)}, u32[]{:S(2)}, u32[]{:S(2)}) collective-permute-start(f32[8,128]{1,0:T(8,128)S(1)} %shard_map.295.refs_0_), channel_id=1, source_target_pairs={{0,2},{1,3},{2,0},{3,1},{4,6},{5,7},{6,4},{7,5},{8,10},{9,11},{10,... | collective-permute-start | bytes 12296 | tf_op jit(solution)/shard_map/ppermute | solution.py:923
  167.9 3.0 %collective-permute-start.9 = (f32[8,128]{1,0:T(8,128)S(1)}, f32[8,128]{1,0:T(8,128)S(1)}, u32[]{:S(2)}, u32[]{:S(2)}) collective-permute-start(f32[8,128]{1,0:T(8,128)S(1)} %shard_map.295.refs_0_), channel_id=1, source_target_pairs={{0,1},{1,0},{2,3},{3,2},{4,5},{5,4},{6,7},{7,6},{8,9},{9,8},{10,11... | collective-permute-start | bytes 12296 | tf_op jit(solution)/shard_map/ppermute | solution.py:923
  169.5 1.4 copy-start.7
  170.9 0.6 copy-start.8
  170.9 0.6 copy-start.9

commit v5 on v4

--- a/solution.py
+++ b/solution.py
@@ -90,7 +90,7 @@
 
 
 def sigmoid(values):
-    return 1.0 / (1.0 + jnp.exp(-values))
+    return 0.5 + 0.5 * jnp.tanh(0.5 * values)
 
 
 def moments(received, pixel_count):
@@ -508,14 +508,14 @@
     )
     hidden = halves(place_ref, own, nc, lambda start: hidden_ref[pl.ds(start, own), :]).astype(bf16)
     for a in range(3):
-        grad = matmul_nt(ordered, cells_ref[:, a * LANES : (a + rows) * LANES]).astype(bf16)
+        grad = matmul_nt(ordered, cells_ref[:, a * LANES : (a + rows) * LANES])
         to = slice(a * one_width, (a + 1) * one_width)
         keep_ref[:, to] = grad[:half]
-        send_ref[:, to] = grad[half:]
-        grad = matmul_nt(hidden, stack_two_ref[:, (2 - a) * LANES : (2 - a + rows) * LANES]).astype(bf16)
+        send_ref[:, to] = grad[half:].astype(bf16)
+        grad = matmul_nt(hidden, stack_two_ref[:, (2 - a) * LANES : (2 - a + rows) * LANES])
         start = 3 * one_width + a * 3 * chans
         keep_ref[:, start : start + 3 * chans] = grad[:half]
-        send_ref[:, start : start + 3 * chans] = grad[half:]
+        send_ref[:, start : start + 3 * chans] = grad[half:].astype(bf16)
 
 
 def inputs_back_body(cfg, stack_ref, kernel_ref, mixed_ref, back_ref):
@@ -550,7 +550,7 @@
 
 
 def add_body(mine_ref, other_ref, out_ref):
-    out_ref[...] = (mine_ref[...].astype(f32) + other_ref[...].astype(f32)).astype(bf16)
+    out_ref[...] = (mine_ref[...] + other_ref[...].astype(f32)).astype(bf16)
 
 
 def sum_body(pieces_ref, out_ref):
@@ -859,7 +859,7 @@
             first_back_body, (rows, chans, own, nc, one_width, groups, pixel_count)
         ),
         [
-            struct((chans // 2, total_width), bf16),
+            struct((chans // 2, total_width), f32),
             struct((chans // 2, total_width), bf16),
             struct((two_width, wide), bf16),
             struct((4, chans), f32),
@@ -889,8 +889,9 @@
         other = lax.ppermute(piece, AXES, [(i, i ^ shift) for i in range(devices)])
         shift *= 2
     merged = call(
-        functools.partial(merge_body, spg), struct((spg, piece_rows, packed_width), bf16), after=(home,)
+        functools.partial(merge_body, spg), struct((spg, piece_rows, packed_width), bf16)
     )(piece, other)
+    merged, home = lax.optimization_barrier((merged, home))
     merged = exchange(merged, strip_groups)
     own_grads = merged.reshape(own, packed_width)
     keep_home, send_home = call(

time: 179 us -> 178 us (level)
    all_to_all x3, waiting for transfers between devices: 18.6 us -> 2.05 us  [exchange(): lax.all_to_all(blocks, AXES, 0, 0, axis_index_groups=parts, tiled=True)]
    ppermute x1, waiting for transfers between devices: 0.01 us -> 15.1 us  [shards(): other = lax.ppermute(piece, AXES, [(i, i ^ shift) for i in range(devices)])]
  transfers between devices with their start and end apart: 15 -> 15, of which waited for: 9 -> 9; matrix products, arithmetic and copies ran while one was open for 2% -> 2% of each run, Pallas kernels for 10% -> 11%
where the time goes in v5:
time: 178 us
  blocking collectives  65 us (37%)
  Pallas kernels  43.7 us (25%)
  waiting for transfers between devices  42.3 us (24%)
  starting transfers between devices  22.4 us (13%)
  local copies, waits for them, and re-layouts  2.17 us (1%)
    all_to_all x4, blocking collectives, everywhere(): return lax.all_to_all(copies, AXES, 0, 0, tiled=True)  43 us
    pallas_call x15, Pallas kernels, run(): pl.pallas_call(lambda *refs: body(*refs[waits:]), out_shape=out_shape, in...  28.3 us
    all_to_all x1, blocking collectives, exchange(): lax.all_to_all(blocks, AXES, 0, 0, axis_index_groups=parts, tiled=True)  21.9 us
    ppermute x4, waiting for transfers between devices, chan_swap(): return lax.ppermute(values, 'chan', [(c, c ^ bit) for c in range(nc)])  19.5 us
    ppermute x1, waiting for transfers between devices, shards(): other = lax.ppermute(piece, AXES, [(i, i ^ shift) for i in range(devices)])  15.1 us
    all_to_all x3, starting transfers between devices, exchange(): lax.all_to_all(blocks, AXES, 0, 0, axis_index_groups=parts, tiled=True)  11.9 us
    pallas_call x1, Pallas kernels, shards(): pl.pallas_call(functools.partial(adam_body, lid, cam, chans, nc, len(smal...  6.85 us
    pallas_call x1, Pallas kernels, shards(): pl.pallas_call(functools.partial(home_body, block), in_specs=[pl.BlockSpe...  5.77 us
  transfers between devices with their start and end apart: 15, of which 9 were waited for; matrix products, arithmetic and copies ran while one was open for 2% of the time, Pallas kernels for 11%

profile of v5, /device:TPU:0, one launch (start us, length us, event | category | flops | bytes accessed | tf_op | source)
XLA Modules:
  0.0 177.9 jit_solution(15103653666413658859)
XLA Ops:
  0.7 2.7 %shard_map.279 = bf16[64,5504]{1,0:T(8,128)(2,1)} custom-call(f32[4,64]{1,0:T(4,128)} %refs_7_.1, f32[3,3,64,256]{3,2,1,0:T(8,128)} %bitcast.32, f32[3,3,64,80]{3,2,1,0:T(8,128)} %bitcast.34, f32[3,3,64,256]{3,2,1,0:T(8,128)} %refs_16_.1), custom_call_target="tpu_custom_call" | custom-call | tf_op jit(solution)/shard_map/pallas_call | solution.py:760
  3.4 3.0 %collective-permute-start = (bf16[1,64,5504]{2,1,0:T(8,128)(2,1)}, bf16[1,64,5504]{2,1,0:T(8,128)(2,1)S(1)}, u32[]{:S(2)}, u32[]{:S(2)}) collective-permute-start(bf16[1,64,5504]{2,1,0:T(8,128)(2,1)} %bitcast.22), channel_id=1, source_target_pairs={{0,2},{1,3},{2,0},{3,1},{4,6},{5,7},{6,4},{7,5},{8,10},{9,11},{10,... | collective-permute-start | bytes 2113544 | tf_op jit(solution)/shard_map/ppermute | solution.py:708
  6.5 0.3 reshape.51.refs_2_
  6.8 0.3 reshape.52.refs_3_
  7.2 4.5 %shard_map.282 = bf16[16,148,256]{2,1,0:T(8,128)(2,1)} custom-call(s32[1,16384]{1,0:T(1,128)S(1)} %bitcast.27, bf16[20,16384]{1,0:T(8,128)(2,1)S(1)} %copy-done.2, bf16[16,64,256]{2,1,0:T(8,128)(2,1)S(1)} %reshape.51.refs_2_, bf16[16,64,256]{2,1,0:T(8,128)(2,1)S(1)} %reshape.52.refs_3_), custom_call_target="tpu_custom_call" | custom-call | tf_op jit(solution)/shard_map/pallas_call | solution.py:43
  11.7 4.0 %all-to-all-start = ((bf16[16,148,256]{2,1,0:T(8,128)(2,1)}), bf16[16,148,256]{2,1,0:T(8,128)(2,1)S(1)}, u32[]{:S(2)}, u32[]{:S(2)}) async-start(bf16[16,148,256]{2,1,0:T(8,128)(2,1)} %shard_map.282), calls=%async_computation | async-start | bytes 2490368 | tf_op jit(solution)/shard_map/all_to_all | solution.py:702
  15.7 17.3 %collective-permute-done.refs_2_ = bf16[1,64,5504]{2,1,0:T(8,128)(2,1)S(1)} collective-permute-done((bf16[1,64,5504]{2,1,0:T(8,128)(2,1)}, bf16[1,64,5504]{2,1,0:T(8,128)(2,1)S(1)}, u32[]{:S(2)}, u32[]{:S(2)}) %collective-permute-start) | collective-permute-done | bytes 704544 | tf_op jit(solution)/shard_map/ppermute | solution.py:708
  33.0 1.2 pad_maximum_fusion
  34.2 0.9 all-to-all-done.refs_0_
  35.2 2.7 %collective-permute-start.2 = (bf16[4,148,128]{2,1,0:T(8,128)(2,1)S(1)}, bf16[4,148,128]{2,1,0:T(8,128)(2,1)S(1)}, u32[]{:S(2)}, u32[]{:S(2)}) collective-permute-start(bf16[4,148,128]{2,1,0:T(8,128)(2,1)S(1)} %slice_select_fusion), channel_id=1, source_target_pairs={{0,16},{1,17},{2,18},{3,19},{4,20},{5,21},{6,22},{7,23},{8,24},{9,... | collective-permute-start | bytes 454664 | tf_op jit(solution)/shard_map/ppermute | solution.py:715
  37.9 1.7 shard_map.280
  39.7 0.8 shard_map.281
  40.5 2.2 %shard_map.283 = (bf16[1024,1280]{1,0:T(8,128)(2,1)S(1)}, bf16[256,1024]{1,0:T(8,128)(2,1)S(1)}, f32[256,1024]{1,0:T(8,128)S(1)}) custom-call(bf16[16,148,256]{2,1,0:T(8,128)(2,1)S(1)} %all-to-all-done.refs_0_, bf16[256,3072]{1,0:T(8,128)(2,1)S(1)} %get-tuple-element.69.refs_0_.refs_1_.refs_6_), custom_call_target="tpu_custom_call" | custom-call | tf_op jit(solution)/shard_map/pallas_call | solution.py:43
  42.7 3.4 %collective-permute-done.2.refs_4_.refs_5_ = bf16[4,148,128]{2,1,0:T(8,128)(2,1)S(1)} collective-permute-done((bf16[4,148,128]{2,1,0:T(8,128)(2,1)S(1)}, bf16[4,148,128]{2,1,0:T(8,128)(2,1)S(1)}, u32[]{:S(2)}, u32[]{:S(2)}) %collective-permute-start.2) | collective-permute-done | bytes 151584 | tf_op jit(solution)/shard_map/ppermute | solution.py:715
  46.0 1.2 shard_map.284
  47.4 13.3 %all_to_all.40.refs_4_ = f32[32,2,256]{2,1,0:T(2,128)S(1)} all-to-all(f32[32,2,256]{2,1,0:T(2,128)S(1)} %get-tuple-element.76), channel_id=1, replica_groups=mesh['strip'=8,'chan'=4] {'strip','chan'}, dimensions={0} | all-to-all | bytes 131072 | tf_op jit(solution)/shard_map/all_to_all | solution.py:705
  60.7 2.8 %shard_map.285 = (f32[256,1024]{1,0:T(8,128)S(1)}, f32[32,2,256]{2,1,0:T(2,128)S(1)}, f32[1,256,128]{2,1,0:T(8,128)S(1)}, f32[256,1024]{1,0:T(8,128)S(1)}, f32[256,128]{1,0:T(8,128)S(1)}) custom-call(s32[2]{0:T(128)S(1)} %pad_add_fusion.refs_0_.refs_2_.place_ref, f32[256,1024]{1,0:T(8,128)S(1)} %get-tuple-element.74.refs_1_.refs_9_.refs_4_, ...), custom_call_target="tpu_custom_call" | custom-call | tf_op jit(solution)/shard_map/pallas_call | solution.py:43
  63.5 0.7 collective-permute-start.4
  64.2 10.0 %all_to_all.41.refs_4_ = f32[32,2,256]{2,1,0:T(2,128)S(1)} all-to-all(f32[32,2,256]{2,1,0:T(2,128)S(1)} %get-tuple-element.80), channel_id=1, replica_groups=mesh['strip'=8,'chan'=4] {'strip','chan'}, dimensions={0} | all-to-all | bytes 131072 | tf_op jit(solution)/shard_map/all_to_all | solution.py:705
  74.2 1.8 %shard_map.286 = (f32[256,1280]{1,0:T(8,128)S(1)}, f32[32,2,256]{2,1,0:T(2,128)S(1)}, f32[256,128]{1,0:T(8,128)S(1)}, bf16[16,64,256]{2,1,0:T(8,128)(2,1)S(1)}) custom-call(s32[2]{0:T(128)S(1)} %pad_add_fusion.refs_0_.refs_2_.place_ref, f32[256,1024]{1,0:T(8,128)S(1)} %get-tuple-element.78.refs_1_.refs_2_, ...), custom_call_target="tpu_custom_call" | custom-call | tf_op jit(solution)/shard_map/pallas_call | solution.py:43
  76.1 9.6 %all_to_all.42.refs_6_ = f32[32,2,256]{2,1,0:T(2,128)S(1)} all-to-all(f32[32,2,256]{2,1,0:T(2,128)S(1)} %get-tuple-element.86), channel_id=1, replica_groups=mesh['strip'=8,'chan'=4] {'strip','chan'}, dimensions={0} | all-to-all | bytes 131072 | tf_op jit(solution)/shard_map/all_to_all | solution.py:705
  85.7 3.0 %shard_map.287 = (f32[256,1024]{1,0:T(8,128)S(1)}, f32[32,2,256]{2,1,0:T(2,128)S(1)}, f32[1,256,128]{2,1,0:T(8,128)S(1)}, bf16[768,1280]{1,0:T(8,128)(2,1)S(1)}, f32[2,256]{1,0:T(2,128)S(1)}) custom-call(s32[2]{0:T(128)S(1)} %pad_add_fusion.refs_0_.refs_2_.place_ref, f32[256,1280]{1,0:T(8,128)S(1)} %get-tuple-element.84.refs_1_, ...), custom_call_target="tpu_custom_call" | custom-call | tf_op jit(solution)/shard_map/pallas_call | solution.py:43
  88.8 0.7 collective-permute-start.5
  89.5 10.0 %all_to_all.43.refs_8_ = f32[32,2,256]{2,1,0:T(2,128)S(1)} all-to-all(f32[32,2,256]{2,1,0:T(2,128)S(1)} %get-tuple-element.90), channel_id=1, replica_groups=mesh['strip'=8,'chan'=4] {'strip','chan'}, dimensions={0} | all-to-all | bytes 131072 | tf_op jit(solution)/shard_map/all_to_all | solution.py:705
  99.5 5.1 %shard_map.288 = (f32[128,5376]{1,0:T(8,128)S(1)}, bf16[128,5376]{1,0:T(8,128)(2,1)S(1)}, bf16[768,1280]{1,0:T(8,128)(2,1)S(1)}, f32[4,256]{1,0:T(4,128)S(1)}, f32[1,1]{1,0:T(1,128)}) custom-call(s32[2]{0:T(128)S(1)} %pad_add_fusion.refs_0_.refs_2_.place_ref, f32[256,1024]{1,0:T(8,128)S(1)} %get-tuple-element.88.refs_1_, ...), custom_call_target="tpu_custom_call" | custom-call | tf_op jit(solution)/shard_map/pallas_call | solution.py:43
  104.6 0.1 collective-permute-start.6
  104.8 2.8 %shard_map.289.refs_0_ = bf16[16,148,256]{2,1,0:T(8,128)(2,1)} custom-call(bf16[768,1280]{1,0:T(8,128)(2,1)S(1)} %get-tuple-element.95.refs_0_, bf16[336,2304]{1,0:T(8,128)(2,1)S(1)} %get-tuple-element.71.refs_0_.refs_1_, bf16[16,64,256]{2,1,0:T(8,128)(2,1)S(1)} %get-tuple-element.96.refs_2_), custom_call_target="tpu_custom_call" | custom-call | tf_op jit(solution)/shard_map/pallas_call | solution.py:43
  107.6 0.2 collective-permute-done.6.refs_2_
  107.8 0.3 shard_map.290
  108.0 21.9 %all_to_all.44.refs_0_ = bf16[8,16,5376]{2,1,0:T(8,128)(2,1)S(1)} all-to-all(bf16[8,16,5376]{2,1,0:T(8,128)(2,1)S(1)} %bitcast.26), channel_id=1, replica_groups={{0,4,8,12,2,6,10,14},{1,5,9,13,3,7,11,15},{16,20,24,28,18,22,26,30},{17..., dimensions={0} | all-to-all | bytes 2752512 | tf_op jit(solution)/shard_map/all_to_all | solution.py:702
  130.0 3.6 %all-to-all-start.6 = ((bf16[16,148,256]{2,1,0:T(8,128)(2,1)}), bf16[16,148,256]{2,1,0:T(8,128)(2,1)S(1)}, u32[]{:S(2)}, u32[]{:S(2)}) async-start(bf16[16,148,256]{2,1,0:T(8,128)(2,1)} %shard_map.289.refs_0_), calls=%async_computation.6 | async-start | bytes 2490368 | tf_op jit(solution)/shard_map/all_to_all | solution.py:702
  133.6 0.2 shard_map.291.refs_0_
  133.7 1.1 collective-permute-start.7
  134.8 15.1 %collective-permute-done.7.refs_1_ = bf16[16,5376]{1,0:T(8,128)(2,1)S(1)} collective-permute-done((bf16[16,5376]{1,0:T(8,128)(2,1)S(1)}, bf16[16,5376]{1,0:T(8,128)(2,1)S(1)}, u32[]{:S(2)}, u32[]{:S(2)}) %collective-permute-start.7) | collective-permute-done | bytes 172064 | tf_op jit(solution)/shard_map/ppermute | solution.py:889
  149.9 1.1 shard_map.292
  151.1 1.1 all-to-all-done.6.refs_1_
  152.2 4.3 %all-to-all-start.7 = ((bf16[4,16,5504]{2,1,0:T(8,128)(2,1)}), bf16[4,16,5504]{2,1,0:T(8,128)(2,1)S(1)}, u32[]{:S(2)}, u32[]{:S(2)}) async-start(bf16[4,16,5504]{2,1,0:T(8,128)(2,1)} %shard_map.292), calls=%async_computation.7 | async-start | bytes 1409024 | tf_op jit(solution)/shard_map/all_to_all | solution.py:702
  156.5 0.6 shard_map.293
  157.3 2.0 %collective-permute-done.8 = bf16[8,148,256]{2,0,1:T(8,128)(2,1)S(1)} collective-permute-done((bf16[8,148,256]{2,0,1:T(8,128)(2,1)S(1)}, bf16[8,148,256]{2,0,1:T(8,128)(2,1)S(1)}, u32[]{:S(2)}, u32[]{:S(2)}) %collective-permute-start.8) | collective-permute-done | bytes 606240 | tf_op jit(solution)/shard_map/ppermute | solution.py:708
  159.4 5.8 %shard_map.294 = (f32[16,64,2,128]{3,2,1,0:T(2,128)}, f32[16,64,2,128]{3,2,1,0:T(2,128)}, f32[20,16384]{1,0:T(8,128)}, f32[8,128]{1,0:T(8,128)S(1)}) custom-call(s32[2]{0:T(128)S(1)} %pad_add_fusion.refs_0_.refs_2_.place_ref, s32[1,16384]{1,0:T(1,128)S(1)} %bitcast.28, bf16[8,148,256]{2,1,0:T(8,128)(2,1)S(1)} %get-tuple-element.100.keep_ref, ...), custom_call_target="tpu_custom_call" | custom-call | tf_op jit(solution)/shard_map/pallas_call | solution.py:901
  165.2 0.1 shard_map.295.refs_0_
  165.4 1.2 collective-permute-start.11
  166.6 0.6 collective-permute-start.10
  167.3 0.7 constant_dynamic-slice_fusion.refs_6_
  168.0 0.5 collective-permute-done.11.refs_3_
  168.5 1.8 collective-permute-done.10.refs_2_
  170.3 0.6 copy-done.8
  170.8 6.8 %shard_map.296 = (f32[4,64]{1,0:T(4,128)}, f32[4,64]{1,0:T(4,128)}, f32[4,64]{1,0:T(4,128)}, f32[1,1]{1,0:T(1,128)}, f32[3,3,64,80]{3,2,1,0:T(8,128)}, /*index=5...) custom-call(f32[8,128]{1,0:T(8,128)} %copy-done.4, ...), custom_call_target="tpu_custom_call" | custom-call | tf_op jit(solution)/shard_map/pallas_call | solution.py:930
  (33 shorter events, 0.6 us)
Async XLA Ops:
  0.6 5.8 %copy-start.5 = (bf16[16,64,2,128]{3,2,1,0:T(2,128)(2,1)S(1)}, bf16[16,64,2,128]{3,2,1,0:T(2,128)(2,1)}, u32[]{:S(2)}) copy-start(bf16[16,64,2,128]{3,2,1,0:T(2,128)(2,1)} %param.18) | copy-start | bytes 1572868
  0.7 6.1 %copy-start.6 = (bf16[16,64,2,128]{3,2,1,0:T(2,128)(2,1)S(1)}, bf16[16,64,2,128]{3,2,1,0:T(2,128)(2,1)}, u32[]{:S(2)}) copy-start(bf16[16,64,2,128]{3,2,1,0:T(2,128)(2,1)} %param.23) | copy-start | bytes 1572868
  3.4 3.7 %copy-start.2 = (bf16[20,16384]{1,0:T(8,128)(2,1)S(1)}, bf16[20,16384]{1,0:T(8,128)(2,1)}, u32[]{:S(2)}) copy-start(bf16[20,16384]{1,0:T(8,128)(2,1)} %refs_1_.1) | copy-start | bytes 1966084
  3.4 3.7 %copy-start.3 = (s32[16384]{0:T(1024)S(1)}, s32[16384]{0:T(1024)}, u32[]{:S(2)}) copy-start(s32[16384]{0:T(1024)} %param.17) | copy-start | bytes 196612
  3.4 29.5 %collective-permute-start = (bf16[1,64,5504]{2,1,0:T(8,128)(2,1)}, bf16[1,64,5504]{2,1,0:T(8,128)(2,1)S(1)}, u32[]{:S(2)}, u32[]{:S(2)}) collective-permute-start(bf16[1,64,5504]{2,1,0:T(8,128)(2,1)} %bitcast.22), channel_id=1, source_target_pairs={{0,2},{1,3},{2,0},{3,1},{4,6},{5,7},{6,4},{7,5},{8,10},{9,11},{10,... | collective-permute-start | bytes 2113544 | tf_op jit(solution)/shard_map/ppermute | solution.py:708
  11.7 21.3 %copy-start = (bf16[64,5504]{1,0:T(8,128)(2,1)S(1)}, bf16[64,5504]{1,0:T(8,128)(2,1)}, u32[]{:S(2)}) copy-start(bf16[64,5504]{1,0:T(8,128)(2,1)} %shard_map.279) | copy-start | bytes 2113540
  11.7 23.5 %all-to-all-start = ((bf16[16,148,256]{2,1,0:T(8,128)(2,1)}), bf16[16,148,256]{2,1,0:T(8,128)(2,1)S(1)}, u32[]{:S(2)}, u32[]{:S(2)}) async-start(bf16[16,148,256]{2,1,0:T(8,128)(2,1)} %shard_map.282), calls=%async_computation | async-start | bytes 2490368 | tf_op jit(solution)/shard_map/all_to_all | solution.py:702
  34.2 3.7 %collective-permute-start.1 = (bf16[2,64,5504]{2,1,0:T(8,128)(2,1)}, bf16[2,64,5504]{2,1,0:T(8,128)(2,1)}, u32[]{:S(2)}, u32[]{:S(2)}) collective-permute-start(bf16[2,64,5504]{2,1,0:T(8,128)(2,1)} %pad_maximum_fusion), channel_id=1, source_target_pairs={{0,1},{1,0},{2,3},{3,2},{4,5},{5,4},{6,7},{7,6},{8,9},{9,8},{10,11... | collective-permute-start | bytes 4227080 | tf_op jit(solution)/shard_map/ppermute | solution.py:708
  35.2 10.9 %collective-permute-start.2 = (bf16[4,148,128]{2,1,0:T(8,128)(2,1)S(1)}, bf16[4,148,128]{2,1,0:T(8,128)(2,1)S(1)}, u32[]{:S(2)}, u32[]{:S(2)}) collective-permute-start(bf16[4,148,128]{2,1,0:T(8,128)(2,1)S(1)} %slice_select_fusion), channel_id=1, source_target_pairs={{0,16},{1,17},{2,18},{3,19},{4,20},{5,21},{6,22},{7,23},{8,24},{9,... | collective-permute-start | bytes 454664 | tf_op jit(solution)/shard_map/ppermute | solution.py:715
  47.3 13.4 %collective-permute-start.3 = (f32[256,128]{1,0:T(8,128)S(1)}, f32[256,128]{1,0:T(8,128)S(1)}, u32[]{:S(2)}, u32[]{:S(2)}) collective-permute-start(f32[256,128]{1,0:T(8,128)S(1)} %bitcast.30), channel_id=1, source_target_pairs={{0,16},{1,17},{2,18},{3,19},{4,20},{5,21},{6,22},{7,23},{8,24},{9,... | collective-permute-start | bytes 393224 | tf_op jit(solution)/shard_map/ppermute | solution.py:715
  63.5 10.8 %collective-permute-start.4 = (f32[256,128]{1,0:T(8,128)S(1)}, f32[256,128]{1,0:T(8,128)S(1)}, u32[]{:S(2)}, u32[]{:S(2)}) collective-permute-start(f32[256,128]{1,0:T(8,128)S(1)} %bitcast.31), channel_id=1, source_target_pairs={{0,16},{1,17},{2,18},{3,19},{4,20},{5,21},{6,22},{7,23},{8,24},{9,... | collective-permute-start | bytes 393224 | tf_op jit(solution)/shard_map/ppermute | solution.py:715
  88.8 10.8 %collective-permute-start.5 = (f32[256,128]{1,0:T(8,128)S(1)}, f32[256,128]{1,0:T(8,128)S(1)}, u32[]{:S(2)}, u32[]{:S(2)}) collective-permute-start(f32[256,128]{1,0:T(8,128)S(1)} %bitcast.29), channel_id=1, source_target_pairs={{0,16},{1,17},{2,18},{3,19},{4,20},{5,21},{6,22},{7,23},{8,24},{9,... | collective-permute-start | bytes 393224 | tf_op jit(solution)/shard_map/ppermute | solution.py:715
  104.6 3.1 %collective-permute-start.6 = (bf16[128,5376]{1,0:T(8,128)(2,1)S(1)}, bf16[128,5376]{1,0:T(8,128)(2,1)S(1)}, u32[]{:S(2)}, u32[]{:S(2)}) collective-permute-start(bf16[128,5376]{1,0:T(8,128)(2,1)S(1)} %get-tuple-element.98), channel_id=1, source_target_pairs={{0,1},{1,0},{2,3},{3,2},{4,5},{5,4},{6,7},{7,6},{8,9},{9,8},{10,11... | collective-permute-start | bytes 4128776 | tf_op jit(solution)/shard_map/ppermute | solution.py:708
  130.0 22.2 %all-to-all-start.6 = ((bf16[16,148,256]{2,1,0:T(8,128)(2,1)}), bf16[16,148,256]{2,1,0:T(8,128)(2,1)S(1)}, u32[]{:S(2)}, u32[]{:S(2)}) async-start(bf16[16,148,256]{2,1,0:T(8,128)(2,1)} %shard_map.289.refs_0_), calls=%async_computation.6 | async-start | bytes 2490368 | tf_op jit(solution)/shard_map/all_to_all | solution.py:702
  133.7 16.2 %collective-permute-start.7 = (bf16[16,5376]{1,0:T(8,128)(2,1)S(1)}, bf16[16,5376]{1,0:T(8,128)(2,1)S(1)}, u32[]{:S(2)}, u32[]{:S(2)}) collective-permute-start(bf16[16,5376]{1,0:T(8,128)(2,1)S(1)} %shard_map.291.refs_0_), channel_id=1, source_target_pairs={{0,16},{1,17},{2,18},{3,19},{4,20},{5,21},{6,22},{7,23},{8,24},{9,... | collective-permute-start | bytes 516104 | tf_op jit(solution)/shard_map/ppermute | solution.py:889
  152.2 13.1 %all-to-all-start.7 = ((bf16[4,16,5504]{2,1,0:T(8,128)(2,1)}), bf16[4,16,5504]{2,1,0:T(8,128)(2,1)S(1)}, u32[]{:S(2)}, u32[]{:S(2)}) async-start(bf16[4,16,5504]{2,1,0:T(8,128)(2,1)} %shard_map.292), calls=%async_computation.7 | async-start | bytes 1409024 | tf_op jit(solution)/shard_map/all_to_all | solution.py:702
  157.2 2.1 %collective-permute-start.8 = (bf16[8,148,256]{2,0,1:T(8,128)(2,1)S(1)}, bf16[8,148,256]{2,0,1:T(8,128)(2,1)S(1)}, u32[]{:S(2)}, u32[]{:S(2)}) collective-permute-start(bf16[8,148,256]{2,0,1:T(8,128)(2,1)S(1)} %copy.32), channel_id=1, source_target_pairs={{0,1},{1,0},{2,3},{3,2},{4,5},{5,4},{6,7},{7,6},{8,9},{9,8},{10,11... | collective-permute-start | bytes 1818632 | tf_op jit(solution)/shard_map/ppermute | solution.py:708
  165.2 5.0 %copy-start.1 = (bf16[4,16,5504]{2,1,0:T(8,128)(2,1)}, bf16[4,16,5504]{2,1,0:T(8,128)(2,1)S(1)}, u32[]{:S(2)}) copy-start(bf16[4,16,5504]{2,1,0:T(8,128)(2,1)S(1)} %all-to-all-done.7.refs_1_) | copy-start | bytes 2113540
  165.4 4.9 %copy-start.4 = (f32[8,128]{1,0:T(8,128)}, f32[8,128]{1,0:T(8,128)S(1)}, u32[]{:S(2)}) copy-start(f32[8,128]{1,0:T(8,128)S(1)} %shard_map.295.refs_0_) | copy-start | bytes 12292
  165.4 3.1 %collective-permute-start.11 = (f32[8,128]{1,0:T(8,128)S(1)}, f32[8,128]{1,0:T(8,128)S(1)}, u32[]{:S(2)}, u32[]{:S(2)}) collective-permute-start(f32[8,128]{1,0:T(8,128)S(1)} %shard_map.295.refs_0_), channel_id=1, source_target_pairs={{0,3},{1,2},{2,1},{3,0},{4,7},{5,6},{6,5},{7,4},{8,11},{9,10},{10,... | collective-permute-start | bytes 12296 | tf_op jit(solution)/shard_map/ppermute | solution.py:924
  166.6 3.6 %collective-permute-start.10 = (f32[8,128]{1,0:T(8,128)S(1)}, f32[8,128]{1,0:T(8,128)S(1)}, u32[]{:S(2)}, u32[]{:S(2)}) collective-permute-start(f32[8,128]{1,0:T(8,128)S(1)} %shard_map.295.refs_0_), channel_id=1, source_target_pairs={{0,2},{1,3},{2,0},{3,1},{4,6},{5,7},{6,4},{7,5},{8,10},{9,11},{10,... | collective-permute-start | bytes 12296 | tf_op jit(solution)/shard_map/ppermute | solution.py:924
  167.2 3.0 %collective-permute-start.9 = (f32[8,128]{1,0:T(8,128)S(1)}, f32[8,128]{1,0:T(8,128)S(1)}, u32[]{:S(2)}, u32[]{:S(2)}) collective-permute-start(f32[8,128]{1,0:T(8,128)S(1)} %shard_map.295.refs_0_), channel_id=1, source_target_pairs={{0,1},{1,0},{2,3},{3,2},{4,5},{5,4},{6,7},{7,6},{8,9},{9,8},{10,11... | collective-permute-start | bytes 12296 | tf_op jit(solution)/shard_map/ppermute | solution.py:924
  168.5 1.8 %copy-start.7 = (f32[8,128]{1,0:T(8,128)}, f32[8,128]{1,0:T(8,128)S(1)}, u32[]{:S(2)}) copy-start(f32[8,128]{1,0:T(8,128)S(1)} %collective-permute-done.11.refs_3_) | copy-start | bytes 12292
  170.2 0.6 copy-start.8
  170.2 0.6 copy-start.9

commit v6 on v5

--- a/solution.py
+++ b/solution.py
@@ -480,7 +480,7 @@
         [total[1:2], total[0:1], grads_two_ref[1:2], grads_two_ref[0:1]], axis=0
     )
     grads_ref[...] = grads
-    squares_ref[...] = jnp.sum(grads * grads).reshape(1, 1)
+    squares_ref[...] = jnp.broadcast_to(jnp.sum(grads * grads), squares_ref.shape)
     columns = to_columns([total[0:1] / pixel_count, total[1:2] / pixel_count])
     shift_mean, gain_mean = columns[:, 0:1], columns[:, 1:2]
     mean, inv = means_ref[:, 0:1], means_ref[:, 1:2]
@@ -580,11 +580,11 @@
 
 
 def adam_body(lid, cam, mid, chans, smalls, *refs):
-    square_refs, grads_ref, refs = refs[:chans], refs[chans], refs[chans + 1 :]
+    grads_far, refs = refs[0], refs[1:]
     small_fars, fars, refs = refs[:smalls], refs[smalls : smalls + 9], refs[smalls + 9 :]
     small_outs, far_outs, refs = refs[:4], refs[4:13], refs[13:]
     small_nears, nears, refs = refs[:smalls], refs[smalls : smalls + 9], refs[smalls + 9 :]
-    small_ins, ins, outs, norm_ref = refs
+    small_ins, ins, outs, norm_ref, grads_ref, grads_sem = refs
     one_width = round_up(3 * lid + 3 * cam, 256)
     first = [
         pltpu.make_async_copy(far, near, small_ins.at[i])
@@ -594,16 +594,17 @@
         [pltpu.make_async_copy(fars[i].at[a], nears[i].at[a], ins.at[i, a]) for i in range(9)]
         for a in range(3)
     ]
-    for group in (first, *reads):
+    grads_copy = pltpu.make_async_copy(grads_far, grads_ref, grads_sem)
+    for group in (first, [grads_copy], *reads):
         for copy in group:
             copy.start()
     for copy in first:
         copy.wait()
-    squares = [ref[0:1, 0:1] for ref in square_refs]
-    norm_squares_ref, norm_grad_ref, *norm_state = small_nears
+    squares = [ref[0:1, 0:1] for ref in small_nears[:chans]]
+    norm_squares_ref, norm_grad_ref, *norm_state = small_nears[chans:]
     while len(squares) > 1:
         squares = [squares[i] + squares[i + 1] for i in range(0, len(squares), 2)]
-    norm = jnp.sqrt(squares[0] + norm_squares_ref[...])
+    norm = jnp.sqrt(squares[0] + norm_squares_ref[0:1, 0:1])
     norm_ref[...] = norm
     factor = jnp.minimum(1.0, clip_norm / (norm + 1e-06))
 
@@ -621,6 +622,7 @@
     ]
     for copy in writes[0]:
         copy.start()
+    grads_copy.wait()
     for a in range(3):
         for copy in reads[a]:
             copy.wait()
@@ -863,7 +865,7 @@
             struct((chans // 2, total_width), bf16),
             struct((two_width, wide), bf16),
             struct((4, chans), f32),
-            struct((1, 1), f32),
+            struct((8, LANES), f32),
         ],
         scratch=[pltpu.VMEM((one_width, wide), bf16)],
         smem=1,
@@ -925,11 +927,11 @@
     ]
     grad_bn = lax.dynamic_slice(grad_bn_all, (0, chan * own), (4, own))
     norm_state = [bn_params, m_bn, v_bn]
-    small = [norm_squares, grad_bn, *norm_state]
-    results = [*norm_state, norm_squares, *state]
+    small = [*squares, norm_squares, grad_bn, *norm_state]
+    results = [*norm_state, struct((1, 1), f32), *state]
     updated = pl.pallas_call(
         functools.partial(adam_body, lid, cam, chans, nc, len(small)),
-        in_specs=[near] * (nc + 1) + [far] * (len(small) + 9),
+        in_specs=[far] * (len(small) + 10),
         out_specs=[far] * 13,
         out_shape=[struct(array.shape, f32) for array in results],
         scratch_shapes=[
@@ -938,9 +940,11 @@
             pltpu.SemaphoreType.DMA((9, 3)),
             pltpu.SemaphoreType.DMA((9, 3)),
             pltpu.VMEM((1, 1), f32),
+            pltpu.VMEM(own_grads.shape, bf16),
+            pltpu.SemaphoreType.DMA,
         ],
         compiler_params=pltpu.CompilerParams(vmem_limit_bytes=VMEM_MOST),
-    )(*squares, own_grads, *small, *state)
+    )(own_grads, *small, *state)
     turned = [tall(array) for array in updated[4:10]]
     return (mixed, grad_cam, grad_lidar, updated[3].reshape(()), *turned, *updated[10:], *updated[:3])
 

time: 178 us -> 177 us (level)
  no operation moved by 1% of the time
where the time goes in v6:
time: 177 us; the launch traced here: 176 us
  blocking collectives  65 us (37%)
  waiting for transfers between devices  42.3 us (24%)
  Pallas kernels  42 us (24%)
  starting transfers between devices  22.4 us (13%)
  local copies, waits for them, and re-layouts  2.16 us (1%)
    all_to_all x4, blocking collectives, everywhere(): return lax.all_to_all(copies, AXES, 0, 0, tiled=True)  43 us
    pallas_call x15, Pallas kernels, run(): pl.pallas_call(lambda *refs: body(*refs[waits:]), out_shape=out_shape, in...  27.9 us
    all_to_all x1, blocking collectives, exchange(): lax.all_to_all(blocks, AXES, 0, 0, axis_index_groups=parts, tiled=True)  22 us
    ppermute x4, waiting for transfers between devices, chan_swap(): return lax.ppermute(values, 'chan', [(c, c ^ bit) for c in range(nc)])  19.5 us
    ppermute x1, waiting for transfers between devices, shards(): other = lax.ppermute(piece, AXES, [(i, i ^ shift) for i in range(devices)])  15.1 us
    all_to_all x3, starting transfers between devices, exchange(): lax.all_to_all(blocks, AXES, 0, 0, axis_index_groups=parts, tiled=True)  11.9 us
    pallas_call x1, Pallas kernels, shards(): pl.pallas_call(functools.partial(home_body, block), in_specs=[pl.BlockSpe...  5.77 us
    pallas_call x1, Pallas kernels, shards(): pl.pallas_call(functools.partial(adam_body, lid, cam, chans, nc, len(smal...  5.54 us
  transfers between devices with their start and end apart: 15, of which 9 were waited for; matrix products, arithmetic and copies ran while one was open for 2% of the time, Pallas kernels for 11%

profile of v6, /device:TPU:0, one launch (start us, length us, event | category | flops | bytes accessed | tf_op | source)
XLA Modules:
  0.0 176.3 jit_solution(3197241671223269100)
XLA Ops:
  0.7 2.7 %shard_map.279 = bf16[64,5504]{1,0:T(8,128)(2,1)} custom-call(f32[4,64]{1,0:T(4,128)} %refs_7_.1, f32[3,3,64,256]{3,2,1,0:T(8,128)} %bitcast.32, f32[3,3,64,80]{3,2,1,0:T(8,128)} %bitcast.34, f32[3,3,64,256]{3,2,1,0:T(8,128)} %refs_16_.1), custom_call_target="tpu_custom_call" | custom-call | tf_op jit(solution)/shard_map/pallas_call | solution.py:762
  3.4 3.0 %collective-permute-start = (bf16[1,64,5504]{2,1,0:T(8,128)(2,1)}, bf16[1,64,5504]{2,1,0:T(8,128)(2,1)S(1)}, u32[]{:S(2)}, u32[]{:S(2)}) collective-permute-start(bf16[1,64,5504]{2,1,0:T(8,128)(2,1)} %bitcast.22), channel_id=1, source_target_pairs={{0,2},{1,3},{2,0},{3,1},{4,6},{5,7},{6,4},{7,5},{8,10},{9,11},{10,... | collective-permute-start | bytes 2113544 | tf_op jit(solution)/shard_map/ppermute | solution.py:710
  6.5 0.3 reshape.51.refs_2_
  6.8 0.3 reshape.52.refs_3_
  7.2 4.5 %shard_map.282 = bf16[16,148,256]{2,1,0:T(8,128)(2,1)} custom-call(s32[1,16384]{1,0:T(1,128)S(1)} %bitcast.27, bf16[20,16384]{1,0:T(8,128)(2,1)S(1)} %copy-done.2, bf16[16,64,256]{2,1,0:T(8,128)(2,1)S(1)} %reshape.51.refs_2_, bf16[16,64,256]{2,1,0:T(8,128)(2,1)S(1)} %reshape.52.refs_3_), custom_call_target="tpu_custom_call" | custom-call | tf_op jit(solution)/shard_map/pallas_call | solution.py:43
  11.7 4.0 %all-to-all-start = ((bf16[16,148,256]{2,1,0:T(8,128)(2,1)}), bf16[16,148,256]{2,1,0:T(8,128)(2,1)S(1)}, u32[]{:S(2)}, u32[]{:S(2)}) async-start(bf16[16,148,256]{2,1,0:T(8,128)(2,1)} %shard_map.282), calls=%async_computation | async-start | bytes 2490368 | tf_op jit(solution)/shard_map/all_to_all | solution.py:704
  15.7 17.3 %collective-permute-done.refs_2_ = bf16[1,64,5504]{2,1,0:T(8,128)(2,1)S(1)} collective-permute-done((bf16[1,64,5504]{2,1,0:T(8,128)(2,1)}, bf16[1,64,5504]{2,1,0:T(8,128)(2,1)S(1)}, u32[]{:S(2)}, u32[]{:S(2)}) %collective-permute-start) | collective-permute-done | bytes 704544 | tf_op jit(solution)/shard_map/ppermute | solution.py:710
  33.0 1.2 pad_maximum_fusion
  34.2 0.9 all-to-all-done.refs_0_
  35.2 2.7 %collective-permute-start.2 = (bf16[4,148,128]{2,1,0:T(8,128)(2,1)S(1)}, bf16[4,148,128]{2,1,0:T(8,128)(2,1)S(1)}, u32[]{:S(2)}, u32[]{:S(2)}) collective-permute-start(bf16[4,148,128]{2,1,0:T(8,128)(2,1)S(1)} %slice_select_fusion), channel_id=1, source_target_pairs={{0,16},{1,17},{2,18},{3,19},{4,20},{5,21},{6,22},{7,23},{8,24},{9,... | collective-permute-start | bytes 454664 | tf_op jit(solution)/shard_map/ppermute | solution.py:717
  37.9 1.7 shard_map.280
  39.7 0.8 shard_map.281
  40.5 2.2 %shard_map.283 = (bf16[1024,1280]{1,0:T(8,128)(2,1)S(1)}, bf16[256,1024]{1,0:T(8,128)(2,1)S(1)}, f32[256,1024]{1,0:T(8,128)S(1)}) custom-call(bf16[16,148,256]{2,1,0:T(8,128)(2,1)S(1)} %all-to-all-done.refs_0_, bf16[256,3072]{1,0:T(8,128)(2,1)S(1)} %get-tuple-element.69.refs_0_.refs_1_.refs_6_), custom_call_target="tpu_custom_call" | custom-call | tf_op jit(solution)/shard_map/pallas_call | solution.py:43
  42.7 3.4 %collective-permute-done.2.refs_4_.refs_5_ = bf16[4,148,128]{2,1,0:T(8,128)(2,1)S(1)} collective-permute-done((bf16[4,148,128]{2,1,0:T(8,128)(2,1)S(1)}, bf16[4,148,128]{2,1,0:T(8,128)(2,1)S(1)}, u32[]{:S(2)}, u32[]{:S(2)}) %collective-permute-start.2) | collective-permute-done | bytes 151584 | tf_op jit(solution)/shard_map/ppermute | solution.py:717
  46.0 1.2 shard_map.284
  47.4 13.3 %all_to_all.40.refs_4_ = f32[32,2,256]{2,1,0:T(2,128)S(1)} all-to-all(f32[32,2,256]{2,1,0:T(2,128)S(1)} %get-tuple-element.76), channel_id=1, replica_groups=mesh['strip'=8,'chan'=4] {'strip','chan'}, dimensions={0} | all-to-all | bytes 131072 | tf_op jit(solution)/shard_map/all_to_all | solution.py:707
  60.7 2.8 %shard_map.285 = (f32[256,1024]{1,0:T(8,128)S(1)}, f32[32,2,256]{2,1,0:T(2,128)S(1)}, f32[1,256,128]{2,1,0:T(8,128)S(1)}, f32[256,1024]{1,0:T(8,128)S(1)}, f32[256,128]{1,0:T(8,128)S(1)}) custom-call(s32[2]{0:T(128)S(1)} %pad_add_fusion.refs_0_.refs_2_.place_ref, f32[256,1024]{1,0:T(8,128)S(1)} %get-tuple-element.74.refs_1_.refs_9_.refs_4_, ...), custom_call_target="tpu_custom_call" | custom-call | tf_op jit(solution)/shard_map/pallas_call | solution.py:43
  63.5 0.7 collective-permute-start.4
  64.2 10.0 %all_to_all.41.refs_4_ = f32[32,2,256]{2,1,0:T(2,128)S(1)} all-to-all(f32[32,2,256]{2,1,0:T(2,128)S(1)} %get-tuple-element.80), channel_id=1, replica_groups=mesh['strip'=8,'chan'=4] {'strip','chan'}, dimensions={0} | all-to-all | bytes 131072 | tf_op jit(solution)/shard_map/all_to_all | solution.py:707
  74.2 1.8 %shard_map.286 = (f32[256,1280]{1,0:T(8,128)S(1)}, f32[32,2,256]{2,1,0:T(2,128)S(1)}, f32[256,128]{1,0:T(8,128)S(1)}, bf16[16,64,256]{2,1,0:T(8,128)(2,1)S(1)}) custom-call(s32[2]{0:T(128)S(1)} %pad_add_fusion.refs_0_.refs_2_.place_ref, f32[256,1024]{1,0:T(8,128)S(1)} %get-tuple-element.78.refs_1_.refs_2_, ...), custom_call_target="tpu_custom_call" | custom-call | tf_op jit(solution)/shard_map/pallas_call | solution.py:43
  76.1 9.6 %all_to_all.42.refs_6_ = f32[32,2,256]{2,1,0:T(2,128)S(1)} all-to-all(f32[32,2,256]{2,1,0:T(2,128)S(1)} %get-tuple-element.86), channel_id=1, replica_groups=mesh['strip'=8,'chan'=4] {'strip','chan'}, dimensions={0} | all-to-all | bytes 131072 | tf_op jit(solution)/shard_map/all_to_all | solution.py:707
  85.7 3.0 %shard_map.287 = (f32[256,1024]{1,0:T(8,128)S(1)}, f32[32,2,256]{2,1,0:T(2,128)S(1)}, f32[1,256,128]{2,1,0:T(8,128)S(1)}, bf16[768,1280]{1,0:T(8,128)(2,1)S(1)}, f32[2,256]{1,0:T(2,128)S(1)}) custom-call(s32[2]{0:T(128)S(1)} %pad_add_fusion.refs_0_.refs_2_.place_ref, f32[256,1280]{1,0:T(8,128)S(1)} %get-tuple-element.84.refs_1_, ...), custom_call_target="tpu_custom_call" | custom-call | tf_op jit(solution)/shard_map/pallas_call | solution.py:43
  88.8 0.7 collective-permute-start.5
  89.5 10.0 %all_to_all.43.refs_8_ = f32[32,2,256]{2,1,0:T(2,128)S(1)} all-to-all(f32[32,2,256]{2,1,0:T(2,128)S(1)} %get-tuple-element.90), channel_id=1, replica_groups=mesh['strip'=8,'chan'=4] {'strip','chan'}, dimensions={0} | all-to-all | bytes 131072 | tf_op jit(solution)/shard_map/all_to_all | solution.py:707
  99.5 4.7 %shard_map.288 = (f32[128,5376]{1,0:T(8,128)S(1)}, bf16[128,5376]{1,0:T(8,128)(2,1)S(1)}, bf16[768,1280]{1,0:T(8,128)(2,1)S(1)}, f32[4,256]{1,0:T(4,128)S(1)}, f32[8,128]{1,0:T(8,128)S(1)}) custom-call(s32[2]{0:T(128)S(1)} %pad_add_fusion.refs_0_.refs_2_.place_ref, f32[256,1024]{1,0:T(8,128)S(1)} %get-tuple-element.88.refs_1_, ...), custom_call_target="tpu_custom_call" | custom-call | tf_op jit(solution)/shard_map/pallas_call | solution.py:43
  104.3 0.2 collective-permute-start.6
  104.5 2.8 %shard_map.289.refs_0_ = bf16[16,148,256]{2,1,0:T(8,128)(2,1)} custom-call(bf16[768,1280]{1,0:T(8,128)(2,1)S(1)} %get-tuple-element.95.refs_0_, bf16[336,2304]{1,0:T(8,128)(2,1)S(1)} %get-tuple-element.71.refs_0_.refs_1_, bf16[16,64,256]{2,1,0:T(8,128)(2,1)S(1)} %get-tuple-element.96.refs_2_), custom_call_target="tpu_custom_call" | custom-call | tf_op jit(solution)/shard_map/pallas_call | solution.py:43
  107.3 0.2 collective-permute-done.6.refs_2_
  107.5 0.3 shard_map.290
  107.7 22.0 %all_to_all.44.refs_0_ = bf16[8,16,5376]{2,1,0:T(8,128)(2,1)S(1)} all-to-all(bf16[8,16,5376]{2,1,0:T(8,128)(2,1)S(1)} %bitcast.26), channel_id=1, replica_groups={{0,4,8,12,2,6,10,14},{1,5,9,13,3,7,11,15},{16,20,24,28,18,22,26,30},{17..., dimensions={0} | all-to-all | bytes 2752512 | tf_op jit(solution)/shard_map/all_to_all | solution.py:704
  129.7 3.6 %all-to-all-start.6 = ((bf16[16,148,256]{2,1,0:T(8,128)(2,1)}), bf16[16,148,256]{2,1,0:T(8,128)(2,1)S(1)}, u32[]{:S(2)}, u32[]{:S(2)}) async-start(bf16[16,148,256]{2,1,0:T(8,128)(2,1)} %shard_map.289.refs_0_), calls=%async_computation.6 | async-start | bytes 2490368 | tf_op jit(solution)/shard_map/all_to_all | solution.py:704
  133.3 0.2 shard_map.291.refs_0_
  133.5 1.1 collective-permute-start.7
  134.5 15.1 %collective-permute-done.7.refs_1_ = bf16[16,5376]{1,0:T(8,128)(2,1)S(1)} collective-permute-done((bf16[16,5376]{1,0:T(8,128)(2,1)S(1)}, bf16[16,5376]{1,0:T(8,128)(2,1)S(1)}, u32[]{:S(2)}, u32[]{:S(2)}) %collective-permute-start.7) | collective-permute-done | bytes 172064 | tf_op jit(solution)/shard_map/ppermute | solution.py:891
  149.7 1.1 shard_map.292
  150.8 1.1 all-to-all-done.6.refs_1_
  151.9 4.3 %all-to-all-start.7 = ((bf16[4,16,5504]{2,1,0:T(8,128)(2,1)}), bf16[4,16,5504]{2,1,0:T(8,128)(2,1)S(1)}, u32[]{:S(2)}, u32[]{:S(2)}) async-start(bf16[4,16,5504]{2,1,0:T(8,128)(2,1)} %shard_map.292), calls=%async_computation.7 | async-start | bytes 1409024 | tf_op jit(solution)/shard_map/all_to_all | solution.py:704
  156.2 0.6 shard_map.293
  157.0 2.0 %collective-permute-done.8 = bf16[8,148,256]{2,0,1:T(8,128)(2,1)S(1)} collective-permute-done((bf16[8,148,256]{2,0,1:T(8,128)(2,1)S(1)}, bf16[8,148,256]{2,0,1:T(8,128)(2,1)S(1)}, u32[]{:S(2)}, u32[]{:S(2)}) %collective-permute-start.8) | collective-permute-done | bytes 606240 | tf_op jit(solution)/shard_map/ppermute | solution.py:710
  159.2 5.8 %shard_map.294 = (f32[16,64,2,128]{3,2,1,0:T(2,128)}, f32[16,64,2,128]{3,2,1,0:T(2,128)}, f32[20,16384]{1,0:T(8,128)}, f32[8,128]{1,0:T(8,128)S(1)}) custom-call(s32[2]{0:T(128)S(1)} %pad_add_fusion.refs_0_.refs_2_.place_ref, s32[1,16384]{1,0:T(1,128)S(1)} %bitcast.28, bf16[8,148,256]{2,1,0:T(8,128)(2,1)S(1)} %get-tuple-element.100.keep_ref, ...), custom_call_target="tpu_custom_call" | custom-call | tf_op jit(solution)/shard_map/pallas_call | solution.py:903
  165.0 0.1 shard_map.295.refs_1_
  165.1 1.2 collective-permute-start.11
  166.3 0.6 collective-permute-start.10
  167.0 0.6 constant_dynamic-slice_fusion.refs_6_
  167.7 0.5 collective-permute-done.11.refs_4_
  168.2 1.8 collective-permute-done.10.refs_3_
  170.0 0.6 copy-done.9
  170.5 5.5 %shard_map.296 = (f32[4,64]{1,0:T(4,128)}, f32[4,64]{1,0:T(4,128)}, f32[4,64]{1,0:T(4,128)}, f32[1,1]{1,0:T(1,128)}, f32[3,3,64,80]{3,2,1,0:T(8,128)}, /*index=5...) custom-call(bf16[64,5504]{1,0:T(8,128)(2,1)} %bitcast.25, ...), custom_call_target="tpu_custom_call" | custom-call | tf_op jit(solution)/shard_map/pallas_call | solution.py:932
  (35 shorter events, 0.6 us)
Async XLA Ops:
  0.6 5.8 %copy-start.6 = (bf16[16,64,2,128]{3,2,1,0:T(2,128)(2,1)S(1)}, bf16[16,64,2,128]{3,2,1,0:T(2,128)(2,1)}, u32[]{:S(2)}) copy-start(bf16[16,64,2,128]{3,2,1,0:T(2,128)(2,1)} %param.18) | copy-start | bytes 1572868
  0.7 6.1 %copy-start.7 = (bf16[16,64,2,128]{3,2,1,0:T(2,128)(2,1)S(1)}, bf16[16,64,2,128]{3,2,1,0:T(2,128)(2,1)}, u32[]{:S(2)}) copy-start(bf16[16,64,2,128]{3,2,1,0:T(2,128)(2,1)} %param.23) | copy-start | bytes 1572868
  3.4 3.7 %copy-start.2 = (bf16[20,16384]{1,0:T(8,128)(2,1)S(1)}, bf16[20,16384]{1,0:T(8,128)(2,1)}, u32[]{:S(2)}) copy-start(bf16[20,16384]{1,0:T(8,128)(2,1)} %refs_1_.1) | copy-start | bytes 1966084
  3.4 3.7 %copy-start.3 = (s32[16384]{0:T(1024)S(1)}, s32[16384]{0:T(1024)}, u32[]{:S(2)}) copy-start(s32[16384]{0:T(1024)} %param.17) | copy-start | bytes 196612
  3.4 29.5 %collective-permute-start = (bf16[1,64,5504]{2,1,0:T(8,128)(2,1)}, bf16[1,64,5504]{2,1,0:T(8,128)(2,1)S(1)}, u32[]{:S(2)}, u32[]{:S(2)}) collective-permute-start(bf16[1,64,5504]{2,1,0:T(8,128)(2,1)} %bitcast.22), channel_id=1, source_target_pairs={{0,2},{1,3},{2,0},{3,1},{4,6},{5,7},{6,4},{7,5},{8,10},{9,11},{10,... | collective-permute-start | bytes 2113544 | tf_op jit(solution)/shard_map/ppermute | solution.py:710
  11.7 21.3 %copy-start = (bf16[64,5504]{1,0:T(8,128)(2,1)S(1)}, bf16[64,5504]{1,0:T(8,128)(2,1)}, u32[]{:S(2)}) copy-start(bf16[64,5504]{1,0:T(8,128)(2,1)} %shard_map.279) | copy-start | bytes 2113540
  11.7 23.5 %all-to-all-start = ((bf16[16,148,256]{2,1,0:T(8,128)(2,1)}), bf16[16,148,256]{2,1,0:T(8,128)(2,1)S(1)}, u32[]{:S(2)}, u32[]{:S(2)}) async-start(bf16[16,148,256]{2,1,0:T(8,128)(2,1)} %shard_map.282), calls=%async_computation | async-start | bytes 2490368 | tf_op jit(solution)/shard_map/all_to_all | solution.py:704
  34.2 3.7 %collective-permute-start.1 = (bf16[2,64,5504]{2,1,0:T(8,128)(2,1)}, bf16[2,64,5504]{2,1,0:T(8,128)(2,1)}, u32[]{:S(2)}, u32[]{:S(2)}) collective-permute-start(bf16[2,64,5504]{2,1,0:T(8,128)(2,1)} %pad_maximum_fusion), channel_id=1, source_target_pairs={{0,1},{1,0},{2,3},{3,2},{4,5},{5,4},{6,7},{7,6},{8,9},{9,8},{10,11... | collective-permute-start | bytes 4227080 | tf_op jit(solution)/shard_map/ppermute | solution.py:710
  35.2 10.9 %collective-permute-start.2 = (bf16[4,148,128]{2,1,0:T(8,128)(2,1)S(1)}, bf16[4,148,128]{2,1,0:T(8,128)(2,1)S(1)}, u32[]{:S(2)}, u32[]{:S(2)}) collective-permute-start(bf16[4,148,128]{2,1,0:T(8,128)(2,1)S(1)} %slice_select_fusion), channel_id=1, source_target_pairs={{0,16},{1,17},{2,18},{3,19},{4,20},{5,21},{6,22},{7,23},{8,24},{9,... | collective-permute-start | bytes 454664 | tf_op jit(solution)/shard_map/ppermute | solution.py:717
  47.3 13.4 %collective-permute-start.3 = (f32[256,128]{1,0:T(8,128)S(1)}, f32[256,128]{1,0:T(8,128)S(1)}, u32[]{:S(2)}, u32[]{:S(2)}) collective-permute-start(f32[256,128]{1,0:T(8,128)S(1)} %bitcast.30), channel_id=1, source_target_pairs={{0,16},{1,17},{2,18},{3,19},{4,20},{5,21},{6,22},{7,23},{8,24},{9,... | collective-permute-start | bytes 393224 | tf_op jit(solution)/shard_map/ppermute | solution.py:717
  63.5 10.8 %collective-permute-start.4 = (f32[256,128]{1,0:T(8,128)S(1)}, f32[256,128]{1,0:T(8,128)S(1)}, u32[]{:S(2)}, u32[]{:S(2)}) collective-permute-start(f32[256,128]{1,0:T(8,128)S(1)} %bitcast.31), channel_id=1, source_target_pairs={{0,16},{1,17},{2,18},{3,19},{4,20},{5,21},{6,22},{7,23},{8,24},{9,... | collective-permute-start | bytes 393224 | tf_op jit(solution)/shard_map/ppermute | solution.py:717
  88.8 10.8 %collective-permute-start.5 = (f32[256,128]{1,0:T(8,128)S(1)}, f32[256,128]{1,0:T(8,128)S(1)}, u32[]{:S(2)}, u32[]{:S(2)}) collective-permute-start(f32[256,128]{1,0:T(8,128)S(1)} %bitcast.29), channel_id=1, source_target_pairs={{0,16},{1,17},{2,18},{3,19},{4,20},{5,21},{6,22},{7,23},{8,24},{9,... | collective-permute-start | bytes 393224 | tf_op jit(solution)/shard_map/ppermute | solution.py:717
  104.3 3.0 %copy-start.5 = (f32[8,128]{1,0:T(8,128)}, f32[8,128]{1,0:T(8,128)S(1)}, u32[]{:S(2)}) copy-start(f32[8,128]{1,0:T(8,128)S(1)} %get-tuple-element.107.refs_5_) | copy-start | bytes 12292
  104.3 3.2 %collective-permute-start.6 = (bf16[128,5376]{1,0:T(8,128)(2,1)S(1)}, bf16[128,5376]{1,0:T(8,128)(2,1)S(1)}, u32[]{:S(2)}, u32[]{:S(2)}) collective-permute-start(bf16[128,5376]{1,0:T(8,128)(2,1)S(1)} %get-tuple-element.98), channel_id=1, source_target_pairs={{0,1},{1,0},{2,3},{3,2},{4,5},{5,4},{6,7},{7,6},{8,9},{9,8},{10,11... | collective-permute-start | bytes 4128776 | tf_op jit(solution)/shard_map/ppermute | solution.py:710
  129.7 22.2 %all-to-all-start.6 = ((bf16[16,148,256]{2,1,0:T(8,128)(2,1)}), bf16[16,148,256]{2,1,0:T(8,128)(2,1)S(1)}, u32[]{:S(2)}, u32[]{:S(2)}) async-start(bf16[16,148,256]{2,1,0:T(8,128)(2,1)} %shard_map.289.refs_0_), calls=%async_computation.6 | async-start | bytes 2490368 | tf_op jit(solution)/shard_map/all_to_all | solution.py:704
  133.5 16.2 %collective-permute-start.7 = (bf16[16,5376]{1,0:T(8,128)(2,1)S(1)}, bf16[16,5376]{1,0:T(8,128)(2,1)S(1)}, u32[]{:S(2)}, u32[]{:S(2)}) collective-permute-start(bf16[16,5376]{1,0:T(8,128)(2,1)S(1)} %shard_map.291.refs_0_), channel_id=1, source_target_pairs={{0,16},{1,17},{2,18},{3,19},{4,20},{5,21},{6,22},{7,23},{8,24},{9,... | collective-permute-start | bytes 516104 | tf_op jit(solution)/shard_map/ppermute | solution.py:891
  151.9 13.1 %all-to-all-start.7 = ((bf16[4,16,5504]{2,1,0:T(8,128)(2,1)}), bf16[4,16,5504]{2,1,0:T(8,128)(2,1)S(1)}, u32[]{:S(2)}, u32[]{:S(2)}) async-start(bf16[4,16,5504]{2,1,0:T(8,128)(2,1)} %shard_map.292), calls=%async_computation.7 | async-start | bytes 1409024 | tf_op jit(solution)/shard_map/all_to_all | solution.py:704
  156.9 2.1 %collective-permute-start.8 = (bf16[8,148,256]{2,0,1:T(8,128)(2,1)S(1)}, bf16[8,148,256]{2,0,1:T(8,128)(2,1)S(1)}, u32[]{:S(2)}, u32[]{:S(2)}) collective-permute-start(bf16[8,148,256]{2,0,1:T(8,128)(2,1)S(1)} %copy.32), channel_id=1, source_target_pairs={{0,1},{1,0},{2,3},{3,2},{4,5},{5,4},{6,7},{7,6},{8,9},{9,8},{10,11... | collective-permute-start | bytes 1818632 | tf_op jit(solution)/shard_map/ppermute | solution.py:710
  164.9 5.0 %copy-start.1 = (bf16[4,16,5504]{2,1,0:T(8,128)(2,1)}, bf16[4,16,5504]{2,1,0:T(8,128)(2,1)S(1)}, u32[]{:S(2)}) copy-start(bf16[4,16,5504]{2,1,0:T(8,128)(2,1)S(1)} %all-to-all-done.7.refs_1_) | copy-start | bytes 2113540
  165.1 4.9 %copy-start.4 = (f32[8,128]{1,0:T(8,128)}, f32[8,128]{1,0:T(8,128)S(1)}, u32[]{:S(2)}) copy-start(f32[8,128]{1,0:T(8,128)S(1)} %shard_map.295.refs_1_) | copy-start | bytes 12292
  165.1 3.1 %collective-permute-start.11 = (f32[8,128]{1,0:T(8,128)S(1)}, f32[8,128]{1,0:T(8,128)S(1)}, u32[]{:S(2)}, u32[]{:S(2)}) collective-permute-start(f32[8,128]{1,0:T(8,128)S(1)} %shard_map.295.refs_1_), channel_id=1, source_target_pairs={{0,3},{1,2},{2,1},{3,0},{4,7},{5,6},{6,5},{7,4},{8,11},{9,10},{10,... | collective-permute-start | bytes 12296 | tf_op jit(solution)/shard_map/ppermute | solution.py:926
  166.3 3.6 %collective-permute-start.10 = (f32[8,128]{1,0:T(8,128)S(1)}, f32[8,128]{1,0:T(8,128)S(1)}, u32[]{:S(2)}, u32[]{:S(2)}) collective-permute-start(f32[8,128]{1,0:T(8,128)S(1)} %shard_map.295.refs_1_), channel_id=1, source_target_pairs={{0,2},{1,3},{2,0},{3,1},{4,6},{5,7},{6,4},{7,5},{8,10},{9,11},{10,... | collective-permute-start | bytes 12296 | tf_op jit(solution)/shard_map/ppermute | solution.py:926
  166.9 3.0 %collective-permute-start.9 = (f32[8,128]{1,0:T(8,128)S(1)}, f32[8,128]{1,0:T(8,128)S(1)}, u32[]{:S(2)}, u32[]{:S(2)}) collective-permute-start(f32[8,128]{1,0:T(8,128)S(1)} %shard_map.295.refs_1_), channel_id=1, source_target_pairs={{0,1},{1,0},{2,3},{3,2},{4,5},{5,4},{6,7},{7,6},{8,9},{9,8},{10,11... | collective-permute-start | bytes 12296 | tf_op jit(solution)/shard_map/ppermute | solution.py:926
  168.2 1.8 %copy-start.8 = (f32[8,128]{1,0:T(8,128)}, f32[8,128]{1,0:T(8,128)S(1)}, u32[]{:S(2)}) copy-start(f32[8,128]{1,0:T(8,128)S(1)} %collective-permute-done.11.refs_4_) | copy-start | bytes 12292
  169.9 0.6 copy-start.9
  170.0 0.6 copy-start.10

commit v7 on v6

--- a/solution.py
+++ b/solution.py
@@ -545,7 +545,7 @@
     second = beta_two * second + (1.0 - beta_two) * gradient * gradient
     fix_one = 1.0 - beta_one**STEP
     fix_two = 1.0 - beta_two**STEP
-    stepped = first / fix_one / (jnp.sqrt(second / fix_two) + adam_eps)
+    stepped = first * (1.0 / fix_one) / (jnp.sqrt(second * (1.0 / fix_two)) + adam_eps)
     return weight - rate * (stepped + weight_decay * weight), first, second
 
 

time: 177 us -> 177 us (level)
  no operation moved by 1% of the time
where the time goes in v7:
time: 177 us; the launch traced here: 176 us
  blocking collectives  65 us (37%)
  waiting for transfers between devices  42.3 us (24%)
  Pallas kernels  42 us (24%)
  starting transfers between devices  22.4 us (13%)
  local copies, waits for them, and re-layouts  2.16 us (1%)
    all_to_all x4, blocking collectives, everywhere(): return lax.all_to_all(copies, AXES, 0, 0, tiled=True)  43 us
    pallas_call x15, Pallas kernels, run(): pl.pallas_call(lambda *refs: body(*refs[waits:]), out_shape=out_shape, in...  27.9 us
    all_to_all x1, blocking collectives, exchange(): lax.all_to_all(blocks, AXES, 0, 0, axis_index_groups=parts, tiled=True)  22 us
    ppermute x4, waiting for transfers between devices, chan_swap(): return lax.ppermute(values, 'chan', [(c, c ^ bit) for c in range(nc)])  19.5 us
    ppermute x1, waiting for transfers between devices, shards(): other = lax.ppermute(piece, AXES, [(i, i ^ shift) for i in range(devices)])  15.1 us
    all_to_all x3, starting transfers between devices, exchange(): lax.all_to_all(blocks, AXES, 0, 0, axis_index_groups=parts, tiled=True)  11.9 us
    pallas_call x1, Pallas kernels, shards(): pl.pallas_call(functools.partial(home_body, block), in_specs=[pl.BlockSpe...  5.77 us
    pallas_call x1, Pallas kernels, shards(): pl.pallas_call(functools.partial(adam_body, lid, cam, chans, nc, len(smal...  5.54 us
  transfers between devices with their start and end apart: 15, of which 9 were waited for; matrix products, arithmetic and copies ran while one was open for 2% of the time, Pallas kernels for 11%

profile of v7, /device:TPU:0, one launch (start us, length us, event | category | flops | bytes accessed | tf_op | source)
XLA Modules:
  0.0 176.3 jit_solution(3197241671223269100)
XLA Ops:
  0.7 2.7 %shard_map.279 = bf16[64,5504]{1,0:T(8,128)(2,1)} custom-call(f32[4,64]{1,0:T(4,128)} %refs_7_.1, f32[3,3,64,256]{3,2,1,0:T(8,128)} %bitcast.32, f32[3,3,64,80]{3,2,1,0:T(8,128)} %bitcast.34, f32[3,3,64,256]{3,2,1,0:T(8,128)} %refs_16_.1), custom_call_target="tpu_custom_call" | custom-call | tf_op jit(solution)/shard_map/pallas_call | solution.py:762
  3.4 3.0 %collective-permute-start = (bf16[1,64,5504]{2,1,0:T(8,128)(2,1)}, bf16[1,64,5504]{2,1,0:T(8,128)(2,1)S(1)}, u32[]{:S(2)}, u32[]{:S(2)}) collective-permute-start(bf16[1,64,5504]{2,1,0:T(8,128)(2,1)} %bitcast.22), channel_id=1, source_target_pairs={{0,2},{1,3},{2,0},{3,1},{4,6},{5,7},{6,4},{7,5},{8,10},{9,11},{10,... | collective-permute-start | bytes 2113544 | tf_op jit(solution)/shard_map/ppermute | solution.py:710
  6.5 0.3 reshape.51.refs_2_
  6.8 0.3 reshape.52.refs_3_
  7.2 4.5 %shard_map.282 = bf16[16,148,256]{2,1,0:T(8,128)(2,1)} custom-call(s32[1,16384]{1,0:T(1,128)S(1)} %bitcast.27, bf16[20,16384]{1,0:T(8,128)(2,1)S(1)} %copy-done.2, bf16[16,64,256]{2,1,0:T(8,128)(2,1)S(1)} %reshape.51.refs_2_, bf16[16,64,256]{2,1,0:T(8,128)(2,1)S(1)} %reshape.52.refs_3_), custom_call_target="tpu_custom_call" | custom-call | tf_op jit(solution)/shard_map/pallas_call | solution.py:43
  11.7 4.0 %all-to-all-start = ((bf16[16,148,256]{2,1,0:T(8,128)(2,1)}), bf16[16,148,256]{2,1,0:T(8,128)(2,1)S(1)}, u32[]{:S(2)}, u32[]{:S(2)}) async-start(bf16[16,148,256]{2,1,0:T(8,128)(2,1)} %shard_map.282), calls=%async_computation | async-start | bytes 2490368 | tf_op jit(solution)/shard_map/all_to_all | solution.py:704
  15.7 17.3 %collective-permute-done.refs_2_ = bf16[1,64,5504]{2,1,0:T(8,128)(2,1)S(1)} collective-permute-done((bf16[1,64,5504]{2,1,0:T(8,128)(2,1)}, bf16[1,64,5504]{2,1,0:T(8,128)(2,1)S(1)}, u32[]{:S(2)}, u32[]{:S(2)}) %collective-permute-start) | collective-permute-done | bytes 704544 | tf_op jit(solution)/shard_map/ppermute | solution.py:710
  33.0 1.2 pad_maximum_fusion
  34.2 0.9 all-to-all-done.refs_0_
  35.2 2.7 %collective-permute-start.2 = (bf16[4,148,128]{2,1,0:T(8,128)(2,1)S(1)}, bf16[4,148,128]{2,1,0:T(8,128)(2,1)S(1)}, u32[]{:S(2)}, u32[]{:S(2)}) collective-permute-start(bf16[4,148,128]{2,1,0:T(8,128)(2,1)S(1)} %slice_select_fusion), channel_id=1, source_target_pairs={{0,16},{1,17},{2,18},{3,19},{4,20},{5,21},{6,22},{7,23},{8,24},{9,... | collective-permute-start | bytes 454664 | tf_op jit(solution)/shard_map/ppermute | solution.py:717
  37.9 1.7 shard_map.280
  39.7 0.8 shard_map.281
  40.5 2.2 %shard_map.283 = (bf16[1024,1280]{1,0:T(8,128)(2,1)S(1)}, bf16[256,1024]{1,0:T(8,128)(2,1)S(1)}, f32[256,1024]{1,0:T(8,128)S(1)}) custom-call(bf16[16,148,256]{2,1,0:T(8,128)(2,1)S(1)} %all-to-all-done.refs_0_, bf16[256,3072]{1,0:T(8,128)(2,1)S(1)} %get-tuple-element.69.refs_0_.refs_1_.refs_6_), custom_call_target="tpu_custom_call" | custom-call | tf_op jit(solution)/shard_map/pallas_call | solution.py:43
  42.7 3.4 %collective-permute-done.2.refs_4_.refs_5_ = bf16[4,148,128]{2,1,0:T(8,128)(2,1)S(1)} collective-permute-done((bf16[4,148,128]{2,1,0:T(8,128)(2,1)S(1)}, bf16[4,148,128]{2,1,0:T(8,128)(2,1)S(1)}, u32[]{:S(2)}, u32[]{:S(2)}) %collective-permute-start.2) | collective-permute-done | bytes 151584 | tf_op jit(solution)/shard_map/ppermute | solution.py:717
  46.0 1.2 shard_map.284
  47.4 13.3 %all_to_all.40.refs_4_ = f32[32,2,256]{2,1,0:T(2,128)S(1)} all-to-all(f32[32,2,256]{2,1,0:T(2,128)S(1)} %get-tuple-element.76), channel_id=1, replica_groups=mesh['strip'=8,'chan'=4] {'strip','chan'}, dimensions={0} | all-to-all | bytes 131072 | tf_op jit(solution)/shard_map/all_to_all | solution.py:707
  60.7 2.8 %shard_map.285 = (f32[256,1024]{1,0:T(8,128)S(1)}, f32[32,2,256]{2,1,0:T(2,128)S(1)}, f32[1,256,128]{2,1,0:T(8,128)S(1)}, f32[256,1024]{1,0:T(8,128)S(1)}, f32[256,128]{1,0:T(8,128)S(1)}) custom-call(s32[2]{0:T(128)S(1)} %pad_add_fusion.refs_0_.refs_2_.place_ref, f32[256,1024]{1,0:T(8,128)S(1)} %get-tuple-element.74.refs_1_.refs_9_.refs_4_, ...), custom_call_target="tpu_custom_call" | custom-call | tf_op jit(solution)/shard_map/pallas_call | solution.py:43
  63.5 0.7 collective-permute-start.4
  64.2 10.0 %all_to_all.41.refs_4_ = f32[32,2,256]{2,1,0:T(2,128)S(1)} all-to-all(f32[32,2,256]{2,1,0:T(2,128)S(1)} %get-tuple-element.80), channel_id=1, replica_groups=mesh['strip'=8,'chan'=4] {'strip','chan'}, dimensions={0} | all-to-all | bytes 131072 | tf_op jit(solution)/shard_map/all_to_all | solution.py:707
  74.2 1.8 %shard_map.286 = (f32[256,1280]{1,0:T(8,128)S(1)}, f32[32,2,256]{2,1,0:T(2,128)S(1)}, f32[256,128]{1,0:T(8,128)S(1)}, bf16[16,64,256]{2,1,0:T(8,128)(2,1)S(1)}) custom-call(s32[2]{0:T(128)S(1)} %pad_add_fusion.refs_0_.refs_2_.place_ref, f32[256,1024]{1,0:T(8,128)S(1)} %get-tuple-element.78.refs_1_.refs_2_, ...), custom_call_target="tpu_custom_call" | custom-call | tf_op jit(solution)/shard_map/pallas_call | solution.py:43
  76.1 9.6 %all_to_all.42.refs_6_ = f32[32,2,256]{2,1,0:T(2,128)S(1)} all-to-all(f32[32,2,256]{2,1,0:T(2,128)S(1)} %get-tuple-element.86), channel_id=1, replica_groups=mesh['strip'=8,'chan'=4] {'strip','chan'}, dimensions={0} | all-to-all | bytes 131072 | tf_op jit(solution)/shard_map/all_to_all | solution.py:707
  85.7 3.0 %shard_map.287 = (f32[256,1024]{1,0:T(8,128)S(1)}, f32[32,2,256]{2,1,0:T(2,128)S(1)}, f32[1,256,128]{2,1,0:T(8,128)S(1)}, bf16[768,1280]{1,0:T(8,128)(2,1)S(1)}, f32[2,256]{1,0:T(2,128)S(1)}) custom-call(s32[2]{0:T(128)S(1)} %pad_add_fusion.refs_0_.refs_2_.place_ref, f32[256,1280]{1,0:T(8,128)S(1)} %get-tuple-element.84.refs_1_, ...), custom_call_target="tpu_custom_call" | custom-call | tf_op jit(solution)/shard_map/pallas_call | solution.py:43
  88.8 0.7 collective-permute-start.5
  89.5 10.0 %all_to_all.43.refs_8_ = f32[32,2,256]{2,1,0:T(2,128)S(1)} all-to-all(f32[32,2,256]{2,1,0:T(2,128)S(1)} %get-tuple-element.90), channel_id=1, replica_groups=mesh['strip'=8,'chan'=4] {'strip','chan'}, dimensions={0} | all-to-all | bytes 131072 | tf_op jit(solution)/shard_map/all_to_all | solution.py:707
  99.5 4.7 %shard_map.288 = (f32[128,5376]{1,0:T(8,128)S(1)}, bf16[128,5376]{1,0:T(8,128)(2,1)S(1)}, bf16[768,1280]{1,0:T(8,128)(2,1)S(1)}, f32[4,256]{1,0:T(4,128)S(1)}, f32[8,128]{1,0:T(8,128)S(1)}) custom-call(s32[2]{0:T(128)S(1)} %pad_add_fusion.refs_0_.refs_2_.place_ref, f32[256,1024]{1,0:T(8,128)S(1)} %get-tuple-element.88.refs_1_, ...), custom_call_target="tpu_custom_call" | custom-call | tf_op jit(solution)/shard_map/pallas_call | solution.py:43
  104.3 0.2 collective-permute-start.6
  104.5 2.8 %shard_map.289.refs_0_ = bf16[16,148,256]{2,1,0:T(8,128)(2,1)} custom-call(bf16[768,1280]{1,0:T(8,128)(2,1)S(1)} %get-tuple-element.95.refs_0_, bf16[336,2304]{1,0:T(8,128)(2,1)S(1)} %get-tuple-element.71.refs_0_.refs_1_, bf16[16,64,256]{2,1,0:T(8,128)(2,1)S(1)} %get-tuple-element.96.refs_2_), custom_call_target="tpu_custom_call" | custom-call | tf_op jit(solution)/shard_map/pallas_call | solution.py:43
  107.3 0.2 collective-permute-done.6.refs_2_
  107.5 0.3 shard_map.290
  107.7 22.0 %all_to_all.44.refs_0_ = bf16[8,16,5376]{2,1,0:T(8,128)(2,1)S(1)} all-to-all(bf16[8,16,5376]{2,1,0:T(8,128)(2,1)S(1)} %bitcast.26), channel_id=1, replica_groups={{0,4,8,12,2,6,10,14},{1,5,9,13,3,7,11,15},{16,20,24,28,18,22,26,30},{17..., dimensions={0} | all-to-all | bytes 2752512 | tf_op jit(solution)/shard_map/all_to_all | solution.py:704
  129.7 3.6 %all-to-all-start.6 = ((bf16[16,148,256]{2,1,0:T(8,128)(2,1)}), bf16[16,148,256]{2,1,0:T(8,128)(2,1)S(1)}, u32[]{:S(2)}, u32[]{:S(2)}) async-start(bf16[16,148,256]{2,1,0:T(8,128)(2,1)} %shard_map.289.refs_0_), calls=%async_computation.6 | async-start | bytes 2490368 | tf_op jit(solution)/shard_map/all_to_all | solution.py:704
  133.3 0.2 shard_map.291.refs_0_
  133.5 1.1 collective-permute-start.7
  134.5 15.1 %collective-permute-done.7.refs_1_ = bf16[16,5376]{1,0:T(8,128)(2,1)S(1)} collective-permute-done((bf16[16,5376]{1,0:T(8,128)(2,1)S(1)}, bf16[16,5376]{1,0:T(8,128)(2,1)S(1)}, u32[]{:S(2)}, u32[]{:S(2)}) %collective-permute-start.7) | collective-permute-done | bytes 172064 | tf_op jit(solution)/shard_map/ppermute | solution.py:891
  149.7 1.1 shard_map.292
  150.8 1.1 all-to-all-done.6.refs_1_
  151.9 4.3 %all-to-all-start.7 = ((bf16[4,16,5504]{2,1,0:T(8,128)(2,1)}), bf16[4,16,5504]{2,1,0:T(8,128)(2,1)S(1)}, u32[]{:S(2)}, u32[]{:S(2)}) async-start(bf16[4,16,5504]{2,1,0:T(8,128)(2,1)} %shard_map.292), calls=%async_computation.7 | async-start | bytes 1409024 | tf_op jit(solution)/shard_map/all_to_all | solution.py:704
  156.2 0.6 shard_map.293
  157.0 2.0 %collective-permute-done.8 = bf16[8,148,256]{2,0,1:T(8,128)(2,1)S(1)} collective-permute-done((bf16[8,148,256]{2,0,1:T(8,128)(2,1)S(1)}, bf16[8,148,256]{2,0,1:T(8,128)(2,1)S(1)}, u32[]{:S(2)}, u32[]{:S(2)}) %collective-permute-start.8) | collective-permute-done | bytes 606240 | tf_op jit(solution)/shard_map/ppermute | solution.py:710
  159.2 5.8 %shard_map.294 = (f32[16,64,2,128]{3,2,1,0:T(2,128)}, f32[16,64,2,128]{3,2,1,0:T(2,128)}, f32[20,16384]{1,0:T(8,128)}, f32[8,128]{1,0:T(8,128)S(1)}) custom-call(s32[2]{0:T(128)S(1)} %pad_add_fusion.refs_0_.refs_2_.place_ref, s32[1,16384]{1,0:T(1,128)S(1)} %bitcast.28, bf16[8,148,256]{2,1,0:T(8,128)(2,1)S(1)} %get-tuple-element.100.keep_ref, ...), custom_call_target="tpu_custom_call" | custom-call | tf_op jit(solution)/shard_map/pallas_call | solution.py:903
  165.0 0.1 shard_map.295.refs_1_
  165.1 1.2 collective-permute-start.11
  166.3 0.6 collective-permute-start.10
  167.0 0.6 constant_dynamic-slice_fusion.refs_6_
  167.7 0.5 collective-permute-done.11.refs_4_
  168.2 1.8 collective-permute-done.10.refs_3_
  170.0 0.6 copy-done.9
  170.5 5.5 %shard_map.296 = (f32[4,64]{1,0:T(4,128)}, f32[4,64]{1,0:T(4,128)}, f32[4,64]{1,0:T(4,128)}, f32[1,1]{1,0:T(1,128)}, f32[3,3,64,80]{3,2,1,0:T(8,128)}, /*index=5...) custom-call(bf16[64,5504]{1,0:T(8,128)(2,1)} %bitcast.25, ...), custom_call_target="tpu_custom_call" | custom-call | tf_op jit(solution)/shard_map/pallas_call | solution.py:932
  (35 shorter events, 0.6 us)
Async XLA Ops:
  0.6 5.8 %copy-start.6 = (bf16[16,64,2,128]{3,2,1,0:T(2,128)(2,1)S(1)}, bf16[16,64,2,128]{3,2,1,0:T(2,128)(2,1)}, u32[]{:S(2)}) copy-start(bf16[16,64,2,128]{3,2,1,0:T(2,128)(2,1)} %param.18) | copy-start | bytes 1572868
  0.7 6.1 %copy-start.7 = (bf16[16,64,2,128]{3,2,1,0:T(2,128)(2,1)S(1)}, bf16[16,64,2,128]{3,2,1,0:T(2,128)(2,1)}, u32[]{:S(2)}) copy-start(bf16[16,64,2,128]{3,2,1,0:T(2,128)(2,1)} %param.23) | copy-start | bytes 1572868
  3.4 3.7 %copy-start.2 = (bf16[20,16384]{1,0:T(8,128)(2,1)S(1)}, bf16[20,16384]{1,0:T(8,128)(2,1)}, u32[]{:S(2)}) copy-start(bf16[20,16384]{1,0:T(8,128)(2,1)} %refs_1_.1) | copy-start | bytes 1966084
  3.4 3.7 %copy-start.3 = (s32[16384]{0:T(1024)S(1)}, s32[16384]{0:T(1024)}, u32[]{:S(2)}) copy-start(s32[16384]{0:T(1024)} %param.17) | copy-start | bytes 196612
  3.4 29.5 %collective-permute-start = (bf16[1,64,5504]{2,1,0:T(8,128)(2,1)}, bf16[1,64,5504]{2,1,0:T(8,128)(2,1)S(1)}, u32[]{:S(2)}, u32[]{:S(2)}) collective-permute-start(bf16[1,64,5504]{2,1,0:T(8,128)(2,1)} %bitcast.22), channel_id=1, source_target_pairs={{0,2},{1,3},{2,0},{3,1},{4,6},{5,7},{6,4},{7,5},{8,10},{9,11},{10,... | collective-permute-start | bytes 2113544 | tf_op jit(solution)/shard_map/ppermute | solution.py:710
  11.7 21.3 %copy-start = (bf16[64,5504]{1,0:T(8,128)(2,1)S(1)}, bf16[64,5504]{1,0:T(8,128)(2,1)}, u32[]{:S(2)}) copy-start(bf16[64,5504]{1,0:T(8,128)(2,1)} %shard_map.279) | copy-start | bytes 2113540
  11.7 23.5 %all-to-all-start = ((bf16[16,148,256]{2,1,0:T(8,128)(2,1)}), bf16[16,148,256]{2,1,0:T(8,128)(2,1)S(1)}, u32[]{:S(2)}, u32[]{:S(2)}) async-start(bf16[16,148,256]{2,1,0:T(8,128)(2,1)} %shard_map.282), calls=%async_computation | async-start | bytes 2490368 | tf_op jit(solution)/shard_map/all_to_all | solution.py:704
  34.2 3.7 %collective-permute-start.1 = (bf16[2,64,5504]{2,1,0:T(8,128)(2,1)}, bf16[2,64,5504]{2,1,0:T(8,128)(2,1)}, u32[]{:S(2)}, u32[]{:S(2)}) collective-permute-start(bf16[2,64,5504]{2,1,0:T(8,128)(2,1)} %pad_maximum_fusion), channel_id=1, source_target_pairs={{0,1},{1,0},{2,3},{3,2},{4,5},{5,4},{6,7},{7,6},{8,9},{9,8},{10,11... | collective-permute-start | bytes 4227080 | tf_op jit(solution)/shard_map/ppermute | solution.py:710
  35.2 10.9 %collective-permute-start.2 = (bf16[4,148,128]{2,1,0:T(8,128)(2,1)S(1)}, bf16[4,148,128]{2,1,0:T(8,128)(2,1)S(1)}, u32[]{:S(2)}, u32[]{:S(2)}) collective-permute-start(bf16[4,148,128]{2,1,0:T(8,128)(2,1)S(1)} %slice_select_fusion), channel_id=1, source_target_pairs={{0,16},{1,17},{2,18},{3,19},{4,20},{5,21},{6,22},{7,23},{8,24},{9,... | collective-permute-start | bytes 454664 | tf_op jit(solution)/shard_map/ppermute | solution.py:717
  47.3 13.4 %collective-permute-start.3 = (f32[256,128]{1,0:T(8,128)S(1)}, f32[256,128]{1,0:T(8,128)S(1)}, u32[]{:S(2)}, u32[]{:S(2)}) collective-permute-start(f32[256,128]{1,0:T(8,128)S(1)} %bitcast.30), channel_id=1, source_target_pairs={{0,16},{1,17},{2,18},{3,19},{4,20},{5,21},{6,22},{7,23},{8,24},{9,... | collective-permute-start | bytes 393224 | tf_op jit(solution)/shard_map/ppermute | solution.py:717
  63.5 10.8 %collective-permute-start.4 = (f32[256,128]{1,0:T(8,128)S(1)}, f32[256,128]{1,0:T(8,128)S(1)}, u32[]{:S(2)}, u32[]{:S(2)}) collective-permute-start(f32[256,128]{1,0:T(8,128)S(1)} %bitcast.31), channel_id=1, source_target_pairs={{0,16},{1,17},{2,18},{3,19},{4,20},{5,21},{6,22},{7,23},{8,24},{9,... | collective-permute-start | bytes 393224 | tf_op jit(solution)/shard_map/ppermute | solution.py:717
  88.8 10.8 %collective-permute-start.5 = (f32[256,128]{1,0:T(8,128)S(1)}, f32[256,128]{1,0:T(8,128)S(1)}, u32[]{:S(2)}, u32[]{:S(2)}) collective-permute-start(f32[256,128]{1,0:T(8,128)S(1)} %bitcast.29), channel_id=1, source_target_pairs={{0,16},{1,17},{2,18},{3,19},{4,20},{5,21},{6,22},{7,23},{8,24},{9,... | collective-permute-start | bytes 393224 | tf_op jit(solution)/shard_map/ppermute | solution.py:717
  104.3 3.0 %copy-start.5 = (f32[8,128]{1,0:T(8,128)}, f32[8,128]{1,0:T(8,128)S(1)}, u32[]{:S(2)}) copy-start(f32[8,128]{1,0:T(8,128)S(1)} %get-tuple-element.107.refs_5_) | copy-start | bytes 12292
  104.3 3.2 %collective-permute-start.6 = (bf16[128,5376]{1,0:T(8,128)(2,1)S(1)}, bf16[128,5376]{1,0:T(8,128)(2,1)S(1)}, u32[]{:S(2)}, u32[]{:S(2)}) collective-permute-start(bf16[128,5376]{1,0:T(8,128)(2,1)S(1)} %get-tuple-element.98), channel_id=1, source_target_pairs={{0,1},{1,0},{2,3},{3,2},{4,5},{5,4},{6,7},{7,6},{8,9},{9,8},{10,11... | collective-permute-start | bytes 4128776 | tf_op jit(solution)/shard_map/ppermute | solution.py:710
  129.7 22.2 %all-to-all-start.6 = ((bf16[16,148,256]{2,1,0:T(8,128)(2,1)}), bf16[16,148,256]{2,1,0:T(8,128)(2,1)S(1)}, u32[]{:S(2)}, u32[]{:S(2)}) async-start(bf16[16,148,256]{2,1,0:T(8,128)(2,1)} %shard_map.289.refs_0_), calls=%async_computation.6 | async-start | bytes 2490368 | tf_op jit(solution)/shard_map/all_to_all | solution.py:704
  133.5 16.2 %collective-permute-start.7 = (bf16[16,5376]{1,0:T(8,128)(2,1)S(1)}, bf16[16,5376]{1,0:T(8,128)(2,1)S(1)}, u32[]{:S(2)}, u32[]{:S(2)}) collective-permute-start(bf16[16,5376]{1,0:T(8,128)(2,1)S(1)} %shard_map.291.refs_0_), channel_id=1, source_target_pairs={{0,16},{1,17},{2,18},{3,19},{4,20},{5,21},{6,22},{7,23},{8,24},{9,... | collective-permute-start | bytes 516104 | tf_op jit(solution)/shard_map/ppermute | solution.py:891
  151.9 13.1 %all-to-all-start.7 = ((bf16[4,16,5504]{2,1,0:T(8,128)(2,1)}), bf16[4,16,5504]{2,1,0:T(8,128)(2,1)S(1)}, u32[]{:S(2)}, u32[]{:S(2)}) async-start(bf16[4,16,5504]{2,1,0:T(8,128)(2,1)} %shard_map.292), calls=%async_computation.7 | async-start | bytes 1409024 | tf_op jit(solution)/shard_map/all_to_all | solution.py:704
  156.9 2.1 %collective-permute-start.8 = (bf16[8,148,256]{2,0,1:T(8,128)(2,1)S(1)}, bf16[8,148,256]{2,0,1:T(8,128)(2,1)S(1)}, u32[]{:S(2)}, u32[]{:S(2)}) collective-permute-start(bf16[8,148,256]{2,0,1:T(8,128)(2,1)S(1)} %copy.32), channel_id=1, source_target_pairs={{0,1},{1,0},{2,3},{3,2},{4,5},{5,4},{6,7},{7,6},{8,9},{9,8},{10,11... | collective-permute-start | bytes 1818632 | tf_op jit(solution)/shard_map/ppermute | solution.py:710
  164.9 5.0 %copy-start.1 = (bf16[4,16,5504]{2,1,0:T(8,128)(2,1)}, bf16[4,16,5504]{2,1,0:T(8,128)(2,1)S(1)}, u32[]{:S(2)}) copy-start(bf16[4,16,5504]{2,1,0:T(8,128)(2,1)S(1)} %all-to-all-done.7.refs_1_) | copy-start | bytes 2113540
  165.1 4.9 %copy-start.4 = (f32[8,128]{1,0:T(8,128)}, f32[8,128]{1,0:T(8,128)S(1)}, u32[]{:S(2)}) copy-start(f32[8,128]{1,0:T(8,128)S(1)} %shard_map.295.refs_1_) | copy-start | bytes 12292
  165.1 3.1 %collective-permute-start.11 = (f32[8,128]{1,0:T(8,128)S(1)}, f32[8,128]{1,0:T(8,128)S(1)}, u32[]{:S(2)}, u32[]{:S(2)}) collective-permute-start(f32[8,128]{1,0:T(8,128)S(1)} %shard_map.295.refs_1_), channel_id=1, source_target_pairs={{0,3},{1,2},{2,1},{3,0},{4,7},{5,6},{6,5},{7,4},{8,11},{9,10},{10,... | collective-permute-start | bytes 12296 | tf_op jit(solution)/shard_map/ppermute | solution.py:926
  166.3 3.6 %collective-permute-start.10 = (f32[8,128]{1,0:T(8,128)S(1)}, f32[8,128]{1,0:T(8,128)S(1)}, u32[]{:S(2)}, u32[]{:S(2)}) collective-permute-start(f32[8,128]{1,0:T(8,128)S(1)} %shard_map.295.refs_1_), channel_id=1, source_target_pairs={{0,2},{1,3},{2,0},{3,1},{4,6},{5,7},{6,4},{7,5},{8,10},{9,11},{10,... | collective-permute-start | bytes 12296 | tf_op jit(solution)/shard_map/ppermute | solution.py:926
  166.9 3.0 %collective-permute-start.9 = (f32[8,128]{1,0:T(8,128)S(1)}, f32[8,128]{1,0:T(8,128)S(1)}, u32[]{:S(2)}, u32[]{:S(2)}) collective-permute-start(f32[8,128]{1,0:T(8,128)S(1)} %shard_map.295.refs_1_), channel_id=1, source_target_pairs={{0,1},{1,0},{2,3},{3,2},{4,5},{5,4},{6,7},{7,6},{8,9},{9,8},{10,11... | collective-permute-start | bytes 12296 | tf_op jit(solution)/shard_map/ppermute | solution.py:926
  168.2 1.8 %copy-start.8 = (f32[8,128]{1,0:T(8,128)}, f32[8,128]{1,0:T(8,128)S(1)}, u32[]{:S(2)}) copy-start(f32[8,128]{1,0:T(8,128)S(1)} %collective-permute-done.11.refs_4_) | copy-start | bytes 12292
  169.9 0.6 copy-start.9
  170.0 0.6 copy-start.10
